TPU v7x, 32 devices: a whole 2x2x4 slice. The times are simulated.
32 devices in a mesh: seq: 8 (over z, x), dp: 2 (over core), tensor: 2 (over y).
Axes of the slice: x: 2, y: 2, z: 4, core: 2. Of those that a mesh axis runs over, the one named last changes fastest.
Arguments:
- head_inputs: bfloat16 [2, 2560, 4096], P('dp', 'tensor', 'seq'), may hold values from -6 to 6
- b_proj: bfloat16 [2, 4096, 128], P('dp', 'seq'), may hold values from -0.59765625 to 0.59765625
- c_proj: bfloat16 [2, 4096, 128], P('dp', 'seq'), may hold values from -0.59765625 to 0.59765625
- dt_raw: float32 [2, 40, 4096], P('dp', 'tensor', 'seq'), may hold values from -2 to 0
- a_log: float32 [40], P('tensor'), as said below
- d_skip: float32 [40], P('tensor'), may hold values from 0.5 to 1.5
- w_out: bfloat16 [2560, 2560], P('tensor', 'dp'), may hold values from -0.125 to 0.125
- out_grad: bfloat16 [2, 2560, 4096], P('dp', 'tensor', 'seq'), may hold values from -6 to 6
Outputs:
- mixed: bfloat16 [2, 2560, 4096], P('dp', 'tensor', 'seq')
- grad_inputs: bfloat16 [2, 2560, 4096], P('dp', 'tensor', 'seq')
- grad_b: bfloat16 [2, 4096, 128], P('dp', 'seq')
- grad_c: bfloat16 [2, 4096, 128], P('dp', 'seq')
- grad_dt: float32 [2, 40, 4096], P('dp', 'tensor', 'seq')
- grad_alog: float32 [40], P('tensor')
- grad_skip: float32 [40], P('tensor')
- grad_w: bfloat16 [2560, 2560], P('tensor', ('seq', 'dp'))
Inputs may be any that keep to these rules, and one draw needn't show every extreme that they name: exp(a_log) lies between 0.1 / 4096 and 0.1.
All inputs are finite; a program needn't handle non-finite values.
Results may differ from a plain program's by a relative error of at most 0.0049.
Values may be sent and summed in bfloat16 or wider, within the bound.
No kernel may reach another device: no remote copies, remote signals or barrier semaphores. Data moves between devices by JAX's collectives and lax.ppermute only.
A program may use at most 192 MiB of HBM per device.

v0:
```python
import jax
import jax.numpy as jnp
from jax import lax
from jax.sharding import PartitionSpec as P

SPAN = 256


HIGH = lax.Precision.HIGHEST


def span_pass(carried, x_block, b_block, c_block, step_block, decay_rate):
    log_decay = step_block * decay_rate[:, None]
    cumulative = jnp.cumsum(log_decay, axis=1)
    block = cumulative.shape[1]
    indices = jnp.arange(block)
    causal = (indices[:, None] >= indices[None, :])[None, :, :]
    spread = cumulative[:, :, None] - cumulative[:, None, :]
    weights = jnp.where(causal, jnp.exp(jnp.where(causal, spread, 0.0)), 0.0)
    affinity = jnp.dot(c_block, b_block.T, precision=HIGH)
    scores = affinity[None, :, :] * weights * step_block[:, None, :]
    block_out = jnp.einsum("hps,hts->hpt", x_block, scores, precision=HIGH)
    block_out = block_out + jnp.exp(cumulative)[:, None, :] * jnp.einsum(
        "hpn,tn->hpt", carried, c_block, precision=HIGH
    )
    tail_weight = jnp.exp(cumulative[:, -1:] - cumulative) * step_block
    updated = jnp.exp(cumulative[:, -1])[:, None, None] * carried
    updated = updated + jnp.einsum(
        "hps,sn->hpn", x_block * tail_weight[:, None, :], b_block, precision=HIGH
    )
    return (updated, block_out)


def sweep(streams, b_rows, c_rows, dt_rows, alog_part, skip_part, state_in):
    head_count, head_width, length = streams.shape
    blocks = length // SPAN
    step_size = jax.nn.softplus(dt_rows)
    decay_rate = -jnp.exp(alog_part)
    x_blocks = streams.reshape(head_count, head_width, blocks, SPAN).transpose(2, 0, 1, 3)
    b_blocks = b_rows.reshape(blocks, SPAN, b_rows.shape[1])
    c_blocks = c_rows.reshape(blocks, SPAN, c_rows.shape[1])
    s_blocks = step_size.reshape(head_count, blocks, SPAN).transpose(1, 0, 2)

    def advance(carried, inputs):
        return span_pass(carried, inputs[0], inputs[1], inputs[2], inputs[3], decay_rate)

    state_end, outputs = lax.scan(advance, state_in, (x_blocks, b_blocks, c_blocks, s_blocks))
    mixed_f = outputs.transpose(1, 2, 0, 3).reshape(head_count, head_width, length)
    return (mixed_f + skip_part[:, None, None] * streams, state_end)


def per_device(head_inputs, b_proj, c_proj, dt_raw, a_log, d_skip, w_out, out_grad):
    head_count = dt_raw.shape[1]
    length = head_inputs.shape[2]
    head_width = head_inputs.shape[1] // head_count
    streams = head_inputs[0].astype(jnp.float32).reshape(head_count, head_width, length)
    b_rows = b_proj[0].astype(jnp.float32)
    c_rows = c_proj[0].astype(jnp.float32)
    dt_rows = dt_raw[0]
    decay_rate = -jnp.exp(a_log)
    step_size = jax.nn.softplus(dt_rows)
    cumulative = jnp.cumsum(step_size * decay_rate[:, None], axis=1)
    device_decay = cumulative[:, -1]
    tail_weight = jnp.exp(device_decay[:, None] - cumulative) * step_size
    local_state = jnp.einsum(
        "hpt,tn->hpn", streams * tail_weight[:, None, :], b_rows, precision=HIGH
    )
    totals = lax.all_gather(device_decay[None, :], "seq", axis=0, tiled=True)
    prefix = jnp.cumsum(totals, axis=0)
    my_index = lax.axis_index("seq")
    reached = lax.dynamic_index_in_dim(prefix, my_index, 0, keepdims=False)
    before = reached - device_decay
    shard_part = lax.all_gather(local_state[None], "seq", axis=0, tiled=True)
    row_count = shard_part.shape[0]
    indices = jnp.arange(row_count, dtype=jnp.int32)
    prefix_ends = prefix
    active = (indices < my_index)[:, None]
    weights = jnp.where(active, jnp.exp(jnp.where(active, before[None, :] - prefix_ends, 0.0)), 0.0)
    state_in = jnp.einsum("jh,jhpn->hpn", weights, shard_part, precision=HIGH)

    def local_sweep(xa, ba, ca, da, aa, sa):
        return sweep(xa, ba, ca, da, aa, sa, state_in)

    primal, pullback = jax.vjp(local_sweep, streams, b_rows, c_rows, dt_rows, a_log, d_skip)
    mixed_half = primal[0].reshape(head_count * head_width, length).astype(jnp.bfloat16)
    g_full = lax.all_gather(out_grad[0], "tensor", axis=0, tiled=True)
    cotan_sum = jnp.dot(
        lax.all_gather(w_out, "dp", axis=1, tiled=True), g_full, preferred_element_type=jnp.float32
    )
    cotan_half = cotan_sum.astype(jnp.bfloat16)
    y_cotan = (
        lax.optimization_barrier(cotan_half)
        .astype(jnp.float32)
        .reshape(head_count, head_width, length)
    )
    local_cotan = jnp.einsum(
        "hpt,tn->hpn", y_cotan * jnp.exp(cumulative)[:, None, :], c_rows, precision=HIGH
    )
    shard_part = lax.all_gather(local_cotan[None], "seq", axis=0, tiled=True)
    row_count = shard_part.shape[0]
    indices = jnp.arange(row_count, dtype=jnp.int32)
    prefix_ends = prefix
    active = (indices > my_index)[:, None]
    weights = jnp.where(
        active, jnp.exp(jnp.where(active, prefix_ends - totals - reached[None, :], 0.0)), 0.0
    )
    cotan_in = jnp.einsum("jh,jhpn->hpn", weights, shard_part, precision=HIGH)
    grads = pullback((y_cotan, cotan_in))
    w_terms = lax.dot_general(
        mixed_half, g_full, (((1,), (1,)), ((), ())), preferred_element_type=jnp.float32
    )
    grad_w = lax.psum_scatter(w_terms, ("seq", "dp"), scatter_dimension=1, tiled=True).astype(
        jnp.bfloat16
    )
    grad_b, grad_c = lax.psum((grads[1], grads[2]), "tensor")
    grad_alog, grad_skip = lax.psum((grads[4], grads[5]), ("seq", "dp"))
    grad_inputs = grads[0].reshape(head_count * head_width, length).astype(jnp.bfloat16)
    return (
        mixed_half[None],
        grad_inputs[None],
        grad_b.astype(jnp.bfloat16)[None],
        grad_c.astype(jnp.bfloat16)[None],
        grads[3][None],
        grad_alog,
        grad_skip,
        grad_w,
    )


def solution(mesh):
    in_specs = (
        P("dp", "tensor", "seq"),
        P("dp", "seq", None),
        P("dp", "seq", None),
        P("dp", "tensor", "seq"),
        P("tensor"),
        P("tensor"),
        P("tensor", "dp"),
        P("dp", "tensor", "seq"),
    )
    out_specs = (
        P("dp", "tensor", "seq"),
        P("dp", "tensor", "seq"),
        P("dp", "seq", None),
        P("dp", "seq", None),
        P("dp", "tensor", "seq"),
        P("tensor"),
        P("tensor"),
        P("tensor", ("seq", "dp")),
    )
    return jax.shard_map(
        per_device, mesh=mesh, in_specs=in_specs, out_specs=out_specs, check_vma=False
    )
```

profile of v0, /device:TPU:0, one launch (start us, length us, event | category | flops | bytes accessed | tf_op | source)
XLA Modules:
  0.0 488.7 jit_solution(11110350961877052653)
XLA Ops:
  14.6 2.7 reshape.737
  18.9 23.1 %all-reduce.2 = f32[160]{0:T(256)S(1)} all-reduce(f32[160]{0:T(256)S(1)} %dynamic-update-slice), channel_id=2, replica_groups=mesh['seq'=8,'dp'=2,'tensor'=2] {'seq'}, use_global_device_ids=true, to_apply=%add.2 | all-reduce | flops 160 | bytes 1280
  48.0 3.3 all-gather.13.cloned.1.call-done
  51.3 18.7 %all-gather.9.cloned.1.call-done = bf16[1280,2560]{1,0:T(8,128)(2,1)} async-done(((bf16[1280,1280]{1,0:T(8,128)(2,1)}), bf16[1280,2560]{1,0:T(8,128)(2,1)}) %all-gather.9.cloned.1.call-update) | async-done | bytes 6553616 | tf_op jit(solution)/shard_map/all_gather | solution.py:88
  70.1 7.2 %convolution_convert_fusion = bf16[1280,512]{1,0:T(8,128)(2,1)S(1)} fusion(bf16[1280,2560]{1,0:T(8,128)(2,1)} %all-gather.9.cloned.1.call-done, bf16[1,2560,512]{2,1,0:T(8,128)(2,1)} %all-gather.13.cloned.1.call-done), kind=kOutput, calls=%fused_computation.170 | convolution fusion | flops 3356098560 | bytes 10485760 | tf_op jit(solution)/shard_map/dot_general | solution.py:87
  81.1 78.6 %all-gather.11.cloned.1.call-done = f32[160,64,128]{2,1,0:T(8,128)} async-done(((f32[20,64,128]{2,1,0:T(8,128)}), f32[160,64,128]{2,1,0:T(8,128)}) %all-gather.11.cloned.1.call-update) | async-done | bytes 5242896 | tf_op jit(solution)/shard_map/all_gather | solution.py:73
  159.7 10.1 %fusion.141 = f32[20,1,64,128]{3,1,2,0:T(1,128)S(1)} fusion(f32[8,20,1,1]{0,2,3,1:T(1,128)} %copy.203, f32[8,20,64,128]{3,2,1,0:T(8,128)} %bitcast.481), kind=kOutput, calls=%fused_computation.168 | convolution fusion | flops 15728640 | bytes 5898880 | tf_op jit(solution)/shard_map/jh,jhpn->hpn/dot_general | solution.py:79
  176.5 77.0 %while.75 = (s32[]{:T(128)}, f32[20,64,128]{2,1,0:T(8,128)S(1)}, f32[2,20,64,256]{3,2,1,0:T(8,128)}, f32[2,20,256,256]{3,2,1,0:T(8,128)}, f32[2,128,256]{1,2,0:T...) while((s32[]{:T(128)}, f32[20,64,128]{2,1,0:T(8,128)S(1)}, ...), condition=%wide.region_6.7_spmd.clone.clone, body=%wide.region_3.6_spmd.clone.clone.sunk | while | flops 2129360896 | bytes 102141104 | solution.py:47
  186.1 8.9 %multiply_dynamic-update-slice_fusion.6 = (f32[2,20,256,256]{3,2,1,0:T(8,128)}, f32[2,20,256,256]{3,2,1,0:T(8,128)}, f32[2,20,256,256]{3,2,1,0:T(8,128)}, f32[2,20,256,256]{3,2,1,0:T(8,128)}) fusion(f32[2,20,256,256]{3,2,1,0:T(8,128)} %get-tuple-element.2181, s32[]{:T(128)} %get-tuple-element.2172, f32[20,256]{1,0:T(8,128)S(1)} %bitcast.483, ...), kind=kLoop, calls=%fused_computation.2.clone.1 | loop fusion | flops 6553600 | bytes 21373440 | tf_op jit(solution)/shard_map/jvp()/while/body/jit(dynamic_update_index_in_dim)/dynamic_update_slice | solution.py:47
  196.7 6.1 %fusion.228 = f32[2,20,64,256]{3,2,1,0:T(8,128)S(1)} fusion(f32[2,20,64,256]{3,2,1,0:T(8,128)S(1)} %copy-done.23, s32[]{:T(128)} %get-tuple-element.2172, f32[20,256]{1,0:T(8,128)S(1)} %bitcast.484, f32[20,256]{1,0:T(8,128)S(1)} %bitcast.472, f32[256,256]{1,0:T(8,128)S(1)} %get-tuple-element.2089, pred[256,256]{1,0:T(8,128)(4,1)S(1)} %copy-done.27, ...), kind=kOutput, calls=%fused_computation.24.clone.1 | convolution fusion | flops 1013841920 | bytes 4359168 | tf_op jit(solution)/shard_map/jvp()/while/body/eval_jaxpr/hps,hts->hpt/dot_general | solution.py:22
  224.2 9.1 %multiply_dynamic-update-slice_fusion.6 = (f32[2,20,256,256]{3,2,1,0:T(8,128)}, f32[2,20,256,256]{3,2,1,0:T(8,128)}, f32[2,20,256,256]{3,2,1,0:T(8,128)}, f32[2,20,256,256]{3,2,1,0:T(8,128)}) fusion(f32[2,20,256,256]{3,2,1,0:T(8,128)} %get-tuple-element.2181, s32[]{:T(128)} %get-tuple-element.2172, f32[20,256]{1,0:T(8,128)S(1)} %bitcast.483, ...), kind=kLoop, calls=%fused_computation.2.clone.1 | loop fusion | flops 6553600 | bytes 21373440 | tf_op jit(solution)/shard_map/jvp()/while/body/jit(dynamic_update_index_in_dim)/dynamic_update_slice | solution.py:47
  235.0 6.1 %fusion.228 = f32[2,20,64,256]{3,2,1,0:T(8,128)S(1)} fusion(f32[2,20,64,256]{3,2,1,0:T(8,128)S(1)} %copy-done.23, s32[]{:T(128)} %get-tuple-element.2172, f32[20,256]{1,0:T(8,128)S(1)} %bitcast.484, f32[20,256]{1,0:T(8,128)S(1)} %bitcast.472, f32[256,256]{1,0:T(8,128)S(1)} %get-tuple-element.2089, pred[256,256]{1,0:T(8,128)(4,1)S(1)} %copy-done.27, ...), kind=kOutput, calls=%fused_computation.24.clone.1 | convolution fusion | flops 1013841920 | bytes 4359168 | tf_op jit(solution)/shard_map/jvp()/while/body/eval_jaxpr/hps,hts->hpt/dot_general | solution.py:22
  253.5 4.7 copy.195
  261.3 6.8 %fusion.146 = f32[1280,2560]{0,1:T(8,128)} fusion(bf16[1,2560,512]{2,1,0:T(8,128)(2,1)S(1)} %copy-done.40, f32[1280,512]{1,0:T(8,128)S(1)} %bitcast.482, bf16[1,1280,512]{2,1,0:T(8,128)(2,1)S(1)} %copy-done.16, f32[1280]{0:T(1024)S(1)} %mul.563), kind=kOutput, calls=%fused_computation.177 | convolution fusion | flops 3358064640 | bytes 19665920 | tf_op jit(solution)/shard_map/dot_general | solution.py:109
  269.4 2.7 reshape_reshape.4
  274.2 5.0 %reshape.722 = f32[1,1280,512]{2,1,0:T(8,128)} reshape(f32[20,64,2,256]{3,2,1,0:T(2,128)} %copy-done.14) | data formatting | bytes 5242880 | tf_op jit(solution)/shard_map/jvp()/reshape | solution.py:48
  279.2 10.9 %fusion.139 = f32[20,1,64,128]{3,1,2,0:T(1,128)S(1)} fusion(f32[8,20,1,1]{0,2,3,1:T(1,128)} %copy.206, f32[8,20,64,128]{3,2,1,0:T(8,128)} %bitcast.480), kind=kOutput, calls=%fused_computation.166 | convolution fusion | flops 15728640 | bytes 5898880 | tf_op jit(solution)/shard_map/jh,jhpn->hpn/dot_general | solution.py:107
  293.9 128.1 %while.76 = (s32[]{:T(128)}, f32[20]{0:T(128)}, f32[20,64,128]{2,1,0:T(8,128)S(1)}, f32[2,20,64,256]{3,2,1,0:T(8,128)}, f32[2,256,128]{2,1,0:T(8,128)}, /*index=...) while((s32[]{:T(128)}, f32[20]{0:T(128)}, ...), condition=%wide.region_19.20_spmd.clone.clone, body=%wide.region_7.19_spmd.clone.clone.sunk | while | flops 4246280192 | bytes 68846072 | solution.py:47
  294.1 4.3 fusion.244
  307.8 11.7 %fusion.242 = (f32[20,256]{1,0:T(8,128)}, f32[20,256]{1,0:T(8,128)}, f32[256,256]{1,0:T(8,128)}, f32[20,256]{1,0:T(8,128)}) fusion(f32[2,20,256,256]{3,2,1,0:T(8,128)} %get-tuple-element.2312, s32[]{:T(128)S(6)} %sub.291, f32[20,256]{1,0:T(8,128)S(1)} %dynamic-slice_bitcast_fusion.7, f32[256,256]{1,0:T(8,128)S(1)} %dynamic-slice_bitcast_fusion.8, ...), kind=kOutput, calls=%fused_computation.120.clone.1 | convolution fusion | flops 1020969984 | bytes 19027456 | tf_op jit(solution)/shard_map/transpose(jvp())/while/body/eval_jaxpr/hps,hts->hpt/dot_general | solution.py:22
  332.5 2.5 reduce-window.62
  339.8 3.4 fusion.256
  348.8 7.2 %fusion.253 = f32[2,20,64,256]{3,2,1,0:T(8,128)} fusion(f32[2,20,64,256]{3,2,1,0:T(8,128)} %get-tuple-element.2264, s32[]{:T(128)S(6)} %sub.291, f32[2,20,256,256]{3,2,1,0:T(8,128)} %get-tuple-element.2317, f32[20,64,256]{2,1,0:T(8,128)S(1)} %copy-done.1, f32[2,20,64,256]{3,2,1,0:T(8,128)S(1)} %get-tuple-element.2307, ...), kind=kOutput, calls=%fused_computation.80.clone.1 | convolution fusion | flops 1007288320 | bytes 9201152 | tf_op jit(solution)/shard_map/transpose(jvp())/while/body/eval_jaxpr/hps,hts->hpt/dot_general | solution.py:22
  357.5 4.4 fusion.244
  371.2 12.1 %fusion.242 = (f32[20,256]{1,0:T(8,128)}, f32[20,256]{1,0:T(8,128)}, f32[256,256]{1,0:T(8,128)}, f32[20,256]{1,0:T(8,128)}) fusion(f32[2,20,256,256]{3,2,1,0:T(8,128)} %get-tuple-element.2312, s32[]{:T(128)S(6)} %sub.291, f32[20,256]{1,0:T(8,128)S(1)} %dynamic-slice_bitcast_fusion.7, f32[256,256]{1,0:T(8,128)S(1)} %dynamic-slice_bitcast_fusion.8, ...), kind=kOutput, calls=%fused_computation.120.clone.1 | convolution fusion | flops 1020969984 | bytes 19027456 | tf_op jit(solution)/shard_map/transpose(jvp())/while/body/eval_jaxpr/hps,hts->hpt/dot_general | solution.py:22
  396.3 2.5 reduce-window.62
  404.2 3.4 fusion.256
  413.2 6.9 %fusion.253 = f32[2,20,64,256]{3,2,1,0:T(8,128)} fusion(f32[2,20,64,256]{3,2,1,0:T(8,128)} %get-tuple-element.2264, s32[]{:T(128)S(6)} %sub.291, f32[2,20,256,256]{3,2,1,0:T(8,128)} %get-tuple-element.2317, f32[20,64,256]{2,1,0:T(8,128)S(1)} %copy-done.1, f32[2,20,64,256]{3,2,1,0:T(8,128)S(1)} %get-tuple-element.2307, ...), kind=kOutput, calls=%fused_computation.80.clone.1 | convolution fusion | flops 1007288320 | bytes 9201152 | tf_op jit(solution)/shard_map/transpose(jvp())/while/body/eval_jaxpr/hps,hts->hpt/dot_general | solution.py:22
  422.1 3.8 copy.200
  429.6 3.2 add_convert_fusion.1
  432.8 30.3 %all-reduce.3 = (f32[20]{0:T(128)}, f32[20]{0:T(128)}) all-reduce(f32[20]{0:T(128)S(1)} %negate_multiply_fusion, f32[20]{0:T(128)S(1)} %reduce_sum.212), channel_id=1, replica_groups=mesh['seq'=8,'dp'=2,'tensor'=2] {'seq','dp'}, use_global_device_ids=true, to_apply=%region_22.23 | all-reduce | flops 40 | bytes 320 | tf_op jit(solution)/shard_map/psum | solution.py:116
  464.0 16.1 %all-reduce.6 = (bf16[512,128]{1,0:T(8,128)(2,1)}, bf16[512,128]{1,0:T(8,128)(2,1)}) all-reduce(f32[512,128]{1,0:T(8,128)S(1)} %bitcast.486, f32[512,128]{1,0:T(8,128)S(1)} %bitcast.487), channel_id=1, replica_groups=mesh['seq'=8,'dp'=2,'tensor'=2] {'tensor'}, use_global_device_ids=true, to_apply=%region_20.21 | all-reduce | flops 131072 | bytes 786432 | tf_op jit(solution)/shard_map/psum | solution.py:115
  (337 shorter events, 156.4 us)
Async XLA Ops:
  7.2 44.1 %all-gather.13.cloned.1.call-start = ((), (), s32[]{:S(2)}) async-start(), calls=%async_computation.4 | async-start | bytes 3932160 | tf_op jit(solution)/shard_map/all_gather | solution.py:86
  7.9 62.1 %all-gather.9.cloned.1.call-start = ((), (), s32[]{:S(2)}) async-start(), calls=%async_computation.1 | async-start | bytes 9830400 | tf_op jit(solution)/shard_map/all_gather | solution.py:88
  8.7 151.0 %all-gather.11.cloned.1.call-start = ((), (), s32[]{:S(2)}) async-start(), calls=%async_computation.3 | async-start | bytes 5898240 | tf_op jit(solution)/shard_map/all_gather | solution.py:73
  14.5 264.7 %all-gather.15.cloned.1.call-start = ((), (), s32[]{:S(2)}) async-start(), calls=%async_computation.5 | async-start | bytes 5898240 | tf_op jit(solution)/shard_map/all_gather | solution.py:99
  80.8 399.3 %reduce-scatter.2.cloned.1.call-start = ((), (), s32[]{:S(2)}) async-start(), calls=%async_computation.2 | async-start | bytes 13926400 | tf_op jit(solution)/shard_map/reduce_scatter | solution.py:112
  186.1 9.1 %copy-start.19 = (f32[1,20,256]{2,0,1:T(1,128)S(1)}, f32[1,20,256]{2,0,1:T(1,128)}, u32[]{:S(2)}) copy-start(f32[1,20,256]{2,0,1:T(1,128)} %copy-done.18) | copy-start | bytes 61444 | tf_op jit(solution)/shard_map/jvp()/while
  186.1 9.2 %copy-start.5 = (f32[2,20,64,256]{3,2,1,0:T(8,128)S(1)}, f32[2,20,64,256]{3,2,1,0:T(8,128)}, u32[]{:S(2)}) copy-start(f32[2,20,64,256]{3,2,1,0:T(8,128)} %get-tuple-element.2184) | copy-start | bytes 7864324 | tf_op jit(solution)/shard_map/jvp()/while
  186.1 9.2 %copy-start.9 = (f32[2,256,128]{2,1,0:T(8,128)S(1)}, f32[2,256,128]{2,1,0:T(8,128)}, u32[]{:S(2)}) copy-start(f32[2,256,128]{2,1,0:T(8,128)} %get-tuple-element.2223) | copy-start | bytes 786436 | tf_op jit(solution)/shard_map/jvp()/while
  224.2 9.3 %copy-start.19 = (f32[1,20,256]{2,0,1:T(1,128)S(1)}, f32[1,20,256]{2,0,1:T(1,128)}, u32[]{:S(2)}) copy-start(f32[1,20,256]{2,0,1:T(1,128)} %copy-done.18) | copy-start | bytes 61444 | tf_op jit(solution)/shard_map/jvp()/while
  224.2 9.4 %copy-start.5 = (f32[2,20,64,256]{3,2,1,0:T(8,128)S(1)}, f32[2,20,64,256]{3,2,1,0:T(8,128)}, u32[]{:S(2)}) copy-start(f32[2,20,64,256]{3,2,1,0:T(8,128)} %get-tuple-element.2184) | copy-start | bytes 7864324 | tf_op jit(solution)/shard_map/jvp()/while
  224.2 9.4 %copy-start.9 = (f32[2,256,128]{2,1,0:T(8,128)S(1)}, f32[2,256,128]{2,1,0:T(8,128)}, u32[]{:S(2)}) copy-start(f32[2,256,128]{2,1,0:T(8,128)} %get-tuple-element.2223) | copy-start | bytes 786436 | tf_op jit(solution)/shard_map/jvp()/while
  294.1 8.7 %copy-start.7 = (f32[2,256,128]{2,1,0:T(8,128)}, f32[2,256,128]{2,1,0:T(8,128)S(1)}, u32[]{:S(2)}) copy-start(f32[2,256,128]{2,1,0:T(8,128)S(1)} %get-tuple-element.2305) | copy-start | bytes 786436 | tf_op jit(solution)/shard_map/transpose(jvp())/while
  319.5 10.1 %copy-start.12 = (f32[20,256]{0,1:T(8,128)S(1)}, f32[20,256]{0,1:T(8,128)}, u32[]{:S(2)}) copy-start(f32[20,256]{0,1:T(8,128)} %copy.294) | copy-start | bytes 61444 | tf_op jit(solution)/shard_map/transpose(jvp())/while
  338.2 9.2 %copy-start.10 = (f32[2,256,128]{2,1,0:T(8,128)S(1)}, f32[2,256,128]{2,1,0:T(8,128)}, u32[]{:S(2)}) copy-start(f32[2,256,128]{2,1,0:T(8,128)} %get-tuple-element.2315) | copy-start | bytes 786436 | tf_op jit(solution)/shard_map/transpose(jvp())/while
  338.2 7.0 %copy-start.4 = (f32[2,20,64,256]{3,2,1,0:T(8,128)S(1)}, f32[2,20,64,256]{3,2,1,0:T(8,128)}, u32[]{:S(2)}) copy-start(f32[2,20,64,256]{3,2,1,0:T(8,128)} %get-tuple-element.2318) | copy-start | bytes 7864324 | tf_op jit(solution)/shard_map/transpose(jvp())/while
  338.2 9.2 %copy-start.13 = (f32[256,256]{1,0:T(8,128)S(1)}, f32[256,256]{1,0:T(8,128)}, u32[]{:S(2)}) copy-start(f32[256,256]{1,0:T(8,128)} %get-tuple-element.2142) | copy-start | bytes 786436 | tf_op jit(solution)/shard_map/transpose(jvp())/while
  338.2 9.2 %copy-start.28 = (f32[2,256,128]{2,1,0:T(8,128)S(1)}, f32[2,256,128]{2,1,0:T(8,128)}, u32[]{:S(2)}) copy-start(f32[2,256,128]{2,1,0:T(8,128)} %get-tuple-element.2265) | copy-start | bytes 786436 | tf_op jit(solution)/shard_map/transpose(jvp())/while
  339.8 9.0 %copy-start.1 = (f32[20,64,256]{2,1,0:T(8,128)S(1)}, f32[20,64,256]{2,1,0:T(8,128)}, u32[]{:S(2)}) copy-start(f32[20,64,256]{2,1,0:T(8,128)} %get-tuple-element.2140) | copy-start | bytes 3932164 | tf_op jit(solution)/shard_map/transpose(jvp())/while
  348.8 7.2 %copy-start.43 = (f32[2,20,1,1]{1,3,2,0:T(1,128)S(1)}, f32[2,20,1,1]{1,3,2,0:T(1,128)}, u32[]{:S(2)}) copy-start(f32[2,20,1,1]{1,3,2,0:T(1,128)} %get-tuple-element.2313) | copy-start | bytes 484 | tf_op jit(solution)/shard_map/transpose(jvp())/while
  348.8 7.2 %copy-start.11 = (f32[2,256,128]{2,1,0:T(8,128)S(1)}, f32[2,256,128]{2,1,0:T(8,128)}, u32[]{:S(2)}) copy-start(f32[2,256,128]{2,1,0:T(8,128)} %get-tuple-element.2315) | copy-start | bytes 786436 | tf_op jit(solution)/shard_map/transpose(jvp())/while
  357.5 8.7 %copy-start.7 = (f32[2,256,128]{2,1,0:T(8,128)}, f32[2,256,128]{2,1,0:T(8,128)S(1)}, u32[]{:S(2)}) copy-start(f32[2,256,128]{2,1,0:T(8,128)S(1)} %get-tuple-element.2305) | copy-start | bytes 786436 | tf_op jit(solution)/shard_map/transpose(jvp())/while
  383.3 10.1 %copy-start.12 = (f32[20,256]{0,1:T(8,128)S(1)}, f32[20,256]{0,1:T(8,128)}, u32[]{:S(2)}) copy-start(f32[20,256]{0,1:T(8,128)} %copy.294) | copy-start | bytes 61444 | tf_op jit(solution)/shard_map/transpose(jvp())/while
  402.1 9.8 %copy-start.10 = (f32[2,256,128]{2,1,0:T(8,128)S(1)}, f32[2,256,128]{2,1,0:T(8,128)}, u32[]{:S(2)}) copy-start(f32[2,256,128]{2,1,0:T(8,128)} %get-tuple-element.2315) | copy-start | bytes 786436 | tf_op jit(solution)/shard_map/transpose(jvp())/while
  402.1 7.5 %copy-start.4 = (f32[2,20,64,256]{3,2,1,0:T(8,128)S(1)}, f32[2,20,64,256]{3,2,1,0:T(8,128)}, u32[]{:S(2)}) copy-start(f32[2,20,64,256]{3,2,1,0:T(8,128)} %get-tuple-element.2318) | copy-start | bytes 7864324 | tf_op jit(solution)/shard_map/transpose(jvp())/while
  402.1 9.8 %copy-start.13 = (f32[256,256]{1,0:T(8,128)S(1)}, f32[256,256]{1,0:T(8,128)}, u32[]{:S(2)}) copy-start(f32[256,256]{1,0:T(8,128)} %get-tuple-element.2142) | copy-start | bytes 786436 | tf_op jit(solution)/shard_map/transpose(jvp())/while
  402.1 9.8 %copy-start.28 = (f32[2,256,128]{2,1,0:T(8,128)S(1)}, f32[2,256,128]{2,1,0:T(8,128)}, u32[]{:S(2)}) copy-start(f32[2,256,128]{2,1,0:T(8,128)} %get-tuple-element.2265) | copy-start | bytes 786436 | tf_op jit(solution)/shard_map/transpose(jvp())/while
  404.2 9.0 %copy-start.1 = (f32[20,64,256]{2,1,0:T(8,128)S(1)}, f32[20,64,256]{2,1,0:T(8,128)}, u32[]{:S(2)}) copy-start(f32[20,64,256]{2,1,0:T(8,128)} %get-tuple-element.2140) | copy-start | bytes 3932164 | tf_op jit(solution)/shard_map/transpose(jvp())/while
  413.2 6.9 %copy-start.11 = (f32[2,256,128]{2,1,0:T(8,128)S(1)}, f32[2,256,128]{2,1,0:T(8,128)}, u32[]{:S(2)}) copy-start(f32[2,256,128]{2,1,0:T(8,128)} %get-tuple-element.2315) | copy-start | bytes 786436 | tf_op jit(solution)/shard_map/transpose(jvp())/while
  429.5 33.5 %copy-start.36 = (f32[2,20,256]{2,1,0:T(8,128)S(1)}, f32[2,20,256]{2,1,0:T(8,128)}, u32[]{:S(2)}) copy-start(f32[2,20,256]{2,1,0:T(8,128)} %get-tuple-element.974) | copy-start | bytes 122884
  429.5 33.6 %copy-start.33 = (f32[1,20,512]{2,0,1:T(1,128)S(1)}, f32[1,20,512]{2,0,1:T(1,128)}, u32[]{:S(2)}) copy-start(f32[1,20,512]{2,0,1:T(1,128)} %param.15) | copy-start | bytes 122884
  429.5 34.5 %copy-start.30 = (f32[2,256,128]{2,1,0:T(8,128)S(1)}, f32[2,256,128]{2,1,0:T(8,128)}, u32[]{:S(2)}) copy-start(f32[2,256,128]{2,1,0:T(8,128)} %get-tuple-element.972) | copy-start | bytes 786436
  429.5 34.5 %copy-start.31 = (f32[2,256,128]{2,1,0:T(8,128)S(1)}, f32[2,256,128]{2,1,0:T(8,128)}, u32[]{:S(2)}) copy-start(f32[2,256,128]{2,1,0:T(8,128)} %get-tuple-element.973) | copy-start | bytes 786436
  (41 other events, 97.5 us)
Sparse Core Ops, SparseCore 0:
  9.6 41.7 all-gather.12
  52.9 17.1 all-gather.8
  72.2 87.4 all-gather.10
  161.7 84.4 all-gather.14
  268.2 136.5 reduce-scatter.1
where the time goes:
time: 498 us; the launch traced here: 489 us
  matrix products  127 us (26%)
  local copies, waits for them, and re-layouts  104 us (21%)
  waiting for transfers between devices  102 us (20%)
  blocking collectives  69.4 us (14%)
  other arithmetic  68.7 us (14%)
  between operations  15 us (3%)
    all_gather x1, waiting for transfers between devices, per_device(): shard_part = lax.all_gather(local_state[None], 'seq', axis=0, tiled=True)  78.6 us
    dot_general x6, matrix products, span_pass(): block_out = jnp.einsum('hps,hts->hpt', x_block, scores, precision=HIGH)  50 us
    psum x1, blocking collectives, per_device(): grad_alog, grad_skip = lax.psum((grads[4], grads[5]), ('seq', 'dp'))  30.3 us
    dynamic_update_slice x10, other arithmetic, sweep(): lax.scan(advance, state_in, (x_blocks, b_blocks, c_blocks, s_blocks))  26.8 us
    unnamed x1, blocking collectives  23.1 us
    another operation x34, local copies, waits for them, and re-layouts  21.8 us
    all_gather x1, waiting for transfers between devices, per_device(): lax.all_gather(w_out, 'dp', axis=1, tiled=True)  18.7 us
    dynamic_slice x14, local copies, waits for them, and re-layouts, sweep(): lax.scan(advance, state_in, (x_blocks, b_blocks, c_blocks, s_blocks))  16.3 us
  transfers between devices with their start and end apart: 5, of which 3 were waited for; matrix products, arithmetic and copies ran while one was open for 58% of the time, Pallas kernels for 0%

commit v1 on v0

v1 whole, which is shorter than its diff:
```python
import jax
import jax.numpy as jnp
from jax import lax
from jax.sharding import PartitionSpec as P

HEAD_DIM = 64
HIGHEST = lax.Precision.HIGHEST
HIGH = lax.Precision.HIGH
F32 = jnp.float32
BF16 = jnp.bfloat16


def swap(value, axis, size, bit):
    return lax.ppermute(value, axis, [(i, i ^ bit) for i in range(size)])


def shifted(value, axis, size, step):
    pairs = [(i, i + step) for i in range(size) if 0 <= i + step < size]
    return lax.ppermute(value, axis, pairs)


def butterfly(value, axis, size):
    bit = 1
    while bit < size:
        value = value + swap(value, axis, size, bit)
        bit *= 2
    return value


def pack(state, total):
    heads, rows, lanes = state.shape
    high = lax.reduce_precision(total, 8, 7)
    middle = lax.reduce_precision(total - high, 8, 7)
    low = total - high - middle
    terms = jnp.stack([high, middle, low]).astype(BF16)
    extra = jnp.pad(terms, ((0, rows - 3), (0, lanes - heads)))
    return jnp.concatenate([state.astype(BF16), extra[None]], axis=0)


def unpack(payload):
    heads = payload.shape[0] - 1
    terms = payload[heads, :3, :heads].astype(F32)
    return payload[:heads].astype(F32), terms[0] + terms[1] + terms[2]


def decay(total):
    return jnp.exp(total)[:, None, None]


def pair_scan(local, total, n_seq, reverse):
    heads, width, lanes = local.shape
    place = lax.axis_index("seq")
    upper = lax.rem(place, 2) == 1
    late = jnp.logical_not(upper) if reverse else upper
    halves = local.reshape(heads, 2, width // 2, lanes)
    mine = jnp.where(upper, halves[:, 1], halves[:, 0])
    theirs = jnp.where(upper, halves[:, 0], halves[:, 1])
    other, other_total = unpack(swap(pack(theirs, total), "seq", n_seq, 1))
    mine = mine.astype(BF16).astype(F32)
    first = jnp.where(late, other, mine)
    second = jnp.where(late, mine, other)
    first_total = jnp.where(late, other_total, total)
    second_total = jnp.where(late, total, other_total)
    span = decay(second_total) * first + second
    span_total = first_total + second_total
    before, before_total = jnp.zeros_like(span), jnp.zeros_like(span_total)
    step = 2
    while step < n_seq:
        moved = shifted(pack(span, span_total), "seq", n_seq, -step if reverse else step)
        earlier, earlier_total = unpack(moved)
        before = decay(before_total) * earlier + before
        span = decay(span_total) * earlier + span
        before_total = before_total + earlier_total
        span_total = span_total + earlier_total
        step *= 2
    for_first = before.astype(BF16)
    for_second = (decay(first_total) * before + first).astype(BF16)
    keep = jnp.where(late, for_second, for_first)
    give = jnp.where(late, for_first, for_second)
    got = swap(give, "seq", n_seq, 1)
    low = jnp.where(upper, got, keep)
    high = jnp.where(upper, keep, got)
    return jnp.concatenate([low[:, None], high[:, None]], axis=1).reshape(heads * width, lanes)


def per_device(mesh, head_inputs, b_proj, c_proj, dt_raw, a_log, d_skip, w_out, out_grad):
    n_seq, n_dp, n_tensor = mesh.shape["seq"], mesh.shape["dp"], mesh.shape["tensor"]
    x, b, c, dt, g = head_inputs[0], b_proj[0], c_proj[0], dt_raw[0], out_grad[0]
    heads, length = dt.shape
    channels = heads * HEAD_DIM
    features = g.shape[0]
    all_features = features * n_tensor
    out_columns = all_features // (n_seq * n_dp)
    my_dp, my_tensor, my_seq = (lax.axis_index(a) for a in ("dp", "tensor", "seq"))

    def rows(values):
        spread = jnp.broadcast_to(values[:, None, :], (heads, HEAD_DIM, values.shape[1]))
        return spread.reshape(channels, values.shape[1])

    def head_sum(values):
        return jnp.sum(values.reshape(heads, HEAD_DIM, values.shape[1]), axis=1)

    if n_tensor == 2:
        g_other = swap(g, "tensor", 2, 1)
        g_full = jnp.where(
            my_tensor == 0, jnp.concatenate([g, g_other]), jnp.concatenate([g_other, g])
        )
    else:
        g_full = lax.all_gather(g, "tensor", axis=0, tiled=True)
    w_other = swap(w_out, "dp", 2, 1)
    w_full = jnp.where(
        my_dp == 0,
        jnp.concatenate([w_out, w_other], axis=1),
        jnp.concatenate([w_other, w_out], axis=1),
    )

    step_size = jax.nn.softplus(dt)
    rate = -jnp.exp(a_log)[:, None]
    log_decay = step_size * rate
    token = jnp.arange(length)
    causal = token[:, None] <= token[None, :]
    cumulative = jnp.dot(log_decay, causal.astype(F32), precision=HIGHEST)
    total = cumulative[:, -1]
    grown = rows(jnp.exp(cumulative))
    shrunk = rows(step_size * jnp.exp(-cumulative))
    skip = rows(d_skip[:, None])
    end_decay = rows(jnp.exp(total)[:, None])

    xs = x.astype(F32) * shrunk
    b32, c32 = b.astype(F32), c.astype(F32)
    gathered = jnp.dot(xs, b32, precision=HIGH)
    local_state = (end_decay * gathered).reshape(heads, HEAD_DIM, -1)
    state_in = pair_scan(local_state, total, n_seq, False)
    affinity_t = lax.dot_general(b, c, (((1,), (1,)), ((), ())), preferred_element_type=F32)
    affinity_t = jnp.where(causal, affinity_t, 0.0)
    inner = jnp.dot(xs, affinity_t, precision=HIGH) + lax.dot_general(
        state_in, c, (((1,), (1,)), ((), ())), preferred_element_type=F32
    )
    mixed = (grown * inner + skip * x.astype(F32)).astype(BF16)

    blocks = g_full.reshape(n_seq, n_dp, out_columns, length)
    g_mine = jnp.where(my_dp == 0, blocks[:, 0], blocks[:, 1])
    g_theirs = jnp.where(my_dp == 0, blocks[:, 1], blocks[:, 0])
    g_pair = jnp.concatenate([g_mine, swap(g_theirs, "dp", 2, 1)], axis=2)
    mixed_pair = jnp.concatenate([mixed, swap(mixed, "dp", 2, 1)], axis=1)

    def halving(mixed_rows, bits):
        n_bits = n_seq.bit_length() - 1
        operand = g_pair.reshape((2,) * n_bits + (out_columns, 2 * length))
        held = None
        left = list(range(n_bits))
        for bit in bits:
            mine = jnp.bitwise_and(my_seq >> bit, 1) == 1
            axis = left.index(n_bits - 1 - bit)
            left.remove(n_bits - 1 - bit)
            source = operand if held is None else held
            zero = lax.index_in_dim(source, 0, axis, keepdims=False)
            one = lax.index_in_dim(source, 1, axis, keepdims=False)
            keep, send = jnp.where(mine, one, zero), jnp.where(mine, zero, one)
            if held is None:
                product = lambda part: lax.dot_general(
                    part, mixed_rows, (((part.ndim - 1,), (1,)), ((), ())), preferred_element_type=F32
                )
                keep, send = product(keep), product(send)
            got = swap(send.astype(BF16), "seq", n_seq, 1 << bit)
            held = keep + got.astype(F32)
        return held

    n_bits = n_seq.bit_length() - 1
    half = channels // 2
    order_a = list(range(n_bits))
    order_b = [1, 0] + order_a[2:]
    grad_w = jnp.concatenate(
        [halving(mixed_pair[:half], order_a), halving(mixed_pair[half:], order_b)], axis=1
    ).T.astype(BF16)

    y_cotan = jnp.dot(w_full, g_full, preferred_element_type=F32)
    y_cotan = lax.optimization_barrier(y_cotan.astype(BF16))
    gs = y_cotan.astype(F32) * grown
    local_cotan = jnp.dot(gs, c32, precision=HIGH).reshape(heads, HEAD_DIM, -1)
    cotan_in = pair_scan(local_cotan, total, n_seq, True)
    cotan_end = (end_decay * cotan_in.astype(F32)).astype(BF16)
    outer = lax.dot_general(
        gs, affinity_t, (((1,), (1,)), ((), ())), precision=HIGH
    ) + lax.dot_general(cotan_end, b, (((1,), (1,)), ((), ())), preferred_element_type=F32)
    grad_inputs = (shrunk * outer + skip * y_cotan.astype(F32)).astype(BF16)
    across = lax.dot_general(xs, gs, (((0,), (0,)), ((), ())), precision=HIGH)
    across = jnp.where(causal, across, 0.0)
    grad_b = jnp.dot(across, c32, precision=HIGH) + lax.dot_general(
        xs.astype(BF16), cotan_end, (((0,), (0,)), ((), ())), preferred_element_type=F32
    )
    grad_c = lax.dot_general(
        across, b32, (((0,), (0,)), ((), ())), precision=HIGH
    ) + lax.dot_general(gs.astype(BF16), state_in, (((0,), (0,)), ((), ())), preferred_element_type=F32)
    grad_bc = jnp.concatenate([grad_b, grad_c], axis=1)
    if n_tensor == 2:
        grad_bc = lax.reduce_precision(grad_bc, 8, 7)
        grad_bc = grad_bc + swap(grad_bc.astype(BF16), "tensor", 2, 1).astype(F32)
    else:
        grad_bc = lax.psum(grad_bc, "tensor")
    grad_bc = grad_bc.astype(BF16)

    from_y = head_sum(gs.astype(F32) * inner)
    from_x = head_sum(xs.astype(F32) * outer)
    ends = cotan_end.astype(F32) * (gathered + state_in.astype(F32))
    from_end = jnp.sum(head_sum(ends), axis=1, keepdims=True)
    flow = jnp.dot(from_y - from_x, causal.astype(F32).T, precision=HIGHEST) + from_end
    grad_dt = (from_x / step_size + flow * rate) * jax.nn.sigmoid(dt)
    alog_part = jnp.sum(flow * log_decay, axis=1)
    skip_part = jnp.sum(head_sum(y_cotan.astype(F32) * x.astype(F32)), axis=1)
    small = jnp.stack([alog_part, skip_part])
    small = butterfly(butterfly(small, "dp", n_dp), "seq", n_seq)
    n_state = b.shape[1]
    return (
        mixed[None],
        grad_inputs[None],
        grad_bc[None, :, :n_state],
        grad_bc[None, :, n_state:],
        grad_dt[None],
        small[0],
        small[1],
        grad_w,
    )


def solution(mesh):
    in_specs = (
        P("dp", "tensor", "seq"),
        P("dp", "seq", None),
        P("dp", "seq", None),
        P("dp", "tensor", "seq"),
        P("tensor"),
        P("tensor"),
        P("tensor", "dp"),
        P("dp", "tensor", "seq"),
    )
    out_specs = (
        P("dp", "tensor", "seq"),
        P("dp", "tensor", "seq"),
        P("dp", "seq", None),
        P("dp", "seq", None),
        P("dp", "tensor", "seq"),
        P("tensor"),
        P("tensor"),
        P("tensor", ("seq", "dp")),
    )

    def whole(*args):
        return per_device(mesh, *args)

    return jax.shard_map(
        whole, mesh=mesh, in_specs=in_specs, out_specs=out_specs, check_vma=False
    )
```

time: 498 us -> 177 us (0.36); the launches traced: 489 us -> 176 us
  local copies, waits for them, and re-layouts: 104 us -> 9.53 us
  matrix products: 127 us -> 42.5 us
  blocking collectives: 69.4 us -> 0 us
  other arithmetic: 68.7 us -> 16.1 us
  starting transfers between devices: 0.45 us -> 40.1 us
  waiting for transfers between devices: 102 us -> 66.6 us
  between operations: 15 us -> 1.34 us
    all_gather x4 -> x0, waiting for transfers between devices: 101 us -> none  [the longest x1 78.6 us: per_device(): shard_part = lax.all_gather(local_state[None], 'seq', axis=0, tiled=True)]
    dot_general x30 -> x19, matrix products: 127 us -> 42.5 us  [the longest x4 9.99 us: halving(): lax.dot_general(part, mixed_rows, (((part.ndim - 1,), (1,)), ((), ())), p...]
    ppermute x0 -> x23, waiting for transfers between devices: none -> 66.6 us  [the longest x19 62.6 us: swap(): return lax.ppermute(value, axis, [(i, i ^ bit) for i in range(size)])]
    psum x2 -> x0, blocking collectives: 46.3 us -> none  [the longest x1 30.3 us: per_device(): grad_alog, grad_skip = lax.psum((grads[4], grads[5]), ('seq', 'dp'))]
    ppermute x0 -> x23, starting transfers between devices: none -> 40.1 us  [the longest x19 27.1 us: swap(): return lax.ppermute(value, axis, [(i, i ^ bit) for i in range(size)])]
    dynamic_update_slice x10 -> x0, other arithmetic: 26.8 us -> none  [sweep(): lax.scan(advance, state_in, (x_blocks, b_blocks, c_blocks, s_blocks))]
    another operation x36 -> x0, local copies, waits for them, and re-layouts: 26.6 us -> none
    unnamed x1 -> x0, blocking collectives: 23.1 us -> none
  transfers between devices with their start and end apart: 5 -> 23, of which waited for: 3 -> 15; matrix products, arithmetic and copies ran while one was open for 58% -> 19% of each run, Pallas kernels for 0% -> 0%
where the time goes in v1:
time: 177 us; the launch traced here: 176 us
  waiting for transfers between devices  66.6 us (38%)
  matrix products  42.5 us (24%)
  starting transfers between devices  40.1 us (23%)
  other arithmetic  16.1 us (9%)
  local copies, waits for them, and re-layouts  9.53 us (5%)
    ppermute x19, waiting for transfers between devices, swap(): return lax.ppermute(value, axis, [(i, i ^ bit) for i in range(size)])  62.6 us
    ppermute x19, starting transfers between devices, swap(): return lax.ppermute(value, axis, [(i, i ^ bit) for i in range(size)])  27.1 us
    ppermute x4, starting transfers between devices, shifted(): return lax.ppermute(value, axis, pairs)  13 us
    dot_general x4, matrix products, halving(): lax.dot_general(part, mixed_rows, (((part.ndim - 1,), (1,)), ((), ())), p...  9.99 us
    dot_general x1, matrix products, per_device(): y_cotan = jnp.dot(w_full, g_full, preferred_element_type=F32)  6.87 us
    unnamed x49, local copies, waits for them, and re-layouts  6.28 us
    dot_general x1, matrix products, per_device(): lax.dot_general(state_in, c, (((1,), (1,)), ((), ())), preferred_element_...  4.56 us
    reduce_sum x2, other arithmetic, head_sum(): return jnp.sum(values.reshape(heads, HEAD_DIM, values.shape[1]), axis=1)  4.22 us
  transfers between devices with their start and end apart: 23, of which 15 were waited for; matrix products, arithmetic and copies ran while one was open for 19% of the time, Pallas kernels for 0%

profile of v1, /device:TPU:0, one launch (start us, length us, event | category | flops | bytes accessed | tf_op | source)
XLA Modules:
  0.0 176.1 jit_solution(17901849282657812531)
XLA Ops:
  0.7 3.0 %collective-permute-start.5 = (bf16[1280,512]{1,0:T(8,128)(2,1)}, bf16[1280,512]{1,0:T(8,128)(2,1)S(1)}, u32[]{:S(2)}, u32[]{:S(2)}) collective-permute-start(bf16[1280,512]{1,0:T(8,128)(2,1)} %bitcast.359), channel_id=1, source_target_pairs={{0,1},{1,0},{2,3},{3,2},{4,5},{5,4},{6,7},{7,6},{8,9},{9,8},{10,11... | collective-permute-start | bytes 3932168 | tf_op jit(solution)/shard_map/ppermute | solution.py:14
  7.4 1.8 %bitcast_multiply_fusion.1 = f32[1280,512]{1,0:T(8,128)S(1)} fusion(bf16[1,1280,512]{2,1,0:T(8,128)(2,1)} %param.8, f32[20,512]{1,0:T(8,128)S(1)} %get-tuple-element.82), kind=kLoop, calls=%fused_computation.9 | loop fusion | flops 1310720 | bytes 3973120 | tf_op jit(solution)/shard_map/mul | solution.py:129
  9.5 23.2 %collective-permute-done.5 = bf16[1280,512]{1,0:T(8,128)(2,1)S(1)} collective-permute-done((bf16[1280,512]{1,0:T(8,128)(2,1)}, bf16[1280,512]{1,0:T(8,128)(2,1)S(1)}, u32[]{:S(2)}, u32[]{:S(2)}) %collective-permute-start.5) | collective-permute-done | bytes 1310752 | tf_op jit(solution)/shard_map/ppermute | solution.py:14
  37.2 3.8 %fusion.164 = f32[1280,512]{1,0:T(8,128)} fusion(f32[1280,512]{1,0:T(8,128)S(1)} %bitcast_multiply_fusion.1, f32[512,512]{1,0:T(8,128)S(1)} %convolution_select_fusion.1), kind=kOutput, calls=%fused_computation.283 | convolution fusion | flops 2013265920 | bytes 6291456 | tf_op jit(solution)/shard_map/dot_general | solution.py:136
  45.3 6.9 %fusion.7 = bf16[1280,512]{1,0:T(8,128)(2,1)S(1)} fusion(bf16[2560,512]{1,0:T(8,128)(2,1)S(1)} %maximum_select_fusion.4, bf16[1280,1280]{1,0:T(8,128)(2,1)} %collective-permute-done.4, bf16[1280,1280]{1,0:T(8,128)(2,1)S(1)} %copy-done.20, pred[]{:T(512)S(6)} %eq.25), kind=kOutput, calls=%fused_computation.16 | convolution fusion | flops 3385589760 | bytes 10485761 | tf_op jit(solution)/shard_map/dot_general | solution.py:177
  52.6 3.8 %fusion.165 = f32[1280,512]{1,0:T(8,128)} fusion(f32[1280,512]{1,0:T(8,128)S(1)} %bitcast_multiply_fusion.2, f32[512,512]{1,0:T(8,128)S(1)} %convolution_select_fusion.1), kind=kOutput, calls=%fused_computation.284 | convolution fusion | flops 2013265920 | bytes 6291456 | tf_op jit(solution)/shard_map/dot_general | solution.py:183
  56.3 2.2 %convolution_select_fusion = f32[512,512]{1,0:T(8,128)S(1)} fusion(f32[1280,512]{1,0:T(8,128)S(1)} %bitcast_multiply_fusion.1, f32[1280,512]{1,0:T(8,128)S(1)} %bitcast_multiply_fusion.2), kind=kOutput, calls=%fused_computation.32 | convolution fusion | flops 2013790208 | bytes 6291456 | tf_op jit(solution)/shard_map/dot_general | solution.py:187
  63.9 3.0 %collective-permute-done.6 = bf16[21,32,128]{2,1,0:T(8,128)(2,1)S(1)} collective-permute-done((bf16[21,32,128]{2,1,0:T(8,128)(2,1)S(1)}, bf16[21,32,128]{2,1,0:T(8,128)(2,1)S(1)}, u32[]{:S(2)}, u32[]{:S(2)}) %collective-permute-start.6) | collective-permute-done | bytes 172064 | tf_op jit(solution)/shard_map/ppermute | solution.py:14
  66.9 2.1 %collective-permute-done = bf16[21,32,128]{2,1,0:T(8,128)(2,1)S(1)} collective-permute-done((bf16[21,32,128]{2,1,0:T(8,128)(2,1)S(1)}, bf16[21,32,128]{2,1,0:T(8,128)(2,1)S(1)}, u32[]{:S(2)}, u32[]{:S(2)}) %collective-permute-start) | collective-permute-done | bytes 172064 | tf_op jit(solution)/shard_map/ppermute | solution.py:14
  70.7 4.6 %collective-permute-start.1 = (bf16[21,32,128]{2,1,0:T(8,128)(2,1)S(1)}, bf16[21,32,128]{2,1,0:T(8,128)(2,1)S(1)}, u32[]{:S(2)}, u32[]{:S(2)}) collective-permute-start(bf16[21,32,128]{2,1,0:T(8,128)(2,1)S(1)} %pad_maximum_fusion.5), channel_id=1, source_target_pairs={{0,8},{4,12},{8,16},{12,20},{16,24},{20,28},{1,9},{5,13},{9,17},{1... | collective-permute-start | bytes 516104 | tf_op jit(solution)/shard_map/ppermute | solution.py:19
  78.4 5.9 %collective-permute-start.2 = (bf16[21,32,128]{2,1,0:T(8,128)(2,1)S(1)}, bf16[21,32,128]{2,1,0:T(8,128)(2,1)S(1)}, u32[]{:S(2)}, u32[]{:S(2)}) collective-permute-start(bf16[21,32,128]{2,1,0:T(8,128)(2,1)S(1)} %pad_maximum_fusion.6), channel_id=1, source_target_pairs={{0,16},{4,20},{8,24},{12,28},{1,17},{5,21},{9,25},{13,29},{2,18},{... | collective-permute-start | bytes 516104 | tf_op jit(solution)/shard_map/ppermute | solution.py:19
  84.3 2.7 %collective-permute-done.8 = bf16[21,32,128]{2,1,0:T(8,128)(2,1)S(1)} collective-permute-done((bf16[21,32,128]{2,1,0:T(8,128)(2,1)S(1)}, bf16[21,32,128]{2,1,0:T(8,128)(2,1)S(1)}, u32[]{:S(2)}, u32[]{:S(2)}) %collective-permute-start.8) | collective-permute-done | bytes 172064 | tf_op jit(solution)/shard_map/ppermute | solution.py:19
  89.5 3.0 %collective-permute-done.9 = bf16[20,32,128]{2,1,0:T(8,128)(2,1)S(1)} collective-permute-done((bf16[20,32,128]{2,1,0:T(8,128)(2,1)S(1)}, bf16[20,32,128]{2,1,0:T(8,128)(2,1)S(1)}, u32[]{:S(2)}, u32[]{:S(2)}) %collective-permute-start.9) | collective-permute-done | bytes 163872 | tf_op jit(solution)/shard_map/ppermute | solution.py:14
  96.4 2.4 %convolution_add_fusion = f32[1280,512]{1,0:T(8,128)S(1)} fusion(f32[1280,512]{1,0:T(8,128)} %fusion.165, bf16[1280,128]{1,0:T(8,128)(2,1)S(1)} %bitcast.355, bf16[1,512,128]{2,1,0:T(8,128)(2,1)S(1)} %copy-done.9), kind=kOutput, calls=%fused_computation.14 | convolution fusion | flops 168427520 | bytes 5701632 | tf_op jit(solution)/shard_map/dot_general | solution.py:185
  99.7 4.6 %fusion.39 = (f32[1280,512]{1,0:T(8,128)}, bf16[1280,512]{1,0:T(8,128)(2,1)}, bf16[1280,512]{1,0:T(8,128)(2,1)}, f32[1280,512]{1,0:T(8,128)}, f32[1280]{0:T(1024)S(1)}) fusion(f32[20,512]{1,0:T(8,128)S(1)} %copy-done.18, bf16[1280,512]{1,0:T(8,128)(2,1)S(1)} %copy-done.7, bf16[1,1280,512]{2,1,0:T(8,128)(2,1)S(1)} %copy-done.2, f32[1280]{0:T(1024)S(1)} %copy-done.19, ...), kind=kOutput, calls=%fused_computation.75 | convolution fusion | flops 178912000 | bytes 16279552 | tf_op jit(solution)/shard_map/dot_general | solution.py:136
  104.3 2.1 %reduce_sum.67 = f32[20,512]{1,0:T(8,128)S(1)} reduce(f32[20,64,512]{2,1,0:T(8,128)} %bitcast.345, f32[]{:T(128)} %constant.9.clone.1), dimensions={1}, to_apply=%region_0.1 | reduce | flops 645120 | bytes 2662404 | tf_op jit(solution)/shard_map/reduce_sum | solution.py:101
  106.5 2.1 %reduce_sum.68 = f32[20,512]{1,0:T(8,128)S(1)} reduce(f32[20,64,512]{2,1,0:T(8,128)} %bitcast.344, f32[]{:T(128)} %constant.9.clone.1), dimensions={1}, to_apply=%region_1.2 | reduce | flops 645120 | bytes 2662404 | tf_op jit(solution)/shard_map/reduce_sum | solution.py:101
  117.6 2.1 %collective-permute-done.13 = f32[2,20]{1,0:T(2,128)S(1)} collective-permute-done((f32[2,20]{1,0:T(2,128)S(1)}, f32[2,20]{1,0:T(2,128)S(1)}, u32[]{:S(2)}, u32[]{:S(2)}) %collective-permute-start.13) | collective-permute-done | bytes 192 | tf_op jit(solution)/shard_map/ppermute | solution.py:14
  119.8 2.8 %collective-permute-start.14 = (f32[2,20]{1,0:T(2,128)S(1)}, f32[2,20]{1,0:T(2,128)S(1)}, u32[]{:S(2)}, u32[]{:S(2)}) collective-permute-start(f32[2,20]{1,0:T(2,128)S(1)} %add.339), channel_id=1, source_target_pairs={{0,16},{4,20},{8,24},{12,28},{16,0},{20,4},{24,8},{28,12},{1,17},{... | collective-permute-start | bytes 488 | tf_op jit(solution)/shard_map/ppermute | solution.py:14
  125.3 2.2 %convolution_convert_fusion = bf16[2,2,160,640]{3,2,0,1:T(8,128)(2,1)} fusion(bf16[2,2,160,1024]{3,2,1,0:T(8,128)(2,1)S(1)} %copy-done.13, bf16[1280,512]{1,0:T(8,128)(2,1)S(1)} %collective-permute-done.16, bf16[1280,512]{1,0:T(8,128)(2,1)S(1)} %copy-done.10), kind=kOutput, calls=%fused_computation.30 | convolution fusion | flops 841891840 | bytes 4751360 | tf_op jit(solution)/shard_map/dot_general | solution.py:161
  127.4 2.0 %collective-permute-start.20 = (bf16[2,2,160,640]{3,2,0,1:T(8,128)(2,1)}, bf16[2,2,160,640]{3,2,0,1:T(8,128)(2,1)}, u32[]{:S(2)}, u32[]{:S(2)}) collective-permute-start(bf16[2,2,160,640]{3,2,0,1:T(8,128)(2,1)} %convolution_convert_fusion), channel_id=1, source_target_pairs={{0,8},{4,12},{8,0},{12,4},{16,24},{20,28},{24,16},{28,20},{1,9},{5... | collective-permute-start | bytes 2457608 | tf_op jit(solution)/shard_map/ppermute | solution.py:14
  129.5 2.2 %convolution_convert_fusion.1 = bf16[2,2,160,640]{3,2,1,0:T(8,128)(2,1)} fusion(pred[]{:T(512)S(6)} %eq.29, bf16[2,2,2,160,1024]{4,3,2,1,0:T(8,128)(2,1)S(1)} %bitcast.348, bf16[1280,512]{1,0:T(8,128)(2,1)S(1)} %copy-done.10, bf16[1280,512]{1,0:T(8,128)(2,1)S(1)} %collective-permute-done.16), kind=kOutput, calls=%fused_computation.31 | convolution fusion | flops 842547200 | bytes 6062081 | tf_op jit(solution)/shard_map/dot_general | solution.py:161
  134.7 10.6 %collective-permute-done.20 = bf16[2,2,160,640]{3,2,0,1:T(8,128)(2,1)} collective-permute-done((bf16[2,2,160,640]{3,2,0,1:T(8,128)(2,1)}, bf16[2,2,160,640]{3,2,0,1:T(8,128)(2,1)}, u32[]{:S(2)}, u32[]{:S(2)}) %collective-permute-start.20) | collective-permute-done | bytes 819232 | tf_op jit(solution)/shard_map/ppermute | solution.py:14
  145.3 3.3 %convert_add_fusion = f32[2,2,160,640]{3,2,0,1:T(8,128)S(1)} fusion(bf16[2,2,160,640]{3,2,0,1:T(8,128)(2,1)} %collective-permute-done.20, bf16[2,2,160,1024]{3,2,1,0:T(8,128)(2,1)} %get-tuple-element.71, bf16[1280,512]{1,0:T(8,128)(2,1)} %copy-done.21, bf16[1280,512]{1,0:T(8,128)(2,1)} %get-tuple-element.67), kind=kOutput, calls=%fused_computation.28 | convolution fusion | flops 842301440 | bytes 6389760 | tf_op jit(solution)/shard_map/dot_general | solution.py:161
  150.3 2.4 %convert_add_fusion.1 = f32[2,2,160,640]{3,2,1,0:T(8,128)S(1)} fusion(bf16[2,2,160,640]{3,2,1,0:T(8,128)(2,1)} %collective-permute-done.17, pred[]{:T(512)S(6)} %eq.29, bf16[2,2,2,160,1024]{4,3,2,1,0:T(8,128)(2,1)S(1)} %bitcast.349, bf16[1280,512]{1,0:T(8,128)(2,1)S(1)} %copy-done.11, bf16[1280,512]{1,0:T(8,128)(2,1)S(1)} %copy-done.22), kind=kOutput, calls=%fused_computation.29 | convolution fusion | flops 842956800 | bytes 7700481 | tf_op jit(solution)/shard_map/dot_general | solution.py:161
  152.7 1.8 %collective-permute-start.18 = (bf16[2,160,640]{2,1,0:T(8,128)(2,1)S(1)}, bf16[2,160,640]{2,1,0:T(8,128)(2,1)S(1)}, u32[]{:S(2)}, u32[]{:S(2)}) collective-permute-start(bf16[2,160,640]{2,1,0:T(8,128)(2,1)S(1)} %fusion.41), channel_id=1, source_target_pairs={{0,8},{4,12},{8,0},{12,4},{16,24},{20,28},{24,16},{28,20},{1,9},{5... | collective-permute-start | bytes 1228808 | tf_op jit(solution)/shard_map/ppermute | solution.py:14
  154.5 3.2 %collective-permute-done.21 = bf16[2,160,640]{2,1,0:T(8,128)(2,1)S(1)} collective-permute-done((bf16[2,160,640]{2,1,0:T(8,128)(2,1)S(1)}, bf16[2,160,640]{2,1,0:T(8,128)(2,1)S(1)}, u32[]{:S(2)}, u32[]{:S(2)}) %collective-permute-start.21) | collective-permute-done | bytes 409632 | tf_op jit(solution)/shard_map/ppermute | solution.py:14
  157.9 1.8 %collective-permute-start.22 = (bf16[160,640]{1,0:T(8,128)(2,1)S(1)}, bf16[160,640]{1,0:T(8,128)(2,1)S(1)}, u32[]{:S(2)}, u32[]{:S(2)}) collective-permute-start(bf16[160,640]{1,0:T(8,128)(2,1)S(1)} %fusion.58), channel_id=1, source_target_pairs={{0,16},{4,20},{8,24},{12,28},{16,0},{20,4},{24,8},{28,12},{1,17},{... | collective-permute-start | bytes 614408 | tf_op jit(solution)/shard_map/ppermute | solution.py:14
  159.6 4.0 %collective-permute-done.18 = bf16[2,160,640]{2,1,0:T(8,128)(2,1)S(1)} collective-permute-done((bf16[2,160,640]{2,1,0:T(8,128)(2,1)S(1)}, bf16[2,160,640]{2,1,0:T(8,128)(2,1)S(1)}, u32[]{:S(2)}, u32[]{:S(2)}) %collective-permute-start.18) | collective-permute-done | bytes 409632 | tf_op jit(solution)/shard_map/ppermute | solution.py:14
  163.8 3.3 %collective-permute-start.19 = (bf16[160,640]{1,0:T(8,128)(2,1)S(1)}, bf16[160,640]{1,0:T(8,128)(2,1)S(1)}, u32[]{:S(2)}, u32[]{:S(2)}) collective-permute-start(bf16[160,640]{1,0:T(8,128)(2,1)S(1)} %fusion.57), channel_id=1, source_target_pairs={{0,16},{4,20},{8,24},{12,28},{16,0},{20,4},{24,8},{28,12},{1,17},{... | collective-permute-start | bytes 614408 | tf_op jit(solution)/shard_map/ppermute | solution.py:14
  167.1 5.9 %collective-permute-done.22 = bf16[160,640]{1,0:T(8,128)(2,1)S(1)} collective-permute-done((bf16[160,640]{1,0:T(8,128)(2,1)S(1)}, bf16[160,640]{1,0:T(8,128)(2,1)S(1)}, u32[]{:S(2)}, u32[]{:S(2)}) %collective-permute-start.22) | collective-permute-done | bytes 204832 | tf_op jit(solution)/shard_map/ppermute | solution.py:14
  173.1 2.1 %collective-permute-done.19 = bf16[160,640]{1,0:T(8,128)(2,1)S(1)} collective-permute-done((bf16[160,640]{1,0:T(8,128)(2,1)S(1)}, bf16[160,640]{1,0:T(8,128)(2,1)S(1)}, u32[]{:S(2)}, u32[]{:S(2)}) %collective-permute-start.19) | collective-permute-done | bytes 204832 | tf_op jit(solution)/shard_map/ppermute | solution.py:14
  (163 shorter events, 48.2 us)
Async XLA Ops:
  0.6 8.6 %copy-start = (bf16[1,512,128]{2,1,0:T(8,128)(2,1)S(1)}, bf16[1,512,128]{2,1,0:T(8,128)(2,1)}, u32[]{:S(2)}) copy-start(bf16[1,512,128]{2,1,0:T(8,128)(2,1)} %param.10) | copy-start | bytes 393220
  0.6 8.6 %copy-start.9 = (bf16[1,512,128]{2,1,0:T(8,128)(2,1)S(1)}, bf16[1,512,128]{2,1,0:T(8,128)(2,1)}, u32[]{:S(2)}) copy-start(bf16[1,512,128]{2,1,0:T(8,128)(2,1)} %param.9) | copy-start | bytes 393220
  0.7 32.0 %collective-permute-start.5 = (bf16[1280,512]{1,0:T(8,128)(2,1)}, bf16[1280,512]{1,0:T(8,128)(2,1)S(1)}, u32[]{:S(2)}, u32[]{:S(2)}) collective-permute-start(bf16[1280,512]{1,0:T(8,128)(2,1)} %bitcast.359), channel_id=1, source_target_pairs={{0,1},{1,0},{2,3},{3,2},{4,5},{5,4},{6,7},{7,6},{8,9},{9,8},{10,11... | collective-permute-start | bytes 3932168 | tf_op jit(solution)/shard_map/ppermute | solution.py:14
  3.7 40.5 %collective-permute-start.4 = (bf16[1280,1280]{1,0:T(8,128)(2,1)}, bf16[1280,1280]{1,0:T(8,128)(2,1)}, u32[]{:S(2)}, u32[]{:S(2)}) collective-permute-start(bf16[1280,1280]{1,0:T(8,128)(2,1)} %param.14), channel_id=1, source_target_pairs={{0,2},{2,0},{1,3},{3,1},{4,6},{6,4},{5,7},{7,5},{8,10},{10,8},{9,1... | collective-permute-start | bytes 9830408 | tf_op jit(solution)/shard_map/ppermute | solution.py:14
  5.6 28.2 %copy-start.15 = (f32[20,512]{1,0:T(8,128)}, f32[20,512]{1,0:T(8,128)S(1)}, u32[]{:S(2)}) copy-start(f32[20,512]{1,0:T(8,128)S(1)} %get-tuple-element.82) | copy-start | bytes 122884
  5.6 46.6 %copy-start.17 = (f32[20,512]{1,0:T(8,128)}, f32[20,512]{1,0:T(8,128)S(1)}, u32[]{:S(2)}) copy-start(f32[20,512]{1,0:T(8,128)S(1)} %get-tuple-element.81) | copy-start | bytes 122884
  7.4 25.3 %copy-start.12 = (bf16[1,1280,512]{2,1,0:T(8,128)(2,1)S(1)}, bf16[1,1280,512]{2,1,0:T(8,128)(2,1)}, u32[]{:S(2)}) copy-start(bf16[1,1280,512]{2,1,0:T(8,128)(2,1)} %param.15) | copy-start | bytes 3932164
  33.7 7.5 %collective-permute-start.15 = (bf16[8,160,512]{2,1,0:T(8,128)(2,1)S(1)}, bf16[8,160,512]{2,1,0:T(8,128)(2,1)S(1)}, u32[]{:S(2)}, u32[]{:S(2)}) collective-permute-start(bf16[8,160,512]{2,1,0:T(8,128)(2,1)S(1)} %fusion.13), channel_id=1, source_target_pairs={{0,2},{2,0},{1,3},{3,1},{4,6},{6,4},{5,7},{7,5},{8,10},{10,8},{9,1... | collective-permute-start | bytes 3932168 | tf_op jit(solution)/shard_map/ppermute | solution.py:14
  59.5 7.4 %collective-permute-start.6 = (bf16[21,32,128]{2,1,0:T(8,128)(2,1)S(1)}, bf16[21,32,128]{2,1,0:T(8,128)(2,1)S(1)}, u32[]{:S(2)}, u32[]{:S(2)}) collective-permute-start(bf16[21,32,128]{2,1,0:T(8,128)(2,1)S(1)} %get-tuple-element.83), channel_id=1, source_target_pairs={{0,4},{4,0},{8,12},{12,8},{16,20},{20,16},{24,28},{28,24},{1,5},{5... | collective-permute-start | bytes 516104 | tf_op jit(solution)/shard_map/ppermute | solution.py:14
  61.3 7.7 %collective-permute-start = (bf16[21,32,128]{2,1,0:T(8,128)(2,1)S(1)}, bf16[21,32,128]{2,1,0:T(8,128)(2,1)S(1)}, u32[]{:S(2)}, u32[]{:S(2)}) collective-permute-start(bf16[21,32,128]{2,1,0:T(8,128)(2,1)S(1)} %get-tuple-element.84), channel_id=1, source_target_pairs={{0,4},{4,0},{8,12},{12,8},{16,20},{20,16},{24,28},{28,24},{1,5},{5... | collective-permute-start | bytes 516104 | tf_op jit(solution)/shard_map/ppermute | solution.py:14
  69.2 7.3 %collective-permute-start.7 = (bf16[21,32,128]{2,1,0:T(8,128)(2,1)S(1)}, bf16[21,32,128]{2,1,0:T(8,128)(2,1)S(1)}, u32[]{:S(2)}, u32[]{:S(2)}) collective-permute-start(bf16[21,32,128]{2,1,0:T(8,128)(2,1)S(1)} %pad_maximum_fusion.7), channel_id=1, source_target_pairs={{8,0},{12,4},{16,8},{20,12},{24,16},{28,20},{9,1},{13,5},{17,9},{2... | collective-permute-start | bytes 516104 | tf_op jit(solution)/shard_map/ppermute | solution.py:19
  70.7 7.5 %collective-permute-start.1 = (bf16[21,32,128]{2,1,0:T(8,128)(2,1)S(1)}, bf16[21,32,128]{2,1,0:T(8,128)(2,1)S(1)}, u32[]{:S(2)}, u32[]{:S(2)}) collective-permute-start(bf16[21,32,128]{2,1,0:T(8,128)(2,1)S(1)} %pad_maximum_fusion.5), channel_id=1, source_target_pairs={{0,8},{4,12},{8,16},{12,20},{16,24},{20,28},{1,9},{5,13},{9,17},{1... | collective-permute-start | bytes 516104 | tf_op jit(solution)/shard_map/ppermute | solution.py:19
  76.8 10.2 %collective-permute-start.8 = (bf16[21,32,128]{2,1,0:T(8,128)(2,1)S(1)}, bf16[21,32,128]{2,1,0:T(8,128)(2,1)S(1)}, u32[]{:S(2)}, u32[]{:S(2)}) collective-permute-start(bf16[21,32,128]{2,1,0:T(8,128)(2,1)S(1)} %pad_maximum_fusion.8), channel_id=1, source_target_pairs={{16,0},{20,4},{24,8},{28,12},{17,1},{21,5},{25,9},{29,13},{18,2},{... | collective-permute-start | bytes 516104 | tf_op jit(solution)/shard_map/ppermute | solution.py:19
  78.4 10.4 %collective-permute-start.2 = (bf16[21,32,128]{2,1,0:T(8,128)(2,1)S(1)}, bf16[21,32,128]{2,1,0:T(8,128)(2,1)S(1)}, u32[]{:S(2)}, u32[]{:S(2)}) collective-permute-start(bf16[21,32,128]{2,1,0:T(8,128)(2,1)S(1)} %pad_maximum_fusion.6), channel_id=1, source_target_pairs={{0,16},{4,20},{8,24},{12,28},{1,17},{5,21},{9,25},{13,29},{2,18},{... | collective-permute-start | bytes 516104 | tf_op jit(solution)/shard_map/ppermute | solution.py:19
  87.1 5.4 %collective-permute-start.9 = (bf16[20,32,128]{2,1,0:T(8,128)(2,1)S(1)}, bf16[20,32,128]{2,1,0:T(8,128)(2,1)S(1)}, u32[]{:S(2)}, u32[]{:S(2)}) collective-permute-start(bf16[20,32,128]{2,1,0:T(8,128)(2,1)S(1)} %get-tuple-element.42), channel_id=1, source_target_pairs={{0,4},{4,0},{8,12},{12,8},{16,20},{20,16},{24,28},{28,24},{1,5},{5... | collective-permute-start | bytes 491528 | tf_op jit(solution)/shard_map/ppermute | solution.py:14
  89.0 5.4 %collective-permute-start.3 = (bf16[20,32,128]{2,1,0:T(8,128)(2,1)S(1)}, bf16[20,32,128]{2,1,0:T(8,128)(2,1)S(1)}, u32[]{:S(2)}, u32[]{:S(2)}) collective-permute-start(bf16[20,32,128]{2,1,0:T(8,128)(2,1)S(1)} %get-tuple-element.53), channel_id=1, source_target_pairs={{0,4},{4,0},{8,12},{12,8},{16,20},{20,16},{24,28},{28,24},{1,5},{5... | collective-permute-start | bytes 491528 | tf_op jit(solution)/shard_map/ppermute | solution.py:14
  108.8 5.2 %copy-start.8 = (bf16[20,64,512]{2,1,0:T(8,128)(2,1)S(1)}, bf16[20,64,512]{2,1,0:T(8,128)(2,1)}, u32[]{:S(2)}) copy-start(bf16[20,64,512]{2,1,0:T(8,128)(2,1)} %get-tuple-element.40) | copy-start | bytes 3932164
  108.8 5.2 %copy-start.14 = (f32[512,128]{0,1:T(8,128)S(1)}, f32[512,128]{0,1:T(8,128)}, u32[]{:S(2)}) copy-start(f32[512,128]{0,1:T(8,128)} %fusion.69) | copy-start | bytes 786436
  110.3 2.2 %collective-permute-start.11 = (f32[2,20]{1,0:T(2,128)S(1)}, f32[2,20]{1,0:T(2,128)S(1)}, u32[]{:S(2)}, u32[]{:S(2)}) collective-permute-start(f32[2,20]{1,0:T(2,128)S(1)} %pad_maximum_fusion.9), channel_id=1, source_target_pairs={{0,2},{2,0},{1,3},{3,1},{4,6},{6,4},{5,7},{7,5},{8,10},{10,8},{9,1... | collective-permute-start | bytes 488 | tf_op jit(solution)/shard_map/ppermute | solution.py:14
  110.4 14.9 %copy-start.10 = (bf16[1280,512]{1,0:T(8,128)(2,1)S(1)}, bf16[1280,512]{1,0:T(8,128)(2,1)}, u32[]{:S(2)}) copy-start(bf16[1280,512]{1,0:T(8,128)(2,1)} %get-tuple-element.67) | copy-start | bytes 3932164
  110.4 14.9 %copy-start.13 = (bf16[2,2,160,1024]{3,2,1,0:T(8,128)(2,1)S(1)}, bf16[2,2,160,1024]{3,2,1,0:T(8,128)(2,1)}, u32[]{:S(2)}) copy-start(bf16[2,2,160,1024]{3,2,1,0:T(8,128)(2,1)} %get-tuple-element.72) | copy-start | bytes 3932164
  110.4 14.8 %collective-permute-start.16 = (bf16[1280,512]{1,0:T(8,128)(2,1)}, bf16[1280,512]{1,0:T(8,128)(2,1)S(1)}, u32[]{:S(2)}, u32[]{:S(2)}) collective-permute-start(bf16[1280,512]{1,0:T(8,128)(2,1)} %get-tuple-element.67), channel_id=1, source_target_pairs={{0,2},{2,0},{1,3},{3,1},{4,6},{6,4},{5,7},{7,5},{8,10},{10,8},{9,1... | collective-permute-start | bytes 3932168 | tf_op jit(solution)/shard_map/ppermute | solution.py:14
  112.5 3.6 %collective-permute-start.12 = (f32[2,20]{1,0:T(2,128)S(1)}, f32[2,20]{1,0:T(2,128)S(1)}, u32[]{:S(2)}, u32[]{:S(2)}) collective-permute-start(f32[2,20]{1,0:T(2,128)S(1)} %fusion.153), channel_id=1, source_target_pairs={{0,4},{4,0},{8,12},{12,8},{16,20},{20,16},{24,28},{28,24},{1,5},{5... | collective-permute-start | bytes 488 | tf_op jit(solution)/shard_map/ppermute | solution.py:14
  116.1 3.6 %collective-permute-start.13 = (f32[2,20]{1,0:T(2,128)S(1)}, f32[2,20]{1,0:T(2,128)S(1)}, u32[]{:S(2)}, u32[]{:S(2)}) collective-permute-start(f32[2,20]{1,0:T(2,128)S(1)} %fusion.182), channel_id=1, source_target_pairs={{0,8},{4,12},{8,0},{12,4},{16,24},{20,28},{24,16},{28,20},{1,9},{5... | collective-permute-start | bytes 488 | tf_op jit(solution)/shard_map/ppermute | solution.py:14
  119.8 4.9 %collective-permute-start.14 = (f32[2,20]{1,0:T(2,128)S(1)}, f32[2,20]{1,0:T(2,128)S(1)}, u32[]{:S(2)}, u32[]{:S(2)}) collective-permute-start(f32[2,20]{1,0:T(2,128)S(1)} %add.339), channel_id=1, source_target_pairs={{0,16},{4,20},{8,24},{12,28},{16,0},{20,4},{24,8},{28,12},{1,17},{... | collective-permute-start | bytes 488 | tf_op jit(solution)/shard_map/ppermute | solution.py:14
  122.5 6.9 %collective-permute-start.10 = (bf16[512,256]{0,1:T(8,128)(2,1)S(1)}, bf16[512,256]{0,1:T(8,128)(2,1)S(1)}, u32[]{:S(2)}, u32[]{:S(2)}) collective-permute-start(bf16[512,256]{0,1:T(8,128)(2,1)S(1)} %fusion.45), channel_id=1, source_target_pairs={{0,1},{1,0},{2,3},{3,2},{4,5},{5,4},{6,7},{7,6},{8,9},{9,8},{10,11... | collective-permute-start | bytes 786440 | tf_op jit(solution)/shard_map/ppermute | solution.py:14
  127.4 17.9 %collective-permute-start.20 = (bf16[2,2,160,640]{3,2,0,1:T(8,128)(2,1)}, bf16[2,2,160,640]{3,2,0,1:T(8,128)(2,1)}, u32[]{:S(2)}, u32[]{:S(2)}) collective-permute-start(bf16[2,2,160,640]{3,2,0,1:T(8,128)(2,1)} %convolution_convert_fusion), channel_id=1, source_target_pairs={{0,8},{4,12},{8,0},{12,4},{16,24},{20,28},{24,16},{28,20},{1,9},{5... | collective-permute-start | bytes 2457608 | tf_op jit(solution)/shard_map/ppermute | solution.py:14
  131.7 18.6 %collective-permute-start.17 = (bf16[2,2,160,640]{3,2,1,0:T(8,128)(2,1)}, bf16[2,2,160,640]{3,2,1,0:T(8,128)(2,1)}, u32[]{:S(2)}, u32[]{:S(2)}) collective-permute-start(bf16[2,2,160,640]{3,2,1,0:T(8,128)(2,1)} %convolution_convert_fusion.1), channel_id=1, source_target_pairs={{0,4},{4,0},{8,12},{12,8},{16,20},{20,16},{24,28},{28,24},{1,5},{5... | collective-permute-start | bytes 2457608 | tf_op jit(solution)/shard_map/ppermute | solution.py:14
  148.7 9.0 %collective-permute-start.21 = (bf16[2,160,640]{2,1,0:T(8,128)(2,1)S(1)}, bf16[2,160,640]{2,1,0:T(8,128)(2,1)S(1)}, u32[]{:S(2)}, u32[]{:S(2)}) collective-permute-start(bf16[2,160,640]{2,1,0:T(8,128)(2,1)S(1)} %fusion.42), channel_id=1, source_target_pairs={{0,4},{4,0},{8,12},{12,8},{16,20},{20,16},{24,28},{28,24},{1,5},{5... | collective-permute-start | bytes 1228808 | tf_op jit(solution)/shard_map/ppermute | solution.py:14
  152.7 10.9 %collective-permute-start.18 = (bf16[2,160,640]{2,1,0:T(8,128)(2,1)S(1)}, bf16[2,160,640]{2,1,0:T(8,128)(2,1)S(1)}, u32[]{:S(2)}, u32[]{:S(2)}) collective-permute-start(bf16[2,160,640]{2,1,0:T(8,128)(2,1)S(1)} %fusion.41), channel_id=1, source_target_pairs={{0,8},{4,12},{8,0},{12,4},{16,24},{20,28},{24,16},{28,20},{1,9},{5... | collective-permute-start | bytes 1228808 | tf_op jit(solution)/shard_map/ppermute | solution.py:14
  157.9 15.1 %collective-permute-start.22 = (bf16[160,640]{1,0:T(8,128)(2,1)S(1)}, bf16[160,640]{1,0:T(8,128)(2,1)S(1)}, u32[]{:S(2)}, u32[]{:S(2)}) collective-permute-start(bf16[160,640]{1,0:T(8,128)(2,1)S(1)} %fusion.58), channel_id=1, source_target_pairs={{0,16},{4,20},{8,24},{12,28},{16,0},{20,4},{24,8},{28,12},{1,17},{... | collective-permute-start | bytes 614408 | tf_op jit(solution)/shard_map/ppermute | solution.py:14
  163.8 11.4 %collective-permute-start.19 = (bf16[160,640]{1,0:T(8,128)(2,1)S(1)}, bf16[160,640]{1,0:T(8,128)(2,1)S(1)}, u32[]{:S(2)}, u32[]{:S(2)}) collective-permute-start(bf16[160,640]{1,0:T(8,128)(2,1)S(1)} %fusion.57), channel_id=1, source_target_pairs={{0,16},{4,20},{8,24},{12,28},{16,0},{20,4},{24,8},{28,12},{1,17},{... | collective-permute-start | bytes 614408 | tf_op jit(solution)/shard_map/ppermute | solution.py:14
  (14 other events, 48.9 us)

commit v2 on v1

v2 whole, which is shorter than its diff:
```python
import functools

import jax
import jax.numpy as jnp
from jax import lax
from jax.experimental import pallas as pl
from jax.experimental.pallas import tpu as pltpu
from jax.sharding import PartitionSpec as P

HEAD_DIM = 64
F32 = jnp.float32
BF16 = jnp.bfloat16
NN = (((1,), (0,)), ((), ()))
NT = (((1,), (1,)), ((), ()))
TN = (((0,), (0,)), ((), ()))
VMEM_BYTES = 32 * 1024 * 1024
COST_SCALE = 20


def dot(a, b, dims=NN):
    return lax.dot_general(a, b, dims, preferred_element_type=F32)


def split(values):
    high = values.astype(BF16)
    return high, (values - high.astype(F32)).astype(BF16)


def dot_split(a, b, dims=NN):
    return dot(a[0], b[0], dims) + dot(a[1], b[0], dims) + dot(a[0], b[1], dims)


def part(pair, index):
    return pair[0][index], pair[1][index]


def running_sum(values, reverse=False):
    length = values.shape[1]
    lane = lax.broadcasted_iota(jnp.int32, values.shape, 1)
    step = 1
    while step < length:
        if reverse:
            moved = jnp.where(lane < length - step, pltpu.roll(values, length - step, 1), 0.0)
        else:
            moved = jnp.where(lane >= step, pltpu.roll(values, step, 1), 0.0)
        values = values + moved
        step *= 2
    return values


def softplus(values):
    return jnp.maximum(values, 0.0) + jnp.log(1.0 + jnp.exp(-jnp.abs(values)))


def causal_affinity(b, c):
    affinity = dot(b, c, NT)
    source = lax.broadcasted_iota(jnp.int32, affinity.shape, 0)
    later = lax.broadcasted_iota(jnp.int32, affinity.shape, 1)
    return jnp.where(source <= later, affinity, 0.0)


def as_column(row):
    square = jnp.broadcast_to(row, (row.shape[1], row.shape[1]))
    along = lax.broadcasted_iota(jnp.int32, square.shape, 0)
    across = lax.broadcasted_iota(jnp.int32, square.shape, 1)
    return jnp.sum(jnp.where(along == across, square, 0.0), axis=1, keepdims=True)


def per_head(values, heads):
    return values.reshape(heads, HEAD_DIM, values.shape[1])


def call(kernel, grid, in_specs, out_specs, out_shape, scratch=(), flops=0, prefetch=0):
    return pl.pallas_call(
        kernel,
        out_shape=out_shape,
        grid_spec=pltpu.PrefetchScalarGridSpec(
            num_scalar_prefetch=prefetch,
            grid=grid,
            in_specs=in_specs,
            out_specs=out_specs,
            scratch_shapes=list(scratch),
        ),
        compiler_params=pltpu.CompilerParams(
            vmem_limit_bytes=VMEM_BYTES, dimension_semantics=("arbitrary",) * len(grid)
        ),
        cost_estimate=pl.CostEstimate(flops=flops * COST_SCALE, bytes_accessed=4_000_000 * COST_SCALE, transcendentals=0),
    )


def whole(*shape):
    return pl.BlockSpec(shape, lambda i, *_: (0,) * len(shape))


def by_row(*shape):
    return pl.BlockSpec(shape, lambda i, *_: (i,) + (0,) * (len(shape) - 1))


ANY = pl.BlockSpec(memory_space=pl.ANY)


def decay_kernel(x_ref, b_ref, dt_ref, alog_ref, skip_ref, grown_ref, shrunk_ref, skips_ref, total_ref, gathered_ref):
    heads, length = dt_ref.shape
    group = x_ref.shape[0] // HEAD_DIM

    @pl.when(pl.program_id(0) == 0)
    def _():
        step_size = softplus(dt_ref[...])
        cumulative = running_sum(step_size * -jnp.exp(as_column(alog_ref[...])))
        grown = jnp.exp(cumulative)
        shrunk = step_size * jnp.exp(-cumulative)
        skips = jnp.broadcast_to(as_column(skip_ref[...]), (heads, length))
        for h in range(heads):
            grown_ref[h] = grown[h : h + 1]
            shrunk_ref[h] = shrunk[h : h + 1]
            skips_ref[h] = skips[h : h + 1]
        total_ref[...] = jnp.broadcast_to(cumulative[:, length - 1 :], total_ref.shape)

    shrunk = shrunk_ref[pl.ds(pl.program_id(0) * group, group)]
    xs = (per_head(x_ref[...].astype(F32), group) * shrunk).reshape(x_ref.shape)
    high, low = split(xs)
    gathered_ref[...] = dot(high, b_ref[...]) + dot(low, b_ref[...])


def inner_kernel(x_ref, b_ref, c_ref, shrunk_ref, after_ref, inner_ref, high_ref, low_ref):
    group = x_ref.shape[0] // HEAD_DIM
    half = x_ref.shape[1] // 2

    @pl.when(pl.program_id(0) == 0)
    def _():
        high_ref[...], low_ref[...] = split(causal_affinity(b_ref[...], c_ref[...]))

    xs = split((per_head(x_ref[...].astype(F32), group) * shrunk_ref[...]).reshape(x_ref.shape))
    affinity = (high_ref, low_ref)
    early = (slice(None), slice(0, half))
    late = (slice(None), slice(half, None))
    corner = (slice(0, half), slice(0, half))
    inner_ref[:, :half] = dot_split(part(xs, early), part(affinity, corner))
    inner_ref[:, half:] = dot_split(xs, part(affinity, late))


def mixed_kernel(inner_ref, state_ref, c_ref, x_ref, grown_ref, skips_ref, after_ref, mixed_ref):
    group = x_ref.shape[0] // HEAD_DIM
    inner = per_head(inner_ref[...] + dot(state_ref[...], c_ref[...], NT), group)
    x = per_head(x_ref[...].astype(F32), group)
    mixed = grown_ref[...] * inner + skips_ref[...] * x
    mixed_ref[...] = mixed.reshape(x_ref.shape).astype(BF16)


def cotan_first_kernel(flag_ref, mine_ref, other_ref, g_ref, after_ref, out_ref):
    @pl.when(flag_ref[0] == 1)
    def _():
        out_ref[...] = dot(mine_ref[...], g_ref[...])

    @pl.when(flag_ref[0] == 0)
    def _():
        out_ref[...] = dot(other_ref[...], g_ref[...])


def cotan_kernel(flag_ref, mine_ref, other_ref, g_ref, first_ref, c_ref, grown_ref, after_ref, cotan_ref, local_ref, sum_ref):
    @pl.when(flag_ref[0] == 0)
    def _():
        sum_ref[...] = first_ref[...] + dot(mine_ref[...], g_ref[...])

    @pl.when(flag_ref[0] == 1)
    def _():
        sum_ref[...] = first_ref[...] + dot(other_ref[...], g_ref[...])

    cotan = sum_ref[...].astype(BF16)
    cotan_ref[...] = cotan
    group = cotan.shape[0] // HEAD_DIM
    gs = (per_head(cotan.astype(F32), group) * grown_ref[...]).reshape(cotan.shape)
    high, low = split(gs)
    local_ref[...] = dot(high, c_ref[...]) + dot(low, c_ref[...])


def terms_kernel(pick_ref, g0_ref, g1_ref, m0_ref, m1_ref, after_ref, out_ref):
    high, _, low, columns, length = g0_ref.shape
    if columns % 16 == 0:
        flat = lambda ref: ref[...].reshape(high * low * columns, length)
        product = dot(flat(g0_ref), m0_ref[...], NT) + dot(flat(g1_ref), m1_ref[...], NT)
        out_ref[...] = product.reshape(out_ref.shape).astype(out_ref.dtype)
    else:
        for i in range(high):
            for j in range(low):
                product = dot(g0_ref[i, 0, j], m0_ref[...], NT) + dot(g1_ref[i, 0, j], m1_ref[...], NT)
                out_ref[i * low + j] = product.astype(out_ref.dtype)


def back_kernel(x_ref, cotan_ref, inner_ref, state_ref, b_ref, c_ref, grown_ref, shrunk_ref, after_ref,
                outer_ref, from_y_ref, grad_b_ref, grad_c_ref, high_ref, low_ref, across_ref):
    step = pl.program_id(0)
    group = x_ref.shape[0] // HEAD_DIM
    half = x_ref.shape[1] // 2

    @pl.when(step == 0)
    def _():
        high_ref[...], low_ref[...] = split(causal_affinity(b_ref[...], c_ref[...]))
        across_ref[...] = jnp.zeros_like(across_ref)
        grad_c_ref[...] = jnp.zeros_like(grad_c_ref)

    x = per_head(x_ref[...].astype(F32), group)
    xs = split((x * shrunk_ref[...]).reshape(x_ref.shape))
    gs_full = (per_head(cotan_ref[...].astype(F32), group) * grown_ref[...]).reshape(x_ref.shape)
    gs = split(gs_full)
    affinity = (high_ref, low_ref)
    late = (slice(None), slice(half, None))
    early = (slice(None), slice(0, half))
    top = (slice(0, half), slice(None))
    corner = (slice(half, None), slice(half, None))
    outer_ref[:, :half] = dot_split(gs, part(affinity, top), NT)
    outer_ref[:, half:] = dot_split(part(gs, late), part(affinity, corner), NT)
    across_ref[:half] += dot_split(part(xs, early), gs, TN)
    across_ref[half:, half:] += dot_split(part(xs, late), part(gs, late), TN)
    state = state_ref[...]
    grad_c_ref[...] += dot(gs[0], state, TN) + dot(gs[1], state, TN)
    inner = inner_ref[...] + dot(state, c_ref[...], NT)
    from_y_ref[...] = jnp.sum(per_head(gs_full * inner, group), axis=1, keepdims=True)

    @pl.when(step == pl.num_programs(0) - 1)
    def _():
        across = across_ref[...]
        source = lax.broadcasted_iota(jnp.int32, across.shape, 0)
        later = lax.broadcasted_iota(jnp.int32, across.shape, 1)
        high, low = split(jnp.where(source <= later, across, 0.0))
        grad_b_ref[...] = dot(high, c_ref[...]) + dot(low, c_ref[...])
        grad_c_ref[...] += dot(high, b_ref[...], TN) + dot(low, b_ref[...], TN)


def last_kernel(x_ref, cotan_ref, outer_ref, ends_ref, gathered_ref, state_ref, shrunk_ref, skips_ref,
                b_ref, dt_ref, alog_ref, from_y_ref, grad_b_ref, grad_c_ref, after_a_ref, after_b_ref,
                grad_inputs_ref, grad_dt_ref, small_ref, both_ref,
                from_x_s, from_end_s, from_skip_s, rows_x, rows_y, rows_skip, rows_end):
    step = pl.program_id(0)
    group = x_ref.shape[0] // HEAD_DIM
    heads, length = dt_ref.shape
    n_state = b_ref.shape[1]
    ends = ends_ref[...]
    outer = per_head(outer_ref[...] + dot(ends, b_ref[...], NT), group)
    x = per_head(x_ref[...].astype(F32), group)
    cotan = per_head(cotan_ref[...].astype(F32), group)
    xs = x * shrunk_ref[...]
    grad_inputs = shrunk_ref[...] * outer + skips_ref[...] * cotan
    grad_inputs_ref[...] = grad_inputs.reshape(x_ref.shape).astype(BF16)
    here = pl.ds(step * group, group)
    from_x_s[here] = jnp.sum(xs * outer, axis=1, keepdims=True)
    from_skip_s[here] = jnp.sum(x * cotan, axis=1, keepdims=True)
    moved = ends.astype(F32) * (gathered_ref[...] + state_ref[...].astype(F32))
    from_end_s[here] = jnp.sum(per_head(moved, group), axis=1, keepdims=True)
    high, low = split(xs.reshape(x_ref.shape))

    @pl.when(step == 0)
    def _():
        both_ref[:, :n_state] = grad_b_ref[...]
        both_ref[:, n_state:] = grad_c_ref[...]

    both_ref[:, :n_state] += dot(high, ends, TN) + dot(low, ends, TN)

    @pl.when(step == pl.num_programs(0) - 1)
    def _():
        for h in range(heads):
            rows_x[h : h + 1] = from_x_s[h]
            rows_y[h : h + 1] = from_y_ref[h]
            rows_skip[h : h + 1] = from_skip_s[h]
            rows_end[h : h + 1] = from_end_s[h]
        from_x = rows_x[...]
        from_end = jnp.sum(rows_end[...], axis=1, keepdims=True)
        flow = running_sum(rows_y[...] - from_x, reverse=True) + from_end
        dt = dt_ref[...]
        step_size = softplus(dt)
        rate = -jnp.exp(as_column(alog_ref[...]))
        grad_dt_ref[...] = (from_x / step_size + flow * rate) / (1.0 + jnp.exp(-dt))
        alog = jnp.sum(flow * step_size * rate, axis=1, keepdims=True)
        skip = jnp.sum(rows_skip[...], axis=1, keepdims=True)
        small_ref[0] = jnp.broadcast_to(alog, small_ref.shape[1:])
        small_ref[1] = jnp.broadcast_to(skip, small_ref.shape[1:])


def swap(value, axis, size, bit):
    return lax.ppermute(value, axis, [(i, i ^ bit) for i in range(size)])


def shifted(value, axis, size, step):
    pairs = [(i, i + step) for i in range(size) if 0 <= i + step < size]
    return lax.ppermute(value, axis, pairs)


def butterfly(value, axis, size):
    bit = 1
    while bit < size:
        value = value + swap(value, axis, size, bit)
        bit *= 2
    return value


def pack(state, total):
    heads, rows, lanes = state.shape
    high = lax.reduce_precision(total, 8, 7)
    middle = lax.reduce_precision(total - high, 8, 7)
    low = total - high - middle
    terms = jnp.stack([high, middle, low]).astype(BF16)
    extra = jnp.pad(terms, ((0, rows - 3), (0, lanes - heads)))
    return jnp.concatenate([state.astype(BF16), extra[None]], axis=0)


def unpack(payload):
    heads = payload.shape[0] - 1
    terms = payload[heads, :3, :heads].astype(F32)
    return payload[:heads].astype(F32), terms[0] + terms[1] + terms[2]


def decay(total):
    return jnp.exp(total)[:, None, None]


def pair_scan(local, total, n_seq, reverse, beside):
    works = []

    def traveling(payload, got):
        if len(works) in beside:
            work = beside[len(works)](payload)
            got, work = lax.optimization_barrier((got, work))
            works.append(work)
        return got

    heads, width, lanes = local.shape
    place = lax.axis_index("seq")
    upper = lax.rem(place, 2) == 1
    late = jnp.logical_not(upper) if reverse else upper
    halves = local.reshape(heads, 2, width // 2, lanes)
    mine = jnp.where(upper, halves[:, 1], halves[:, 0])
    theirs = jnp.where(upper, halves[:, 0], halves[:, 1])
    payload = pack(theirs, total)
    other, other_total = unpack(traveling(payload, swap(payload, "seq", n_seq, 1)))
    first = jnp.where(late, other, mine)
    second = jnp.where(late, mine, other)
    first_total = jnp.where(late, other_total, total)
    second_total = jnp.where(late, total, other_total)
    span = decay(second_total) * first + second
    span_total = first_total + second_total
    before, before_total = jnp.zeros_like(span), jnp.zeros_like(span_total)
    step = 2
    while step < n_seq:
        payload = pack(span, span_total)
        moved = shifted(payload, "seq", n_seq, -step if reverse else step)
        earlier, earlier_total = unpack(traveling(payload, moved))
        before = decay(before_total) * earlier + before
        span = decay(span_total) * earlier + span
        before_total = before_total + earlier_total
        span_total = span_total + earlier_total
        step *= 2
    for_first = before
    for_second = decay(first_total) * before + first
    if reverse:
        for_first = decay(first_total) * for_first
        for_second = decay(second_total) * for_second
    keep = jnp.where(late, for_second, for_first).astype(BF16)
    give = jnp.where(late, for_first, for_second).astype(BF16)
    got = swap(give, "seq", n_seq, 1)
    low = jnp.where(upper, got, keep)
    high = jnp.where(upper, keep, got)
    result = jnp.concatenate([low[:, None], high[:, None]], axis=1).reshape(heads * width, lanes)
    return works, result, give


def per_device(mesh, head_inputs, b_proj, c_proj, dt_raw, a_log, d_skip, w_out, out_grad):
    n_seq, n_dp, n_tensor = mesh.shape["seq"], mesh.shape["dp"], mesh.shape["tensor"]
    x, b, c, dt, g = head_inputs[0], b_proj[0], c_proj[0], dt_raw[0], out_grad[0]
    heads, length = dt.shape
    channels = heads * HEAD_DIM
    n_state = b.shape[1]
    features = g.shape[0] * n_tensor
    out_columns = features // (n_seq * n_dp)
    my_dp, my_tensor, my_seq = (lax.axis_index(a) for a in ("dp", "tensor", "seq"))
    group = 4 if heads % 4 == 0 else 1
    block = group * HEAD_DIM
    grid = (heads // group,)
    alog2, skip2 = a_log[None], d_skip[None]

    if n_tensor == 2:
        g_first, half_index = g, my_tensor
        g_second = swap(g, "tensor", 2, 1)
    else:
        g_all = lax.all_gather(g, "tensor", axis=0, tiled=True)
        g_first, g_second, half_index = g_all[: features // 2], g_all[features // 2 :], 0

    long = jax.ShapeDtypeStruct((heads, 1, length), F32)
    grown, shrunk, skips, totals, gathered = call(
        decay_kernel,
        grid,
        [by_row(block, length), whole(length, n_state), whole(heads, length), whole(1, heads), whole(1, heads)],
        [whole(heads, 1, length)] * 3 + [whole(heads, 128), by_row(block, n_state)],
        [long] * 3
        + [jax.ShapeDtypeStruct((heads, 128), F32), jax.ShapeDtypeStruct((channels, n_state), F32)],
        flops=4 * channels * length * n_state,
    )(x, b, dt, alog2, skip2)
    total = totals[:, 0]
    local_state = decay(total) * gathered.reshape(heads, HEAD_DIM, n_state)

    inners = lambda after: call(
        inner_kernel,
        grid,
        [by_row(block, length), whole(length, n_state), whole(length, n_state), by_row(group, 1, length), ANY],
        by_row(block, length),
        jax.ShapeDtypeStruct((channels, length), F32),
        [pltpu.VMEM((length, length), BF16)] * 2,
        flops=5 * channels * length * length,
    )(x, b, c, shrunk, after)

    w_other = swap(w_out, "dp", 2, 1)
    flag = (my_dp == half_index).astype(jnp.int32).reshape(1)
    half_features = features // 2
    wide_group = heads // 2 if heads % 2 == 0 else 1
    wide_block = wide_group * HEAD_DIM
    wide_grid = (heads // wide_group,)

    def weights(wanted):
        return pl.BlockSpec(
            (wide_block, half_features), lambda i, flag: (jnp.where(flag[0] == wanted, i, 0), 0)
        )

    first = lambda after: call(
        cotan_first_kernel,
        wide_grid,
        [weights(1), weights(0), whole(half_features, length), ANY],
        by_row(wide_block, length),
        jax.ShapeDtypeStruct((channels, length), F32),
        flops=2 * channels * half_features * length,
        prefetch=1,
    )(flag, w_out, w_other, g_first, after)
    cotans = lambda g_second, first, after: call(
        cotan_kernel,
        wide_grid,
        [weights(0), weights(1)]
        + [whole(half_features, length), by_row(wide_block, length), whole(length, n_state), by_row(wide_group, 1, length), ANY],
        [by_row(wide_block, length), by_row(wide_block, n_state)],
        [jax.ShapeDtypeStruct((channels, length), BF16), jax.ShapeDtypeStruct((channels, n_state), F32)],
        [pltpu.VMEM((wide_block, length), F32)],
        flops=2 * channels * length * (half_features + 2 * n_state),
        prefetch=1,
    )(flag, w_out, w_other, g_second, first, c, grown, after)

    beside = {0: inners, 1: first}
    (inner, first_sum), state_in, give = pair_scan(local_state, total, n_seq, False, beside)
    if n_tensor == 2:
        g_second, give = lax.optimization_barrier((g_second, give))
    y_cotan, local_cotan = cotans(g_second, first_sum, give)

    def mix(after):
        return call(
            mixed_kernel,
            grid,
            [by_row(block, length), by_row(block, n_state), whole(length, n_state), by_row(block, length)]
            + [by_row(group, 1, length)] * 2
            + [ANY],
            by_row(block, length),
            jax.ShapeDtypeStruct((channels, length), BF16),
            flops=2 * channels * length * n_state,
        )(inner, state_in, c, x, grown, skips, after)

    firsts = g_first.reshape(n_seq // 2, n_dp, out_columns, length)
    seconds = g_second.reshape(n_seq // 2, n_dp, out_columns, length)

    def chosen(place):
        pick = lambda blocks: lax.dynamic_index_in_dim(blocks, place, 1, keepdims=False)
        return jnp.concatenate([pick(firsts), pick(seconds)])

    g_mine = chosen(my_dp)
    g_other = swap(chosen(1 - my_dp), "dp", 2, 1)
    n_bits = n_seq.bit_length() - 1
    half = channels // 2

    def my_bit(bit):
        value = jnp.bitwise_and(my_seq >> bit, 1)
        return value ^ half_index if bit == n_bits - 1 else value

    def terms(mixed, mixed_other, stream, bit, value, dtype, after):
        low = 1 << bit
        high = n_seq // (2 * low)
        rows = pl.BlockSpec((half, length), lambda i, pick: (stream, 0))
        columns = pl.BlockSpec(
            (high, 1, low, out_columns, length), lambda i, pick: (0, pick[0], 0, 0, 0)
        )
        split_blocks = lambda blocks: blocks.reshape(high, 2, low, out_columns, length)
        return call(
            terms_kernel,
            (1,),
            [columns, columns, rows, rows, ANY],
            whole(n_seq // 2, out_columns, half),
            jax.ShapeDtypeStruct((n_seq // 2, out_columns, half), dtype),
            flops=n_seq * out_columns * half * 2 * length,
            prefetch=1,
        )(
            value.astype(jnp.int32).reshape(1),
            split_blocks(g_mine), split_blocks(g_other), mixed, mixed_other, after,
        )

    orders = [list(range(n_bits)), [1, 0] + list(range(2, n_bits))]
    held = {}

    def traded(after):
        mixed = mix(after)
        held["mixed"] = mixed, swap(mixed, "dp", 2, 1)
        return mixed

    def sending(after):
        held["sends"] = [
            terms(*held["mixed"], s, orders[s][0], 1 - my_bit(orders[s][0]), BF16, after) for s in (0, 1)
        ]
        return held["sends"]

    def keeping(after):
        sends = held["sends"]
        held["gots"] = [swap(sends[s], "seq", n_seq, 1 << orders[s][0]) for s in (0, 1)]
        held["keeps"] = [
            terms(*held["mixed"], s, orders[s][0], my_bit(orders[s][0]), F32, after) for s in (0, 1)
        ]
        held["back"] = back(after)
        return held["keeps"], held["back"]

    long = jax.ShapeDtypeStruct((heads, 1, length), F32)
    wide = jax.ShapeDtypeStruct((length, n_state), F32)
    back = lambda after: call(
        back_kernel,
        grid,
        [by_row(block, length)] * 3
        + [by_row(block, n_state), whole(length, n_state), whole(length, n_state)]
        + [by_row(group, 1, length)] * 2
        + [ANY],
        [by_row(block, length), by_row(group, 1, length), whole(length, n_state), whole(length, n_state)],
        [jax.ShapeDtypeStruct((channels, length), F32), long, wide, wide],
        [pltpu.VMEM((length, length), BF16)] * 2 + [pltpu.VMEM((length, length), F32)],
        flops=10 * channels * length * length,
    )(x, y_cotan, inner, state_in, b, c, grown, shrunk, after)
    _, cotan_end, _ = pair_scan(
        local_cotan.reshape(heads, HEAD_DIM, n_state), total, n_seq, True,
        {0: traded, 1: sending, 2: keeping},
    )
    mixed = held["mixed"][0]
    outer, from_y, grad_b, grad_c = held["back"]

    def halve(sums, left):
        axis = sorted(left, reverse=True).index(left[0])
        pick = lambda value: lax.dynamic_index_in_dim(sums, value, axis, keepdims=False)
        return pick(my_bit(left[0])), pick(1 - my_bit(left[0])).astype(BF16)

    streams = []
    for s in (0, 1):
        sums = held["keeps"][s] + held["gots"][s].astype(F32)
        sums = sums.reshape((2,) * (n_bits - 1) + (out_columns, half))
        streams.append(halve(sums, orders[s][1:]))
    grad_inputs, grad_dt, small, both = call(
        last_kernel,
        grid,
        [by_row(block, length)] * 3
        + [by_row(block, n_state)] * 3
        + [by_row(group, 1, length)] * 2
        + [whole(length, n_state), whole(heads, length), whole(1, heads), whole(heads, 1, length)]
        + [whole(length, n_state)] * 2
        + [ANY] * 2,
        [
            by_row(block, length),
            whole(heads, length),
            whole(2, heads, 128),
            whole(length, 2 * n_state),
        ],
        [
            jax.ShapeDtypeStruct((channels, length), BF16),
            jax.ShapeDtypeStruct((heads, length), F32),
            jax.ShapeDtypeStruct((2, heads, 128), F32),
            jax.ShapeDtypeStruct((length, 2 * n_state), F32),
        ],
        [
            pltpu.VMEM((heads, 1, length), F32),
            pltpu.VMEM((heads, 1, n_state), F32),
            pltpu.VMEM((heads, 1, length), F32),
            pltpu.VMEM((heads, length), F32),
            pltpu.VMEM((heads, length), F32),
            pltpu.VMEM((heads, length), F32),
            pltpu.VMEM((heads, n_state), F32),
        ],
        flops=6 * channels * length * n_state,
    )(
        x, y_cotan, outer, cotan_end, gathered, state_in, shrunk, skips,
        b, dt, alog2, from_y, grad_b, grad_c, streams[0][1], streams[1][1],
    )
    if n_tensor == 2:
        both_other = swap(both, "tensor", 2, 1)
    small = butterfly(small, "dp", n_dp)
    for done in range(1, n_bits):
        pairs = []
        for s in (0, 1):
            keep, send = streams[s]
            pairs.append(keep + swap(send, "seq", n_seq, 1 << orders[s][done]).astype(F32))
        if done + 1 < n_bits:
            streams = [halve(pairs[s], orders[s][done + 1 :]) for s in (0, 1)]
            if done + 2 == n_bits:
                small, streams = lax.optimization_barrier((small, streams))
    small = butterfly(small, "seq", n_seq)
    if n_tensor == 2:
        both_other, small = lax.optimization_barrier((both_other, small))
        both = both + both_other
    else:
        both = lax.psum(both, "tensor")
    both = both.astype(BF16)
    grad_w = jnp.concatenate(pairs, axis=1).T.astype(BF16)
    return (
        mixed[None],
        grad_inputs[None],
        both[None, :, :n_state],
        both[None, :, n_state:],
        grad_dt[None],
        small[0, :, 0],
        small[1, :, 0],
        grad_w,
    )


def solution(mesh):
    in_specs = (
        P("dp", "tensor", "seq"),
        P("dp", "seq", None),
        P("dp", "seq", None),
        P("dp", "tensor", "seq"),
        P("tensor"),
        P("tensor"),
        P("tensor", "dp"),
        P("dp", "tensor", "seq"),
    )
    out_specs = (
        P("dp", "tensor", "seq"),
        P("dp", "tensor", "seq"),
        P("dp", "seq", None),
        P("dp", "seq", None),
        P("dp", "tensor", "seq"),
        P("tensor"),
        P("tensor"),
        P("tensor", ("seq", "dp")),
    )
    return jax.shard_map(
        functools.partial(per_device, mesh),
        mesh=mesh,
        in_specs=in_specs,
        out_specs=out_specs,
        check_vma=False,
    )
```

time: 177 us -> 140 us (0.79)
  matrix products: 42.5 us -> 0 us
  Pallas kernels: 0 us -> 33.4 us
  waiting for transfers between devices: 66.6 us -> 49.4 us
  starting transfers between devices: 40.1 us -> 32 us
  other arithmetic: 16.1 us -> 10 us
  local copies, waits for them, and re-layouts: 9.53 us -> 13.4 us
    dot_general x19 -> x0, matrix products: 42.5 us -> none  [the longest x4 9.99 us: halving(): lax.dot_general(part, mixed_rows, (((part.ndim - 1,), (1,)), ((), ())), p...]
    pallas_call x0 -> x11, Pallas kernels: none -> 33.4 us  [the longest x1 6.52 us: per_device(): call(back_kernel, grid, [by_row(block, length)] * 3 + [by_row(block, n_st...]
    ppermute x19, waiting for transfers between devices: 62.6 us -> 43.8 us  [swap(): return lax.ppermute(value, axis, [(i, i ^ bit) for i in range(size)])]
    ppermute x19, starting transfers between devices: 27.1 us -> 20.3 us  [swap(): return lax.ppermute(value, axis, [(i, i ^ bit) for i in range(size)])]
    reduce_sum x5 -> x0, other arithmetic: 5.48 us -> none  [the longest x2 4.22 us: head_sum(): return jnp.sum(values.reshape(heads, HEAD_DIM, values.shape[1]), axis=1)]
    unnamed x49 -> x78, local copies, waits for them, and re-layouts: 6.28 us -> 11.5 us
    add x2 -> x4, other arithmetic: 0.2 us -> 4.05 us  [the longest x2 2.45 us: per_device(): keep + swap(send, 'seq', n_seq, 1 << orders[s][done]).astype(F32)]
    select_n x6 -> x0, other arithmetic: 3.21 us -> none  [the longest x1 1.72 us: halving(): keep, send = (jnp.where(mine, one, zero), jnp.where(mine, zero, one))]
  transfers between devices with their start and end apart: 23 -> 23, of which waited for: 15 -> 12; matrix products, arithmetic and copies ran while one was open for 19% -> 8% of each run, Pallas kernels for 0% -> 22%
where the time goes in v2:
time: 140 us
  waiting for transfers between devices  49.4 us (35%)
  Pallas kernels  33.4 us (24%)
  starting transfers between devices  32 us (23%)
  local copies, waits for them, and re-layouts  13.4 us (10%)
  other arithmetic  10 us (7%)
  between operations  1.46 us (1%)
    ppermute x19, waiting for transfers between devices, swap(): return lax.ppermute(value, axis, [(i, i ^ bit) for i in range(size)])  43.8 us
    ppermute x19, starting transfers between devices, swap(): return lax.ppermute(value, axis, [(i, i ^ bit) for i in range(size)])  20.3 us
    ppermute x4, starting transfers between devices, shifted(): return lax.ppermute(value, axis, pairs)  11.7 us
    unnamed x78, local copies, waits for them, and re-layouts  11.5 us
    pallas_call x1, Pallas kernels, per_device(): call(back_kernel, grid, [by_row(block, length)] * 3 + [by_row(block, n_st...  6.52 us
    pallas_call x4, Pallas kernels, terms(): call(terms_kernel, (1,), [columns, columns, rows, rows, ANY], whole(n_seq...  5.74 us
    ppermute x4, waiting for transfers between devices, shifted(): return lax.ppermute(value, axis, pairs)  5.6 us
    pallas_call x1, Pallas kernels, per_device(): call(last_kernel, grid, [by_row(block, length)] * 3 + [by_row(block, n_st...  5.25 us
  transfers between devices with their start and end apart: 23, of which 12 were waited for; matrix products, arithmetic and copies ran while one was open for 8% of the time, Pallas kernels for 22%

profile of v2, /device:TPU:0, one launch (start us, length us, event | category | flops | bytes accessed | tf_op | source)
XLA Modules:
  0.0 139.8 jit_solution(13781493221653596628)
XLA Ops:
  1.4 1.3 copy-done.8
  5.0 2.3 %shard_map.143 = (f32[20,1,512]{2,1,0:T(1,128)S(1)}, f32[20,1,512]{2,1,0:T(1,128)S(1)}, f32[20,1,512]{2,1,0:T(1,128)S(1)}, f32[20,128]{1,0:T(8,128)S(1)}, f32[1280,128]{1,0:T(8,128)S(1)}) custom-call(bf16[1280,512]{1,0:T(8,128)(2,1)S(1)} %bitcast.212, bf16[512,128]{1,0:T(8,128)(2,1)S(1)} %bitcast.226, f32[20,512]{1,0:T(8,128)S(1)} %bitcast.209, ...), custom_call_target="tpu_custom_call" | custom-call | flops 6710886400 | bytes 80000000 | tf_op jit(solution)/shard_map/pallas_call | solution.py:388
  7.7 3.0 %collective-permute-start = (bf16[21,32,128]{2,1,0:T(8,128)(2,1)S(1)}, bf16[21,32,128]{2,1,0:T(8,128)(2,1)S(1)}, u32[]{:S(2)}, u32[]{:S(2)}) collective-permute-start(bf16[21,32,128]{2,1,0:T(8,128)(2,1)S(1)} %pad_maximum_fusion.5.after_ref), channel_id=1, source_target_pairs={{0,4},{4,0},{8,12},{12,8},{16,20},{20,16},{24,28},{28,24},{1,5},{5... | collective-permute-start | bytes 516104 | tf_op jit(solution)/shard_map/ppermute | solution.py:280
  10.7 1.6 %collective-permute-start.5 = (bf16[1280,512]{1,0:T(8,128)(2,1)S(1)}, bf16[1280,512]{1,0:T(8,128)(2,1)S(1)}, u32[]{:S(2)}, u32[]{:S(2)}) collective-permute-start(bf16[1280,512]{1,0:T(8,128)(2,1)S(1)} %bitcast.196), channel_id=1, source_target_pairs={{0,1},{1,0},{2,3},{3,2},{4,5},{5,4},{6,7},{7,6},{8,9},{9,8},{10,11... | collective-permute-start | bytes 3932168 | tf_op jit(solution)/shard_map/ppermute | solution.py:280
  13.6 2.8 %shard_map.144.inner_ref = f32[1280,512]{1,0:T(8,128)S(1)} custom-call(bf16[1280,512]{1,0:T(8,128)(2,1)S(1)} %bitcast.213, bf16[512,128]{1,0:T(8,128)(2,1)S(1)} %bitcast.227, bf16[512,128]{1,0:T(8,128)(2,1)S(1)} %bitcast.222, f32[20,1,512]{2,1,0:T(1,128)S(1)} %get-tuple-element.41.shrunk_ref, bf16[21,32,128]{2,1,0:T(8,128)(2,1)S(1)} %pad_maximum_fusion.5.after_ref), custom_call_target="tpu_custom_call" | custom-call | flops 33554432000 | bytes 80000000 | tf_op jit(solution)/shard_map/pallas_call | solution.py:400
  16.4 1.5 %copy-done.20 = f32[1280,512]{1,0:T(8,128)} copy-done((f32[1280,512]{1,0:T(8,128)}, f32[1280,512]{1,0:T(8,128)S(1)}, u32[]{:S(2)}) %copy-start.20) | copy-done | bytes 2621464
  19.1 3.5 %collective-permute-start.1 = (bf16[21,32,128]{2,1,0:T(8,128)(2,1)S(1)}, bf16[21,32,128]{2,1,0:T(8,128)(2,1)S(1)}, u32[]{:S(2)}, u32[]{:S(2)}) collective-permute-start(bf16[21,32,128]{2,1,0:T(8,128)(2,1)S(1)} %pad_maximum_fusion.6.after_ref), channel_id=1, source_target_pairs={{0,8},{4,12},{8,16},{12,20},{16,24},{20,28},{1,9},{5,13},{9,17},{1... | collective-permute-start | bytes 516104 | tf_op jit(solution)/shard_map/ppermute | solution.py:285
  22.6 3.5 %shard_map.145.first_ref = f32[1280,512]{1,0:T(8,128)S(1)} custom-call(s32[1]{0:T(128)} %bitcast.12.flag_ref, bf16[1280,1280]{1,0:T(8,128)(2,1)S(1)} %copy-done.7, bf16[1280,1280]{1,0:T(8,128)(2,1)} %collective-permute-done.2.other_ref, bf16[1280,512]{1,0:T(8,128)(2,1)S(1)} %bitcast.198, bf16[21,32,128]{2,1,0:T(8,128)(2,1)S(1)} %pad_maximum_fusion.6.after_ref), custom_call_target="tpu_custom_call" | custom-call | flops 33554432000 | bytes 80000000 | tf_op jit(solution)/shard_map/pallas_call | solution.py:422
  26.8 5.4 %collective-permute-start.3 = (bf16[21,32,128]{2,1,0:T(8,128)(2,1)S(1)}, bf16[21,32,128]{2,1,0:T(8,128)(2,1)S(1)}, u32[]{:S(2)}, u32[]{:S(2)}) collective-permute-start(bf16[21,32,128]{2,1,0:T(8,128)(2,1)S(1)} %pad_maximum_fusion.7), channel_id=1, source_target_pairs={{0,16},{4,20},{8,24},{12,28},{1,17},{5,21},{9,25},{13,29},{2,18},{... | collective-permute-start | bytes 516104 | tf_op jit(solution)/shard_map/ppermute | solution.py:285
  32.2 3.2 %collective-permute-done.3 = bf16[21,32,128]{2,1,0:T(8,128)(2,1)S(1)} collective-permute-done((bf16[21,32,128]{2,1,0:T(8,128)(2,1)S(1)}, bf16[21,32,128]{2,1,0:T(8,128)(2,1)S(1)}, u32[]{:S(2)}, u32[]{:S(2)}) %collective-permute-start.3) | collective-permute-done | bytes 172064 | tf_op jit(solution)/shard_map/ppermute | solution.py:285
  36.0 6.0 %collective-permute-done.5.g_ref = bf16[1280,512]{1,0:T(8,128)(2,1)S(1)} collective-permute-done((bf16[1280,512]{1,0:T(8,128)(2,1)S(1)}, bf16[1280,512]{1,0:T(8,128)(2,1)S(1)}, u32[]{:S(2)}, u32[]{:S(2)}) %collective-permute-start.5) | collective-permute-done | bytes 1310752 | tf_op jit(solution)/shard_map/ppermute | solution.py:280
  41.9 4.5 %shard_map.146 = (bf16[1280,512]{1,0:T(8,128)(2,1)S(1)}, f32[1280,128]{1,0:T(8,128)S(1)}) custom-call(s32[1]{0:T(128)} %bitcast.12.flag_ref, bf16[1280,1280]{1,0:T(8,128)(2,1)S(1)} %copy-done.7, bf16[1280,1280]{1,0:T(8,128)(2,1)} %collective-permute-done.2.other_ref, bf16[1280,512]{1,0:T(8,128)(2,1)S(1)} %collective-permute-done.5.g_ref, ...), custom_call_target="tpu_custom_call" | custom-call | flops 40265318400 | bytes 80000000 | tf_op jit(solution)/shard_map/pallas_call | solution.py:431
  48.0 1.4 copy-done.21
  49.7 2.8 %shard_map.147.m0_ref = bf16[1280,512]{1,0:T(8,128)(2,1)} custom-call(f32[1280,512]{1,0:T(8,128)S(1)} %copy-done.21, bf16[1280,128]{1,0:T(8,128)(2,1)S(1)} %bitcast.205, bf16[512,128]{1,0:T(8,128)(2,1)S(1)} %bitcast.224, bf16[1280,512]{1,0:T(8,128)(2,1)S(1)} %bitcast.214, f32[20,1,512]{2,1,0:T(1,128)S(1)} %get-tuple-element.45.grown_ref, ...), custom_call_target="tpu_custom_call" | custom-call | flops 3355443200 | bytes 80000000 | tf_op jit(solution)/shard_map/pallas_call | solution.py:450
  55.9 2.1 %shard_map.148 = bf16[4,160,640]{2,1,0:T(8,128)(2,1)} custom-call(s32[1]{0:T(128)} %bitcast.27.pick_ref, bf16[4,2,1,160,512]{4,3,2,1,0:T(8,128)(2,1)S(1)} %bitcast.200, bf16[4,2,1,160,512]{4,3,2,1,0:T(8,128)(2,1)S(1)} %bitcast.218, bf16[1280,512]{1,0:T(8,128)(2,1)S(1)} %copy-done.12, bf16[1280,512]{1,0:T(8,128)(2,1)S(1)} %collective-permute-done.9.m1_ref, ...), custom_call_target="tpu_custom_call" | custom-call | flops 16777216000 | bytes 80000000 | tf_op jit(solution)/shard_map/pallas_call | solution.py:485
  58.0 1.5 %collective-permute-start.12 = (bf16[4,160,640]{2,1,0:T(8,128)(2,1)}, bf16[4,160,640]{2,1,0:T(8,128)(2,1)}, u32[]{:S(2)}, u32[]{:S(2)}) collective-permute-start(bf16[4,160,640]{2,1,0:T(8,128)(2,1)} %shard_map.148), channel_id=1, source_target_pairs={{0,4},{4,0},{8,12},{12,8},{16,20},{20,16},{24,28},{28,24},{1,5},{5... | collective-permute-start | bytes 2457608 | tf_op jit(solution)/shard_map/ppermute | solution.py:280
  61.9 1.5 %collective-permute-start.10 = (bf16[21,32,128]{2,1,0:T(8,128)(2,1)S(1)}, bf16[21,32,128]{2,1,0:T(8,128)(2,1)S(1)}, u32[]{:S(2)}, u32[]{:S(2)}) collective-permute-start(bf16[21,32,128]{2,1,0:T(8,128)(2,1)S(1)} %pad_maximum_fusion.9.after_ref), channel_id=1, source_target_pairs={{16,0},{20,4},{24,8},{28,12},{17,1},{21,5},{25,9},{29,13},{18,2},{... | collective-permute-start | bytes 516104 | tf_op jit(solution)/shard_map/ppermute | solution.py:285
  63.4 6.5 %shard_map.150 = (f32[1280,512]{1,0:T(8,128)S(1)}, f32[20,1,512]{2,1,0:T(1,128)S(1)}, f32[512,128]{1,0:T(8,128)S(1)}, f32[512,128]{1,0:T(8,128)S(1)}) custom-call(bf16[1280,512]{1,0:T(8,128)(2,1)S(1)} %bitcast.215, bf16[1280,512]{1,0:T(8,128)(2,1)S(1)} %get-tuple-element.51.cotan_ref, f32[1280,512]{1,0:T(8,128)S(1)} %copy-done.21, ...), custom_call_target="tpu_custom_call" | custom-call | flops 67108864000 | bytes 80000000 | tf_op jit(solution)/shard_map/pallas_call | solution.py:523
  74.8 1.4 %collective-permute-start.11 = (bf16[20,32,128]{2,1,0:T(8,128)(2,1)}, bf16[20,32,128]{2,1,0:T(8,128)(2,1)}, u32[]{:S(2)}, u32[]{:S(2)}) collective-permute-start(bf16[20,32,128]{2,1,0:T(8,128)(2,1)} %select_convert_fusion.1), channel_id=1, source_target_pairs={{0,4},{4,0},{8,12},{12,8},{16,20},{20,16},{24,28},{28,24},{1,5},{5... | collective-permute-start | bytes 491528 | tf_op jit(solution)/shard_map/ppermute | solution.py:280
  76.8 5.6 %collective-permute-done.11 = bf16[20,32,128]{2,1,0:T(8,128)(2,1)} collective-permute-done((bf16[20,32,128]{2,1,0:T(8,128)(2,1)}, bf16[20,32,128]{2,1,0:T(8,128)(2,1)}, u32[]{:S(2)}, u32[]{:S(2)}) %collective-permute-start.11) | collective-permute-done | bytes 163872 | tf_op jit(solution)/shard_map/ppermute | solution.py:280
  82.4 1.4 select_bitcast_fusion.1
  84.8 1.4 convert_add_fusion.1
  86.4 1.6 %collective-permute-start.16 = (bf16[2,160,640]{2,1,0:T(8,128)(2,1)S(1)}, bf16[2,160,640]{2,1,0:T(8,128)(2,1)S(1)}, u32[]{:S(2)}, u32[]{:S(2)}) collective-permute-start(bf16[2,160,640]{2,1,0:T(8,128)(2,1)S(1)} %fusion.after_a_ref), channel_id=1, source_target_pairs={{0,8},{4,12},{8,0},{12,4},{16,24},{20,28},{24,16},{28,20},{1,9},{5... | collective-permute-start | bytes 1228808 | tf_op jit(solution)/shard_map/ppermute | solution.py:280
  88.0 9.6 %collective-permute-done.13 = bf16[4,160,640]{2,1,0:T(8,128)(2,1)S(1)} collective-permute-done((bf16[4,160,640]{2,1,0:T(8,128)(2,1)}, bf16[4,160,640]{2,1,0:T(8,128)(2,1)S(1)}, u32[]{:S(2)}, u32[]{:S(2)}) %collective-permute-start.13) | collective-permute-done | bytes 819232 | tf_op jit(solution)/shard_map/ppermute | solution.py:280
  99.1 5.3 %shard_map.153 = (bf16[1280,512]{1,0:T(8,128)(2,1)}, f32[20,512]{1,0:T(8,128)S(1)}, f32[2,20,128]{2,1,0:T(8,128)S(1)}, f32[512,256]{1,0:T(8,128)S(1)}) custom-call(bf16[1280,512]{1,0:T(8,128)(2,1)S(1)} %bitcast.216, bf16[1280,512]{1,0:T(8,128)(2,1)S(1)} %copy-done.25, f32[1280,512]{1,0:T(8,128)S(1)} %copy-done.23, bf16[1280,128]{1,0:T(8,128)(2,1)S(1)} %bitcast.208, ...), custom_call_target="tpu_custom_call" | custom-call | flops 10066329600 | bytes 80000000 | tf_op jit(solution)/shard_map/pallas_call | solution.py:552
  104.4 1.5 %collective-permute-start.14 = (f32[512,256]{1,0:T(8,128)S(1)}, f32[512,256]{1,0:T(8,128)S(1)}, u32[]{:S(2)}, u32[]{:S(2)}) collective-permute-start(f32[512,256]{1,0:T(8,128)S(1)} %get-tuple-element.60), channel_id=1, source_target_pairs={{0,1},{1,0},{2,3},{3,2},{4,5},{5,4},{6,7},{7,6},{8,9},{9,8},{10,11... | collective-permute-start | bytes 1572872 | tf_op jit(solution)/shard_map/ppermute | solution.py:280
  109.6 2.8 %collective-permute-done.18 = f32[2,20,128]{2,1,0:T(8,128)S(1)} collective-permute-done((f32[2,20,128]{2,1,0:T(8,128)S(1)}, f32[2,20,128]{2,1,0:T(8,128)S(1)}, u32[]{:S(2)}, u32[]{:S(2)}) %collective-permute-start.18) | collective-permute-done | bytes 20512 | tf_op jit(solution)/shard_map/ppermute | solution.py:280
  113.0 3.3 %collective-permute-done.19 = f32[2,20,128]{2,1,0:T(8,128)S(1)} collective-permute-done((f32[2,20,128]{2,1,0:T(8,128)S(1)}, f32[2,20,128]{2,1,0:T(8,128)S(1)}, u32[]{:S(2)}, u32[]{:S(2)}) %collective-permute-start.19) | collective-permute-done | bytes 20512 | tf_op jit(solution)/shard_map/ppermute | solution.py:280
  116.3 2.4 %collective-permute-start.20 = (f32[2,20,128]{2,1,0:T(8,128)S(1)}, f32[2,20,128]{2,1,0:T(8,128)S(1)}, u32[]{:S(2)}, u32[]{:S(2)}) collective-permute-start(f32[2,20,128]{2,1,0:T(8,128)S(1)} %add.334), channel_id=1, source_target_pairs={{0,16},{4,20},{8,24},{12,28},{16,0},{20,4},{24,8},{28,12},{1,17},{... | collective-permute-start | bytes 61448 | tf_op jit(solution)/shard_map/ppermute | solution.py:280
  119.9 2.4 %collective-permute-start.21 = (bf16[160,640]{1,0:T(8,128)(2,1)S(1)}, bf16[160,640]{1,0:T(8,128)(2,1)S(1)}, u32[]{:S(2)}, u32[]{:S(2)}) collective-permute-start(bf16[160,640]{1,0:T(8,128)(2,1)S(1)} %fusion.10), channel_id=1, source_target_pairs={{0,16},{4,20},{8,24},{12,28},{16,0},{20,4},{24,8},{28,12},{1,17},{... | collective-permute-start | bytes 614408 | tf_op jit(solution)/shard_map/ppermute | solution.py:280
  123.8 11.7 %collective-permute-done.22 = bf16[160,640]{1,0:T(8,128)(2,1)S(1)} collective-permute-done((bf16[160,640]{1,0:T(8,128)(2,1)S(1)}, bf16[160,640]{1,0:T(8,128)(2,1)S(1)}, u32[]{:S(2)}, u32[]{:S(2)}) %collective-permute-start.22) | collective-permute-done | bytes 204832 | tf_op jit(solution)/shard_map/ppermute | solution.py:280
  135.5 3.4 %collective-permute-done.21 = bf16[160,640]{1,0:T(8,128)(2,1)S(1)} collective-permute-done((bf16[160,640]{1,0:T(8,128)(2,1)S(1)}, bf16[160,640]{1,0:T(8,128)(2,1)S(1)}, u32[]{:S(2)}, u32[]{:S(2)}) %collective-permute-start.21) | collective-permute-done | bytes 204832 | tf_op jit(solution)/shard_map/ppermute | solution.py:280
  (175 shorter events, 30.0 us)
Async XLA Ops:
  7.7 10.3 %collective-permute-start = (bf16[21,32,128]{2,1,0:T(8,128)(2,1)S(1)}, bf16[21,32,128]{2,1,0:T(8,128)(2,1)S(1)}, u32[]{:S(2)}, u32[]{:S(2)}) collective-permute-start(bf16[21,32,128]{2,1,0:T(8,128)(2,1)S(1)} %pad_maximum_fusion.5.after_ref), channel_id=1, source_target_pairs={{0,4},{4,0},{8,12},{12,8},{16,20},{20,16},{24,28},{28,24},{1,5},{5... | collective-permute-start | bytes 516104 | tf_op jit(solution)/shard_map/ppermute | solution.py:280
  10.7 12.0 %collective-permute-start.2 = (bf16[1280,1280]{1,0:T(8,128)(2,1)}, bf16[1280,1280]{1,0:T(8,128)(2,1)}, u32[]{:S(2)}, u32[]{:S(2)}) collective-permute-start(bf16[1280,1280]{1,0:T(8,128)(2,1)} %mine_ref.3), channel_id=1, source_target_pairs={{0,2},{2,0},{1,3},{3,1},{4,6},{6,4},{5,7},{7,5},{8,10},{10,8},{9,1... | collective-permute-start | bytes 9830408 | tf_op jit(solution)/shard_map/ppermute | solution.py:280
  10.7 31.2 %collective-permute-start.5 = (bf16[1280,512]{1,0:T(8,128)(2,1)S(1)}, bf16[1280,512]{1,0:T(8,128)(2,1)S(1)}, u32[]{:S(2)}, u32[]{:S(2)}) collective-permute-start(bf16[1280,512]{1,0:T(8,128)(2,1)S(1)} %bitcast.196), channel_id=1, source_target_pairs={{0,1},{1,0},{2,3},{3,2},{4,5},{5,4},{6,7},{7,6},{8,9},{9,8},{10,11... | collective-permute-start | bytes 3932168 | tf_op jit(solution)/shard_map/ppermute | solution.py:280
  19.1 7.4 %collective-permute-start.1 = (bf16[21,32,128]{2,1,0:T(8,128)(2,1)S(1)}, bf16[21,32,128]{2,1,0:T(8,128)(2,1)S(1)}, u32[]{:S(2)}, u32[]{:S(2)}) collective-permute-start(bf16[21,32,128]{2,1,0:T(8,128)(2,1)S(1)} %pad_maximum_fusion.6.after_ref), channel_id=1, source_target_pairs={{0,8},{4,12},{8,16},{12,20},{16,24},{20,28},{1,9},{5,13},{9,17},{1... | collective-permute-start | bytes 516104 | tf_op jit(solution)/shard_map/ppermute | solution.py:285
  26.8 8.6 %collective-permute-start.3 = (bf16[21,32,128]{2,1,0:T(8,128)(2,1)S(1)}, bf16[21,32,128]{2,1,0:T(8,128)(2,1)S(1)}, u32[]{:S(2)}, u32[]{:S(2)}) collective-permute-start(bf16[21,32,128]{2,1,0:T(8,128)(2,1)S(1)} %pad_maximum_fusion.7), channel_id=1, source_target_pairs={{0,16},{4,20},{8,24},{12,28},{1,17},{5,21},{9,25},{13,29},{2,18},{... | collective-permute-start | bytes 516104 | tf_op jit(solution)/shard_map/ppermute | solution.py:285
  35.6 12.1 %collective-permute-start.4 = (bf16[20,32,128]{2,1,0:T(8,128)(2,1)S(1)}, bf16[20,32,128]{2,1,0:T(8,128)(2,1)S(1)}, u32[]{:S(2)}, u32[]{:S(2)}) collective-permute-start(bf16[20,32,128]{2,1,0:T(8,128)(2,1)S(1)} %select_convert_fusion.4.after_ref), channel_id=1, source_target_pairs={{0,4},{4,0},{8,12},{12,8},{16,20},{20,16},{24,28},{28,24},{1,5},{5... | collective-permute-start | bytes 491528 | tf_op jit(solution)/shard_map/ppermute | solution.py:280
  46.5 16.9 %copy-start.24 = (bf16[1280,512]{1,0:T(8,128)(2,1)}, bf16[1280,512]{1,0:T(8,128)(2,1)S(1)}, u32[]{:S(2)}) copy-start(bf16[1280,512]{1,0:T(8,128)(2,1)S(1)} %get-tuple-element.51.cotan_ref) | copy-start | bytes 3932164
  46.5 6.5 %collective-permute-start.6 = (bf16[21,32,128]{2,1,0:T(8,128)(2,1)S(1)}, bf16[21,32,128]{2,1,0:T(8,128)(2,1)S(1)}, u32[]{:S(2)}, u32[]{:S(2)}) collective-permute-start(bf16[21,32,128]{2,1,0:T(8,128)(2,1)S(1)} %pad_maximum_fusion.4.after_ref), channel_id=1, source_target_pairs={{0,4},{4,0},{8,12},{12,8},{16,20},{20,16},{24,28},{28,24},{1,5},{5... | collective-permute-start | bytes 516104 | tf_op jit(solution)/shard_map/ppermute | solution.py:280
  47.4 7.2 %collective-permute-start.8 = (bf16[8,160,512]{2,1,0:T(8,128)(2,1)S(1)}, bf16[8,160,512]{2,1,0:T(8,128)(2,1)S(1)}, u32[]{:S(2)}, u32[]{:S(2)}) collective-permute-start(bf16[8,160,512]{2,1,0:T(8,128)(2,1)S(1)} %pad_maximum_fusion.1), channel_id=1, source_target_pairs={{0,2},{2,0},{1,3},{3,1},{4,6},{6,4},{5,7},{7,5},{8,10},{10,8},{9,1... | collective-permute-start | bytes 3932168 | tf_op jit(solution)/shard_map/ppermute | solution.py:280
  48.0 15.4 %copy-start.3 = (bf16[20,2,32,128]{3,2,1,0:T(8,128)(2,1)}, bf16[20,2,32,128]{3,2,1,0:T(8,128)(2,1)S(1)}, u32[]{:S(2)}) copy-start(bf16[20,2,32,128]{3,2,1,0:T(8,128)(2,1)S(1)} %copy.20) | copy-start | bytes 983044
  52.6 3.4 %collective-permute-start.9 = (bf16[1280,512]{1,0:T(8,128)(2,1)}, bf16[1280,512]{1,0:T(8,128)(2,1)S(1)}, u32[]{:S(2)}, u32[]{:S(2)}) collective-permute-start(bf16[1280,512]{1,0:T(8,128)(2,1)} %shard_map.147.m0_ref), channel_id=1, source_target_pairs={{0,2},{2,0},{1,3},{3,1},{4,6},{6,4},{5,7},{7,5},{8,10},{10,8},{9,1... | collective-permute-start | bytes 3932168 | tf_op jit(solution)/shard_map/ppermute | solution.py:280
  53.1 20.9 %copy-start.35 = (bf16[21,32,128]{2,1,0:T(8,128)(2,1)}, bf16[21,32,128]{2,1,0:T(8,128)(2,1)S(1)}, u32[]{:S(2)}) copy-start(bf16[21,32,128]{2,1,0:T(8,128)(2,1)S(1)} %collective-permute-done.6) | copy-start | bytes 516100
  53.3 20.7 %copy-start.30 = (f32[20,1,32,128]{3,2,0,1:T(8,128)}, f32[20,1,32,128]{3,2,0,1:T(8,128)S(1)}, u32[]{:S(2)}) copy-start(f32[20,1,32,128]{3,2,0,1:T(8,128)S(1)} %get-tuple-element.95) | copy-start | bytes 983044
  53.3 8.3 %collective-permute-start.7 = (bf16[21,32,128]{2,1,0:T(8,128)(2,1)S(1)}, bf16[21,32,128]{2,1,0:T(8,128)(2,1)S(1)}, u32[]{:S(2)}, u32[]{:S(2)}) collective-permute-start(bf16[21,32,128]{2,1,0:T(8,128)(2,1)S(1)} %pad_maximum_fusion.8.after_ref), channel_id=1, source_target_pairs={{8,0},{12,4},{16,8},{20,12},{24,16},{28,20},{9,1},{13,5},{17,9},{2... | collective-permute-start | bytes 516104 | tf_op jit(solution)/shard_map/ppermute | solution.py:285
  58.0 26.8 %collective-permute-start.12 = (bf16[4,160,640]{2,1,0:T(8,128)(2,1)}, bf16[4,160,640]{2,1,0:T(8,128)(2,1)}, u32[]{:S(2)}, u32[]{:S(2)}) collective-permute-start(bf16[4,160,640]{2,1,0:T(8,128)(2,1)} %shard_map.148), channel_id=1, source_target_pairs={{0,4},{4,0},{8,12},{12,8},{16,20},{20,16},{24,28},{28,24},{1,5},{5... | collective-permute-start | bytes 2457608 | tf_op jit(solution)/shard_map/ppermute | solution.py:280
  61.9 12.1 %collective-permute-start.10 = (bf16[21,32,128]{2,1,0:T(8,128)(2,1)S(1)}, bf16[21,32,128]{2,1,0:T(8,128)(2,1)S(1)}, u32[]{:S(2)}, u32[]{:S(2)}) collective-permute-start(bf16[21,32,128]{2,1,0:T(8,128)(2,1)S(1)} %pad_maximum_fusion.9.after_ref), channel_id=1, source_target_pairs={{16,0},{20,4},{24,8},{28,12},{17,1},{21,5},{25,9},{29,13},{18,2},{... | collective-permute-start | bytes 516104 | tf_op jit(solution)/shard_map/ppermute | solution.py:285
  74.8 7.6 %collective-permute-start.11 = (bf16[20,32,128]{2,1,0:T(8,128)(2,1)}, bf16[20,32,128]{2,1,0:T(8,128)(2,1)}, u32[]{:S(2)}, u32[]{:S(2)}) collective-permute-start(bf16[20,32,128]{2,1,0:T(8,128)(2,1)} %select_convert_fusion.1), channel_id=1, source_target_pairs={{0,4},{4,0},{8,12},{12,8},{16,20},{20,16},{24,28},{28,24},{1,5},{5... | collective-permute-start | bytes 491528 | tf_op jit(solution)/shard_map/ppermute | solution.py:280
  76.3 21.4 %collective-permute-start.13 = (bf16[4,160,640]{2,1,0:T(8,128)(2,1)}, bf16[4,160,640]{2,1,0:T(8,128)(2,1)S(1)}, u32[]{:S(2)}, u32[]{:S(2)}) collective-permute-start(bf16[4,160,640]{2,1,0:T(8,128)(2,1)} %copy-done.13), channel_id=1, source_target_pairs={{0,8},{4,12},{8,0},{12,4},{16,24},{20,28},{24,16},{28,20},{1,9},{5... | collective-permute-start | bytes 2457608 | tf_op jit(solution)/shard_map/ppermute | solution.py:280
  84.8 14.3 %copy-start.25 = (bf16[1280,512]{1,0:T(8,128)(2,1)S(1)}, bf16[1280,512]{1,0:T(8,128)(2,1)}, u32[]{:S(2)}) copy-start(bf16[1280,512]{1,0:T(8,128)(2,1)} %copy-done.24) | copy-start | bytes 3932164
  86.2 12.8 %copy-start.23 = (f32[1280,512]{1,0:T(8,128)S(1)}, f32[1280,512]{1,0:T(8,128)}, u32[]{:S(2)}) copy-start(f32[1280,512]{1,0:T(8,128)} %copy-done.22) | copy-start | bytes 7864324
  86.3 12.8 %copy-start.2 = (f32[1280,128]{1,0:T(8,128)S(1)}, f32[1280,128]{1,0:T(8,128)}, u32[]{:S(2)}) copy-start(f32[1280,128]{1,0:T(8,128)} %copy-done.1) | copy-start | bytes 1966084
  86.3 12.8 %copy-start.4 = (bf16[20,2,32,128]{3,2,1,0:T(8,128)(2,1)S(1)}, bf16[20,2,32,128]{3,2,1,0:T(8,128)(2,1)}, u32[]{:S(2)}) copy-start(bf16[20,2,32,128]{3,2,1,0:T(8,128)(2,1)} %copy-done.3) | copy-start | bytes 983044
  86.3 12.8 %copy-start.6 = (f32[1,20,512]{2,1,0:T(8,128)S(1)}, f32[1,20,512]{2,1,0:T(8,128)}, u32[]{:S(2)}) copy-start(f32[1,20,512]{2,1,0:T(8,128)} %copy-done.5) | copy-start | bytes 122884
  86.4 19.5 %collective-permute-start.16 = (bf16[2,160,640]{2,1,0:T(8,128)(2,1)S(1)}, bf16[2,160,640]{2,1,0:T(8,128)(2,1)S(1)}, u32[]{:S(2)}, u32[]{:S(2)}) collective-permute-start(bf16[2,160,640]{2,1,0:T(8,128)(2,1)S(1)} %fusion.after_a_ref), channel_id=1, source_target_pairs={{0,8},{4,12},{8,0},{12,4},{16,24},{20,28},{24,16},{28,20},{1,9},{5... | collective-permute-start | bytes 1228808 | tf_op jit(solution)/shard_map/ppermute | solution.py:280
  98.0 9.2 %collective-permute-start.17 = (bf16[2,160,640]{2,1,0:T(8,128)(2,1)S(1)}, bf16[2,160,640]{2,1,0:T(8,128)(2,1)S(1)}, u32[]{:S(2)}, u32[]{:S(2)}) collective-permute-start(bf16[2,160,640]{2,1,0:T(8,128)(2,1)S(1)} %fusion.1.after_b_ref), channel_id=1, source_target_pairs={{0,4},{4,0},{8,12},{12,8},{16,20},{20,16},{24,28},{28,24},{1,5},{5... | collective-permute-start | bytes 1228808 | tf_op jit(solution)/shard_map/ppermute | solution.py:280
  104.4 1.5 %collective-permute-start.15 = (f32[2,20,128]{2,1,0:T(8,128)S(1)}, f32[2,20,128]{2,1,0:T(8,128)S(1)}, u32[]{:S(2)}, u32[]{:S(2)}) collective-permute-start(f32[2,20,128]{2,1,0:T(8,128)S(1)} %get-tuple-element.61), channel_id=1, source_target_pairs={{0,2},{2,0},{1,3},{3,1},{4,6},{6,4},{5,7},{7,5},{8,10},{10,8},{9,1... | collective-permute-start | bytes 61448 | tf_op jit(solution)/shard_map/ppermute | solution.py:280
  104.4 17.9 %collective-permute-start.14 = (f32[512,256]{1,0:T(8,128)S(1)}, f32[512,256]{1,0:T(8,128)S(1)}, u32[]{:S(2)}, u32[]{:S(2)}) collective-permute-start(f32[512,256]{1,0:T(8,128)S(1)} %get-tuple-element.60), channel_id=1, source_target_pairs={{0,1},{1,0},{2,3},{3,2},{4,5},{5,4},{6,7},{7,6},{8,9},{9,8},{10,11... | collective-permute-start | bytes 1572872 | tf_op jit(solution)/shard_map/ppermute | solution.py:280
  108.6 3.9 %collective-permute-start.18 = (f32[2,20,128]{2,1,0:T(8,128)S(1)}, f32[2,20,128]{2,1,0:T(8,128)S(1)}, u32[]{:S(2)}, u32[]{:S(2)}) collective-permute-start(f32[2,20,128]{2,1,0:T(8,128)S(1)} %add.326), channel_id=1, source_target_pairs={{0,4},{4,0},{8,12},{12,8},{16,20},{20,16},{24,28},{28,24},{1,5},{5... | collective-permute-start | bytes 61448 | tf_op jit(solution)/shard_map/ppermute | solution.py:280
  112.5 3.8 %collective-permute-start.19 = (f32[2,20,128]{2,1,0:T(8,128)S(1)}, f32[2,20,128]{2,1,0:T(8,128)S(1)}, u32[]{:S(2)}, u32[]{:S(2)}) collective-permute-start(f32[2,20,128]{2,1,0:T(8,128)S(1)} %add.333), channel_id=1, source_target_pairs={{0,8},{4,12},{8,0},{12,4},{16,24},{20,28},{24,16},{28,20},{1,9},{5... | collective-permute-start | bytes 61448 | tf_op jit(solution)/shard_map/ppermute | solution.py:280
  116.3 6.0 %collective-permute-start.20 = (f32[2,20,128]{2,1,0:T(8,128)S(1)}, f32[2,20,128]{2,1,0:T(8,128)S(1)}, u32[]{:S(2)}, u32[]{:S(2)}) collective-permute-start(f32[2,20,128]{2,1,0:T(8,128)S(1)} %add.334), channel_id=1, source_target_pairs={{0,16},{4,20},{8,24},{12,28},{16,0},{20,4},{24,8},{28,12},{1,17},{... | collective-permute-start | bytes 61448 | tf_op jit(solution)/shard_map/ppermute | solution.py:280
  119.4 16.1 %collective-permute-start.22 = (bf16[160,640]{1,0:T(8,128)(2,1)S(1)}, bf16[160,640]{1,0:T(8,128)(2,1)S(1)}, u32[]{:S(2)}, u32[]{:S(2)}) collective-permute-start(bf16[160,640]{1,0:T(8,128)(2,1)S(1)} %fusion.11), channel_id=1, source_target_pairs={{0,16},{4,20},{8,24},{12,28},{16,0},{20,4},{24,8},{28,12},{1,17},{... | collective-permute-start | bytes 614408 | tf_op jit(solution)/shard_map/ppermute | solution.py:280
  119.9 19.1 %collective-permute-start.21 = (bf16[160,640]{1,0:T(8,128)(2,1)S(1)}, bf16[160,640]{1,0:T(8,128)(2,1)S(1)}, u32[]{:S(2)}, u32[]{:S(2)}) collective-permute-start(bf16[160,640]{1,0:T(8,128)(2,1)S(1)} %fusion.10), channel_id=1, source_target_pairs={{0,16},{4,20},{8,24},{12,28},{16,0},{20,4},{24,8},{28,12},{1,17},{... | collective-permute-start | bytes 614408 | tf_op jit(solution)/shard_map/ppermute | solution.py:280
  (29 other events, 137.0 us)

commit v3 on v2

--- a/solution.py
+++ b/solution.py
@@ -15,6 +15,7 @@
 TN = (((0,), (0,)), ((), ()))
 VMEM_BYTES = 32 * 1024 * 1024
 COST_SCALE = 20
+FIRST_VMEM_BYTES = 32 * 1024 * 1024
 
 
 def dot(a, b, dims=NN):
@@ -70,7 +71,7 @@
     return values.reshape(heads, HEAD_DIM, values.shape[1])
 
 
-def call(kernel, grid, in_specs, out_specs, out_shape, scratch=(), flops=0, prefetch=0):
+def call(kernel, grid, in_specs, out_specs, out_shape, scratch=(), flops=0, prefetch=0, vmem=VMEM_BYTES):
     return pl.pallas_call(
         kernel,
         out_shape=out_shape,
@@ -82,7 +83,7 @@
             scratch_shapes=list(scratch),
         ),
         compiler_params=pltpu.CompilerParams(
-            vmem_limit_bytes=VMEM_BYTES, dimension_semantics=("arbitrary",) * len(grid)
+            vmem_limit_bytes=vmem, dimension_semantics=("arbitrary",) * len(grid)
         ),
         cost_estimate=pl.CostEstimate(flops=flops * COST_SCALE, bytes_accessed=4_000_000 * COST_SCALE, transcendentals=0),
     )
@@ -283,14 +284,6 @@
 def shifted(value, axis, size, step):
     pairs = [(i, i + step) for i in range(size) if 0 <= i + step < size]
     return lax.ppermute(value, axis, pairs)
-
-
-def butterfly(value, axis, size):
-    bit = 1
-    while bit < size:
-        value = value + swap(value, axis, size, bit)
-        bit *= 2
-    return value
 
 
 def pack(state, total):
@@ -393,6 +386,7 @@
         [long] * 3
         + [jax.ShapeDtypeStruct((heads, 128), F32), jax.ShapeDtypeStruct((channels, n_state), F32)],
         flops=4 * channels * length * n_state,
+        vmem=FIRST_VMEM_BYTES,
     )(x, b, dt, alog2, skip2)
     total = totals[:, 0]
     local_state = decay(total) * gathered.reshape(heads, HEAD_DIM, n_state)
@@ -516,7 +510,7 @@
             terms(*held["mixed"], s, orders[s][0], my_bit(orders[s][0]), F32, after) for s in (0, 1)
         ]
         held["back"] = back(after)
-        return held["keeps"], held["back"]
+        return held["keeps"], held["back"], held["gots"]
 
     long = jax.ShapeDtypeStruct((heads, 1, length), F32)
     wide = jax.ShapeDtypeStruct((length, n_state), F32)
@@ -532,12 +526,12 @@
         [pltpu.VMEM((length, length), BF16)] * 2 + [pltpu.VMEM((length, length), F32)],
         flops=10 * channels * length * length,
     )(x, y_cotan, inner, state_in, b, c, grown, shrunk, after)
-    _, cotan_end, _ = pair_scan(
+    works, cotan_end, _ = pair_scan(
         local_cotan.reshape(heads, HEAD_DIM, n_state), total, n_seq, True,
         {0: traded, 1: sending, 2: keeping},
     )
     mixed = held["mixed"][0]
-    outer, from_y, grad_b, grad_c = held["back"]
+    keeps, (outer, from_y, grad_b, grad_c), gots = works[2]
 
     def halve(sums, left):
         axis = sorted(left, reverse=True).index(left[0])
@@ -546,7 +540,7 @@
 
     streams = []
     for s in (0, 1):
-        sums = held["keeps"][s] + held["gots"][s].astype(F32)
+        sums = keeps[s] + gots[s].astype(F32)
         sums = sums.reshape((2,) * (n_bits - 1) + (out_columns, half))
         streams.append(halve(sums, orders[s][1:]))
     grad_inputs, grad_dt, small, both = call(
@@ -586,17 +580,18 @@
     )
     if n_tensor == 2:
         both_other = swap(both, "tensor", 2, 1)
-    small = butterfly(small, "dp", n_dp)
+    small = small + swap(small, "dp", 2, 1)
     for done in range(1, n_bits):
-        pairs = []
-        for s in (0, 1):
-            keep, send = streams[s]
-            pairs.append(keep + swap(send, "seq", n_seq, 1 << orders[s][done]).astype(F32))
+        gots = [swap(streams[s][1], "seq", n_seq, 1 << orders[s][done]) for s in (0, 1)]
+        if done == 1:
+            gots, both, small = lax.optimization_barrier((gots, both, small))
+        pairs = [streams[s][0] + gots[s].astype(F32) for s in (0, 1)]
         if done + 1 < n_bits:
             streams = [halve(pairs[s], orders[s][done + 1 :]) for s in (0, 1)]
             if done + 2 == n_bits:
-                small, streams = lax.optimization_barrier((small, streams))
-    small = butterfly(small, "seq", n_seq)
+                small, _ = lax.optimization_barrier((small, [stream[1] for stream in streams]))
+    small = lax.all_to_all(jnp.broadcast_to(small, (n_seq,) + small.shape), "seq", 0, 0)
+    small = jnp.sum(small[:, :, :, 0], axis=0)
     if n_tensor == 2:
         both_other, small = lax.optimization_barrier((both_other, small))
         both = both + both_other
@@ -610,8 +605,8 @@
         both[None, :, :n_state],
         both[None, :, n_state:],
         grad_dt[None],
-        small[0, :, 0],
-        small[1, :, 0],
+        small[0],
+        small[1],
         grad_w,
     )
 

time: 140 us -> 127 us (0.907)
  waiting for transfers between devices: 49.4 us -> 35.5 us
  starting transfers between devices: 32 us -> 34.9 us
  other arithmetic: 10 us -> 7.95 us
    ppermute x19 -> x16, waiting for transfers between devices: 43.8 us -> 31.7 us  [swap(): return lax.ppermute(value, axis, [(i, i ^ bit) for i in range(size)])]
    all_to_all x0 -> x1, starting transfers between devices: none -> 4.52 us  [per_device(): lax.all_to_all(jnp.broadcast_to(small, (n_seq,) + small.shape), 'seq', 0, 0)]
    ppermute x4, waiting for transfers between devices: 5.6 us -> 3.7 us  [shifted(): return lax.ppermute(value, axis, pairs)]
    ppermute x19 -> x16, starting transfers between devices: 20.3 us -> 18.8 us  [swap(): return lax.ppermute(value, axis, [(i, i ^ bit) for i in range(size)])]
    add x8 -> x5, other arithmetic: 4.07 us -> 2.72 us  [the longest x2 2.44 us: per_device(): pairs = [streams[s][0] + gots[s].astype(F32) for s in (0, 1)]]
    unnamed x78 -> x52, local copies, waits for them, and re-layouts: 11.5 us -> 11.4 us
  transfers between devices with their start and end apart: 23 -> 21, of which waited for: 12 -> 11; matrix products, arithmetic and copies ran while one was open for 8% -> 7% of each run, Pallas kernels for 22% -> 24%
where the time goes in v3:
time: 127 us; the launch traced here: 126 us
  waiting for transfers between devices  35.5 us (28%)
  starting transfers between devices  34.9 us (27%)
  Pallas kernels  32.5 us (26%)
  local copies, waits for them, and re-layouts  14.1 us (11%)
  other arithmetic  7.95 us (6%)
  between operations  1.35 us (1%)
    ppermute x16, waiting for transfers between devices, swap(): return lax.ppermute(value, axis, [(i, i ^ bit) for i in range(size)])  31.7 us
    ppermute x16, starting transfers between devices, swap(): return lax.ppermute(value, axis, [(i, i ^ bit) for i in range(size)])  18.8 us
    ppermute x4, starting transfers between devices, shifted(): return lax.ppermute(value, axis, pairs)  11.6 us
    unnamed x52, local copies, waits for them, and re-layouts  11.4 us
    pallas_call x1, Pallas kernels, per_device(): call(back_kernel, grid, [by_row(block, length)] * 3 + [by_row(block, n_st...  6.47 us
    pallas_call x1, Pallas kernels, per_device(): call(last_kernel, grid, [by_row(block, length)] * 3 + [by_row(block, n_st...  5.33 us
    pallas_call x4, Pallas kernels, terms(): call(terms_kernel, (1,), [columns, columns, rows, rows, ANY], whole(n_seq...  4.81 us
    pallas_call x1, Pallas kernels, per_device(): call(cotan_kernel, wide_grid, [weights(0), weights(1)] + [whole(half_feat...  4.57 us
  transfers between devices with their start and end apart: 21, of which 11 were waited for; matrix products, arithmetic and copies ran while one was open for 7% of the time, Pallas kernels for 24%

profile of v3, /device:TPU:0, one launch (start us, length us, event | category | flops | bytes accessed | tf_op | source)
XLA Modules:
  0.0 126.3 jit_solution(4236678016626975429)
XLA Ops:
  1.4 1.3 %copy-done.6 = bf16[1,1280,512]{2,1,0:T(8,128)(2,1)S(1)} copy-done((bf16[1,1280,512]{2,1,0:T(8,128)(2,1)S(1)}, bf16[1,1280,512]{2,1,0:T(8,128)(2,1)}, u32[]{:S(2)}) %copy-start.6) | copy-done | bytes 1310744
  5.0 2.3 %shard_map.143 = (f32[20,1,512]{2,1,0:T(1,128)S(1)}, f32[20,1,512]{2,1,0:T(1,128)S(1)}, f32[20,1,512]{2,1,0:T(1,128)S(1)}, f32[20,128]{1,0:T(8,128)S(1)}, f32[1280,128]{1,0:T(8,128)S(1)}) custom-call(bf16[1280,512]{1,0:T(8,128)(2,1)S(1)} %bitcast.216, bf16[512,128]{1,0:T(8,128)(2,1)S(1)} %bitcast.230, f32[20,512]{1,0:T(8,128)S(1)} %bitcast.213, ...), custom_call_target="tpu_custom_call" | custom-call | flops 6710886400 | bytes 80000000 | tf_op jit(solution)/shard_map/pallas_call | solution.py:381
  7.7 3.0 %collective-permute-start = (bf16[21,32,128]{2,1,0:T(8,128)(2,1)S(1)}, bf16[21,32,128]{2,1,0:T(8,128)(2,1)S(1)}, u32[]{:S(2)}, u32[]{:S(2)}) collective-permute-start(bf16[21,32,128]{2,1,0:T(8,128)(2,1)S(1)} %pad_maximum_fusion.5.after_ref), channel_id=1, source_target_pairs={{0,4},{4,0},{8,12},{12,8},{16,20},{20,16},{24,28},{28,24},{1,5},{5... | collective-permute-start | bytes 516104 | tf_op jit(solution)/shard_map/ppermute | solution.py:281
  10.7 1.6 %collective-permute-start.5 = (bf16[1280,512]{1,0:T(8,128)(2,1)S(1)}, bf16[1280,512]{1,0:T(8,128)(2,1)S(1)}, u32[]{:S(2)}, u32[]{:S(2)}) collective-permute-start(bf16[1280,512]{1,0:T(8,128)(2,1)S(1)} %bitcast.200), channel_id=1, source_target_pairs={{0,1},{1,0},{2,3},{3,2},{4,5},{5,4},{6,7},{7,6},{8,9},{9,8},{10,11... | collective-permute-start | bytes 3932168 | tf_op jit(solution)/shard_map/ppermute | solution.py:281
  12.3 1.3 %copy-done.7 = bf16[1,1280,512]{2,1,0:T(8,128)(2,1)S(1)} copy-done((bf16[1,1280,512]{2,1,0:T(8,128)(2,1)S(1)}, bf16[1,1280,512]{2,1,0:T(8,128)(2,1)}, u32[]{:S(2)}) %copy-start.7) | copy-done | bytes 1310744
  13.6 2.8 %shard_map.144.inner_ref = f32[1280,512]{1,0:T(8,128)S(1)} custom-call(bf16[1280,512]{1,0:T(8,128)(2,1)S(1)} %bitcast.217, bf16[512,128]{1,0:T(8,128)(2,1)S(1)} %bitcast.231, bf16[512,128]{1,0:T(8,128)(2,1)S(1)} %bitcast.226, f32[20,1,512]{2,1,0:T(1,128)S(1)} %get-tuple-element.49.shrunk_ref, bf16[21,32,128]{2,1,0:T(8,128)(2,1)S(1)} %pad_maximum_fusion.5.after_ref), custom_call_target="tpu_custom_call" | custom-call | flops 33554432000 | bytes 80000000 | tf_op jit(solution)/shard_map/pallas_call | solution.py:394
  16.4 1.5 %copy-done.16 = f32[1280,512]{1,0:T(8,128)} copy-done((f32[1280,512]{1,0:T(8,128)}, f32[1280,512]{1,0:T(8,128)S(1)}, u32[]{:S(2)}) %copy-start.16) | copy-done | bytes 2621464
  19.1 3.5 %collective-permute-start.1 = (bf16[21,32,128]{2,1,0:T(8,128)(2,1)S(1)}, bf16[21,32,128]{2,1,0:T(8,128)(2,1)S(1)}, u32[]{:S(2)}, u32[]{:S(2)}) collective-permute-start(bf16[21,32,128]{2,1,0:T(8,128)(2,1)S(1)} %pad_maximum_fusion.6.after_ref), channel_id=1, source_target_pairs={{0,8},{4,12},{8,16},{12,20},{16,24},{20,28},{1,9},{5,13},{9,17},{1... | collective-permute-start | bytes 516104 | tf_op jit(solution)/shard_map/ppermute | solution.py:286
  22.6 3.5 %shard_map.145.first_ref = f32[1280,512]{1,0:T(8,128)S(1)} custom-call(s32[1]{0:T(128)} %bitcast.12.flag_ref, bf16[1280,1280]{1,0:T(8,128)(2,1)S(1)} %copy-done.5, bf16[1280,1280]{1,0:T(8,128)(2,1)} %collective-permute-done.2.other_ref, bf16[1280,512]{1,0:T(8,128)(2,1)S(1)} %bitcast.202, bf16[21,32,128]{2,1,0:T(8,128)(2,1)S(1)} %pad_maximum_fusion.6.after_ref), custom_call_target="tpu_custom_call" | custom-call | flops 33554432000 | bytes 80000000 | tf_op jit(solution)/shard_map/pallas_call | solution.py:416
  26.8 5.4 %collective-permute-start.3 = (bf16[21,32,128]{2,1,0:T(8,128)(2,1)S(1)}, bf16[21,32,128]{2,1,0:T(8,128)(2,1)S(1)}, u32[]{:S(2)}, u32[]{:S(2)}) collective-permute-start(bf16[21,32,128]{2,1,0:T(8,128)(2,1)S(1)} %pad_maximum_fusion.7), channel_id=1, source_target_pairs={{0,16},{4,20},{8,24},{12,28},{1,17},{5,21},{9,25},{13,29},{2,18},{... | collective-permute-start | bytes 516104 | tf_op jit(solution)/shard_map/ppermute | solution.py:286
  32.2 3.1 %collective-permute-done.3 = bf16[21,32,128]{2,1,0:T(8,128)(2,1)S(1)} collective-permute-done((bf16[21,32,128]{2,1,0:T(8,128)(2,1)S(1)}, bf16[21,32,128]{2,1,0:T(8,128)(2,1)S(1)}, u32[]{:S(2)}, u32[]{:S(2)}) %collective-permute-start.3) | collective-permute-done | bytes 172064 | tf_op jit(solution)/shard_map/ppermute | solution.py:286
  36.0 5.8 %collective-permute-done.5.g_ref = bf16[1280,512]{1,0:T(8,128)(2,1)S(1)} collective-permute-done((bf16[1280,512]{1,0:T(8,128)(2,1)S(1)}, bf16[1280,512]{1,0:T(8,128)(2,1)S(1)}, u32[]{:S(2)}, u32[]{:S(2)}) %collective-permute-start.5) | collective-permute-done | bytes 1310752 | tf_op jit(solution)/shard_map/ppermute | solution.py:281
  41.9 4.6 %shard_map.146 = (bf16[1280,512]{1,0:T(8,128)(2,1)S(1)}, f32[1280,128]{1,0:T(8,128)S(1)}) custom-call(s32[1]{0:T(128)} %bitcast.12.flag_ref, bf16[1280,1280]{1,0:T(8,128)(2,1)S(1)} %copy-done.5, bf16[1280,1280]{1,0:T(8,128)(2,1)} %collective-permute-done.2.other_ref, bf16[1280,512]{1,0:T(8,128)(2,1)S(1)} %collective-permute-done.5.g_ref, ...), custom_call_target="tpu_custom_call" | custom-call | flops 40265318400 | bytes 80000000 | tf_op jit(solution)/shard_map/pallas_call | solution.py:425
  48.1 1.3 copy-done.17
  49.7 2.8 %shard_map.147.m0_ref = bf16[1280,512]{1,0:T(8,128)(2,1)} custom-call(f32[1280,512]{1,0:T(8,128)S(1)} %copy-done.17, bf16[1280,128]{1,0:T(8,128)(2,1)S(1)} %bitcast.209, bf16[512,128]{1,0:T(8,128)(2,1)S(1)} %bitcast.228, bf16[1280,512]{1,0:T(8,128)(2,1)S(1)} %bitcast.218, f32[20,1,512]{2,1,0:T(1,128)S(1)} %get-tuple-element.53.grown_ref, ...), custom_call_target="tpu_custom_call" | custom-call | flops 3355443200 | bytes 80000000 | tf_op jit(solution)/shard_map/pallas_call | solution.py:444
  53.2 1.3 %collective-permute-start.7 = (bf16[21,32,128]{2,1,0:T(8,128)(2,1)S(1)}, bf16[21,32,128]{2,1,0:T(8,128)(2,1)S(1)}, u32[]{:S(2)}, u32[]{:S(2)}) collective-permute-start(bf16[21,32,128]{2,1,0:T(8,128)(2,1)S(1)} %pad_maximum_fusion.8.after_ref), channel_id=1, source_target_pairs={{8,0},{12,4},{16,8},{20,12},{24,16},{28,20},{9,1},{13,5},{17,9},{2... | collective-permute-start | bytes 516104 | tf_op jit(solution)/shard_map/ppermute | solution.py:286
  54.6 1.3 %collective-permute-done.9.m1_ref = bf16[1280,512]{1,0:T(8,128)(2,1)S(1)} collective-permute-done((bf16[1280,512]{1,0:T(8,128)(2,1)}, bf16[1280,512]{1,0:T(8,128)(2,1)S(1)}, u32[]{:S(2)}, u32[]{:S(2)}) %collective-permute-start.9) | collective-permute-done | bytes 1310752 | tf_op jit(solution)/shard_map/ppermute | solution.py:281
  57.1 1.5 %collective-permute-start.11 = (bf16[4,160,640]{2,1,0:T(8,128)(2,1)S(1)}, bf16[4,160,640]{2,1,0:T(8,128)(2,1)S(1)}, u32[]{:S(2)}, u32[]{:S(2)}) collective-permute-start(bf16[4,160,640]{2,1,0:T(8,128)(2,1)S(1)} %shard_map.148), channel_id=1, source_target_pairs={{0,4},{4,0},{8,12},{12,8},{16,20},{20,16},{24,28},{28,24},{1,5},{5... | collective-permute-start | bytes 2457608 | tf_op jit(solution)/shard_map/ppermute | solution.py:281
  59.8 1.6 %collective-permute-start.12 = (bf16[4,160,640]{2,1,0:T(8,128)(2,1)S(1)}, bf16[4,160,640]{2,1,0:T(8,128)(2,1)S(1)}, u32[]{:S(2)}, u32[]{:S(2)}) collective-permute-start(bf16[4,160,640]{2,1,0:T(8,128)(2,1)S(1)} %shard_map.149), channel_id=1, source_target_pairs={{0,8},{4,12},{8,0},{12,4},{16,24},{20,28},{24,16},{28,20},{1,9},{5... | collective-permute-start | bytes 2457608 | tf_op jit(solution)/shard_map/ppermute | solution.py:281
  61.8 1.5 %collective-permute-start.10 = (bf16[21,32,128]{2,1,0:T(8,128)(2,1)S(1)}, bf16[21,32,128]{2,1,0:T(8,128)(2,1)S(1)}, u32[]{:S(2)}, u32[]{:S(2)}) collective-permute-start(bf16[21,32,128]{2,1,0:T(8,128)(2,1)S(1)} %pad_maximum_fusion.9.after_ref), channel_id=1, source_target_pairs={{16,0},{20,4},{24,8},{28,12},{17,1},{21,5},{25,9},{29,13},{18,2},{... | collective-permute-start | bytes 516104 | tf_op jit(solution)/shard_map/ppermute | solution.py:286
  63.3 6.5 %shard_map.152 = (f32[1280,512]{1,0:T(8,128)S(1)}, f32[20,1,512]{2,1,0:T(1,128)S(1)}, f32[512,128]{1,0:T(8,128)S(1)}, f32[512,128]{1,0:T(8,128)S(1)}) custom-call(bf16[1280,512]{1,0:T(8,128)(2,1)S(1)} %bitcast.219, bf16[1280,512]{1,0:T(8,128)(2,1)S(1)} %get-tuple-element.59.cotan_ref, f32[1280,512]{1,0:T(8,128)S(1)} %copy-done.17, ...), custom_call_target="tpu_custom_call" | custom-call | flops 67108864000 | bytes 80000000 | tf_op jit(solution)/shard_map/pallas_call | solution.py:517
  72.2 5.5 %collective-permute-done.11 = bf16[4,160,640]{2,1,0:T(8,128)(2,1)S(1)} collective-permute-done((bf16[4,160,640]{2,1,0:T(8,128)(2,1)S(1)}, bf16[4,160,640]{2,1,0:T(8,128)(2,1)S(1)}, u32[]{:S(2)}, u32[]{:S(2)}) %collective-permute-start.11) | collective-permute-done | bytes 819232 | tf_op jit(solution)/shard_map/ppermute | solution.py:281
  77.7 6.0 %collective-permute-done.12 = bf16[4,160,640]{2,1,0:T(8,128)(2,1)S(1)} collective-permute-done((bf16[4,160,640]{2,1,0:T(8,128)(2,1)S(1)}, bf16[4,160,640]{2,1,0:T(8,128)(2,1)S(1)}, u32[]{:S(2)}, u32[]{:S(2)}) %collective-permute-start.12) | collective-permute-done | bytes 819232 | tf_op jit(solution)/shard_map/ppermute | solution.py:281
  84.9 2.6 %collective-permute-start.14 = (bf16[2,160,640]{2,1,0:T(8,128)(2,1)S(1)}, bf16[2,160,640]{2,1,0:T(8,128)(2,1)}, u32[]{:S(2)}, u32[]{:S(2)}) collective-permute-start(bf16[2,160,640]{2,1,0:T(8,128)(2,1)S(1)} %fusion.after_a_ref), channel_id=1, source_target_pairs={{0,8},{4,12},{8,0},{12,4},{16,24},{20,28},{24,16},{28,20},{1,9},{5... | collective-permute-start | bytes 1228808 | tf_op jit(solution)/shard_map/ppermute | solution.py:281
  87.8 1.4 %collective-permute-start.15 = (bf16[2,160,640]{2,1,0:T(8,128)(2,1)S(1)}, bf16[2,160,640]{2,1,0:T(8,128)(2,1)}, u32[]{:S(2)}, u32[]{:S(2)}) collective-permute-start(bf16[2,160,640]{2,1,0:T(8,128)(2,1)S(1)} %fusion.1.after_b_ref), channel_id=1, source_target_pairs={{0,4},{4,0},{8,12},{12,8},{16,20},{20,16},{24,28},{28,24},{1,5},{5... | collective-permute-start | bytes 1228808 | tf_op jit(solution)/shard_map/ppermute | solution.py:281
  89.9 5.3 %shard_map.153 = (bf16[1280,512]{1,0:T(8,128)(2,1)}, f32[20,512]{1,0:T(8,128)S(1)}, f32[2,20,128]{2,1,0:T(8,128)S(1)}, f32[512,256]{1,0:T(8,128)S(1)}) custom-call(bf16[1280,512]{1,0:T(8,128)(2,1)S(1)} %bitcast.220, bf16[1280,512]{1,0:T(8,128)(2,1)S(1)} %get-tuple-element.59.cotan_ref, f32[1280,512]{1,0:T(8,128)S(1)} %get-tuple-element.66.outer_ref, ...), custom_call_target="tpu_custom_call" | custom-call | flops 10066329600 | bytes 80000000 | tf_op jit(solution)/shard_map/pallas_call | solution.py:546
  95.2 1.5 %collective-permute-start.17 = (f32[512,256]{1,0:T(8,128)S(1)}, f32[512,256]{1,0:T(8,128)}, u32[]{:S(2)}, u32[]{:S(2)}) collective-permute-start(f32[512,256]{1,0:T(8,128)S(1)} %get-tuple-element.78), channel_id=1, source_target_pairs={{0,1},{1,0},{2,3},{3,2},{4,5},{5,4},{6,7},{7,6},{8,9},{9,8},{10,11... | collective-permute-start | bytes 1572872 | tf_op jit(solution)/shard_map/ppermute | solution.py:281
  98.2 1.3 %bitcast_add_fusion = f32[2,160,640]{2,1,0:T(8,128)S(1)} fusion(bf16[2,160,640]{2,1,0:T(8,128)(2,1)} %collective-permute-done.15, f32[2,2,160,640]{3,2,1,0:T(8,128)} %bitcast.240, s32[]{:T(128)S(6)} %select_n.238), kind=kLoop, calls=%fused_computation.6 | loop fusion | flops 409600 | bytes 2048004 | tf_op jit(solution)/shard_map/add | solution.py:588
  101.8 3.0 %collective-permute-start.18 = (bf16[160,640]{1,0:T(8,128)(2,1)S(1)}, bf16[160,640]{1,0:T(8,128)(2,1)S(1)}, u32[]{:S(2)}, u32[]{:S(2)}) collective-permute-start(bf16[160,640]{1,0:T(8,128)(2,1)S(1)} %fusion.12), channel_id=1, source_target_pairs={{0,16},{4,20},{8,24},{12,28},{16,0},{20,4},{24,8},{28,12},{1,17},{... | collective-permute-start | bytes 614408 | tf_op jit(solution)/shard_map/ppermute | solution.py:281
  105.5 4.5 %all-to-all-start = ((f32[8,2,20,128]{3,1,2,0:T(2,128)}), f32[8,2,20,128]{3,1,2,0:T(2,128)S(1)}, u32[]{:S(2)}, u32[]{:S(2)}) async-start(f32[8,2,20,128]{3,1,2,0:T(2,128)} %broadcast_in_dim.76), calls=%async_computation | async-start | bytes 327680 | tf_op jit(solution)/shard_map/all_to_all | solution.py:593
  110.0 9.2 %collective-permute-done.19 = bf16[160,640]{1,0:T(8,128)(2,1)} collective-permute-done((bf16[160,640]{1,0:T(8,128)(2,1)S(1)}, bf16[160,640]{1,0:T(8,128)(2,1)}, u32[]{:S(2)}, u32[]{:S(2)}) %collective-permute-start.19) | collective-permute-done | bytes 204832 | tf_op jit(solution)/shard_map/ppermute | solution.py:281
  120.2 2.5 %collective-permute-done.18 = bf16[160,640]{1,0:T(8,128)(2,1)S(1)} collective-permute-done((bf16[160,640]{1,0:T(8,128)(2,1)S(1)}, bf16[160,640]{1,0:T(8,128)(2,1)S(1)}, u32[]{:S(2)}, u32[]{:S(2)}) %collective-permute-start.18) | collective-permute-done | bytes 204832 | tf_op jit(solution)/shard_map/ppermute | solution.py:281
  (143 shorter events, 24.6 us)
Async XLA Ops:
  1.4 5.8 %copy-start.3 = (f32[1,20,512]{2,1,0:T(8,128)}, f32[1,20,512]{2,1,0:T(8,128)S(1)}, u32[]{:S(2)}) copy-start(f32[1,20,512]{2,1,0:T(8,128)S(1)} %copy.61) | copy-start | bytes 122884
  7.3 3.4 %copy-start.1 = (f32[1280,128]{1,0:T(8,128)}, f32[1280,128]{1,0:T(8,128)S(1)}, u32[]{:S(2)}) copy-start(f32[1280,128]{1,0:T(8,128)S(1)} %get-tuple-element.48.gathered_ref) | copy-start | bytes 1966084
  7.3 3.4 %copy-start = (bf16[1,1280,512]{2,1,0:T(8,128)(2,1)S(1)}, bf16[1,1280,512]{2,1,0:T(8,128)(2,1)}, u32[]{:S(2)}) copy-start(bf16[1,1280,512]{2,1,0:T(8,128)(2,1)} %param.15) | copy-start | bytes 3932164
  7.3 5.0 %copy-start.10 = (bf16[1,512,128]{2,1,0:T(8,128)(2,1)S(1)}, bf16[1,512,128]{2,1,0:T(8,128)(2,1)}, u32[]{:S(2)}) copy-start(bf16[1,512,128]{2,1,0:T(8,128)(2,1)} %param.10) | copy-start | bytes 393220
  7.3 5.0 %copy-start.12 = (bf16[1,512,128]{2,1,0:T(8,128)(2,1)S(1)}, bf16[1,512,128]{2,1,0:T(8,128)(2,1)}, u32[]{:S(2)}) copy-start(bf16[1,512,128]{2,1,0:T(8,128)(2,1)} %param.9) | copy-start | bytes 393220
  7.6 4.7 %copy-start.21 = (f32[20,2,32,128]{3,2,0,1:T(8,128)}, f32[20,2,32,128]{3,2,0,1:T(8,128)S(1)}, u32[]{:S(2)}) copy-start(f32[20,2,32,128]{3,2,0,1:T(8,128)S(1)} %copy_multiply_fusion) | copy-start | bytes 1966084
  7.7 10.3 %collective-permute-start = (bf16[21,32,128]{2,1,0:T(8,128)(2,1)S(1)}, bf16[21,32,128]{2,1,0:T(8,128)(2,1)S(1)}, u32[]{:S(2)}, u32[]{:S(2)}) collective-permute-start(bf16[21,32,128]{2,1,0:T(8,128)(2,1)S(1)} %pad_maximum_fusion.5.after_ref), channel_id=1, source_target_pairs={{0,4},{4,0},{8,12},{12,8},{16,20},{20,16},{24,28},{28,24},{1,5},{5... | collective-permute-start | bytes 516104 | tf_op jit(solution)/shard_map/ppermute | solution.py:281
  10.7 12.0 %collective-permute-start.2 = (bf16[1280,1280]{1,0:T(8,128)(2,1)}, bf16[1280,1280]{1,0:T(8,128)(2,1)}, u32[]{:S(2)}, u32[]{:S(2)}) collective-permute-start(bf16[1280,1280]{1,0:T(8,128)(2,1)} %mine_ref.3), channel_id=1, source_target_pairs={{0,2},{2,0},{1,3},{3,1},{4,6},{6,4},{5,7},{7,5},{8,10},{10,8},{9,1... | collective-permute-start | bytes 9830408 | tf_op jit(solution)/shard_map/ppermute | solution.py:281
  10.7 31.2 %collective-permute-start.5 = (bf16[1280,512]{1,0:T(8,128)(2,1)S(1)}, bf16[1280,512]{1,0:T(8,128)(2,1)S(1)}, u32[]{:S(2)}, u32[]{:S(2)}) collective-permute-start(bf16[1280,512]{1,0:T(8,128)(2,1)S(1)} %bitcast.200), channel_id=1, source_target_pairs={{0,1},{1,0},{2,3},{3,2},{4,5},{5,4},{6,7},{7,6},{8,9},{9,8},{10,11... | collective-permute-start | bytes 3932168 | tf_op jit(solution)/shard_map/ppermute | solution.py:281
  17.9 4.7 %copy-start.5 = (bf16[1280,1280]{1,0:T(8,128)(2,1)S(1)}, bf16[1280,1280]{1,0:T(8,128)(2,1)}, u32[]{:S(2)}) copy-start(bf16[1280,1280]{1,0:T(8,128)(2,1)} %mine_ref.3) | copy-start | bytes 9830404
  19.1 7.5 %collective-permute-start.1 = (bf16[21,32,128]{2,1,0:T(8,128)(2,1)S(1)}, bf16[21,32,128]{2,1,0:T(8,128)(2,1)S(1)}, u32[]{:S(2)}, u32[]{:S(2)}) collective-permute-start(bf16[21,32,128]{2,1,0:T(8,128)(2,1)S(1)} %pad_maximum_fusion.6.after_ref), channel_id=1, source_target_pairs={{0,8},{4,12},{8,16},{12,20},{16,24},{20,28},{1,9},{5,13},{9,17},{1... | collective-permute-start | bytes 516104 | tf_op jit(solution)/shard_map/ppermute | solution.py:286
  26.8 8.5 %collective-permute-start.3 = (bf16[21,32,128]{2,1,0:T(8,128)(2,1)S(1)}, bf16[21,32,128]{2,1,0:T(8,128)(2,1)S(1)}, u32[]{:S(2)}, u32[]{:S(2)}) collective-permute-start(bf16[21,32,128]{2,1,0:T(8,128)(2,1)S(1)} %pad_maximum_fusion.7), channel_id=1, source_target_pairs={{0,16},{4,20},{8,24},{12,28},{1,17},{5,21},{9,25},{13,29},{2,18},{... | collective-permute-start | bytes 516104 | tf_op jit(solution)/shard_map/ppermute | solution.py:286
  35.5 12.3 %collective-permute-start.4 = (bf16[20,32,128]{2,1,0:T(8,128)(2,1)S(1)}, bf16[20,32,128]{2,1,0:T(8,128)(2,1)S(1)}, u32[]{:S(2)}, u32[]{:S(2)}) collective-permute-start(bf16[20,32,128]{2,1,0:T(8,128)(2,1)S(1)} %select_convert_fusion.4.after_ref), channel_id=1, source_target_pairs={{0,4},{4,0},{8,12},{12,8},{16,20},{20,16},{24,28},{28,24},{1,5},{5... | collective-permute-start | bytes 491528 | tf_op jit(solution)/shard_map/ppermute | solution.py:281
  46.5 6.5 %collective-permute-start.6 = (bf16[21,32,128]{2,1,0:T(8,128)(2,1)S(1)}, bf16[21,32,128]{2,1,0:T(8,128)(2,1)S(1)}, u32[]{:S(2)}, u32[]{:S(2)}) collective-permute-start(bf16[21,32,128]{2,1,0:T(8,128)(2,1)S(1)} %pad_maximum_fusion.4.after_ref), channel_id=1, source_target_pairs={{0,4},{4,0},{8,12},{12,8},{16,20},{20,16},{24,28},{28,24},{1,5},{5... | collective-permute-start | bytes 516104 | tf_op jit(solution)/shard_map/ppermute | solution.py:281
  47.5 7.1 %collective-permute-start.8 = (bf16[8,160,512]{2,1,0:T(8,128)(2,1)S(1)}, bf16[8,160,512]{2,1,0:T(8,128)(2,1)S(1)}, u32[]{:S(2)}, u32[]{:S(2)}) collective-permute-start(bf16[8,160,512]{2,1,0:T(8,128)(2,1)S(1)} %pad_maximum_fusion.1), channel_id=1, source_target_pairs={{0,2},{2,0},{1,3},{3,1},{4,6},{6,4},{5,7},{7,5},{8,10},{10,8},{9,1... | collective-permute-start | bytes 3932168 | tf_op jit(solution)/shard_map/ppermute | solution.py:281
  52.5 3.4 %copy-start.9 = (bf16[1280,512]{1,0:T(8,128)(2,1)S(1)}, bf16[1280,512]{1,0:T(8,128)(2,1)}, u32[]{:S(2)}) copy-start(bf16[1280,512]{1,0:T(8,128)(2,1)} %shard_map.147.m0_ref) | copy-start | bytes 3932164
  52.5 3.4 %collective-permute-start.9 = (bf16[1280,512]{1,0:T(8,128)(2,1)}, bf16[1280,512]{1,0:T(8,128)(2,1)S(1)}, u32[]{:S(2)}, u32[]{:S(2)}) collective-permute-start(bf16[1280,512]{1,0:T(8,128)(2,1)} %shard_map.147.m0_ref), channel_id=1, source_target_pairs={{0,2},{2,0},{1,3},{3,1},{4,6},{6,4},{5,7},{7,5},{8,10},{10,8},{9,1... | collective-permute-start | bytes 3932168 | tf_op jit(solution)/shard_map/ppermute | solution.py:281
  53.2 8.3 %collective-permute-start.7 = (bf16[21,32,128]{2,1,0:T(8,128)(2,1)S(1)}, bf16[21,32,128]{2,1,0:T(8,128)(2,1)S(1)}, u32[]{:S(2)}, u32[]{:S(2)}) collective-permute-start(bf16[21,32,128]{2,1,0:T(8,128)(2,1)S(1)} %pad_maximum_fusion.8.after_ref), channel_id=1, source_target_pairs={{8,0},{12,4},{16,8},{20,12},{24,16},{28,20},{9,1},{13,5},{17,9},{2... | collective-permute-start | bytes 516104 | tf_op jit(solution)/shard_map/ppermute | solution.py:286
  57.1 20.6 %collective-permute-start.11 = (bf16[4,160,640]{2,1,0:T(8,128)(2,1)S(1)}, bf16[4,160,640]{2,1,0:T(8,128)(2,1)S(1)}, u32[]{:S(2)}, u32[]{:S(2)}) collective-permute-start(bf16[4,160,640]{2,1,0:T(8,128)(2,1)S(1)} %shard_map.148), channel_id=1, source_target_pairs={{0,4},{4,0},{8,12},{12,8},{16,20},{20,16},{24,28},{28,24},{1,5},{5... | collective-permute-start | bytes 2457608 | tf_op jit(solution)/shard_map/ppermute | solution.py:281
  59.8 24.0 %collective-permute-start.12 = (bf16[4,160,640]{2,1,0:T(8,128)(2,1)S(1)}, bf16[4,160,640]{2,1,0:T(8,128)(2,1)S(1)}, u32[]{:S(2)}, u32[]{:S(2)}) collective-permute-start(bf16[4,160,640]{2,1,0:T(8,128)(2,1)S(1)} %shard_map.149), channel_id=1, source_target_pairs={{0,8},{4,12},{8,0},{12,4},{16,24},{20,28},{24,16},{28,20},{1,9},{5... | collective-permute-start | bytes 2457608 | tf_op jit(solution)/shard_map/ppermute | solution.py:281
  61.8 10.4 %collective-permute-start.10 = (bf16[21,32,128]{2,1,0:T(8,128)(2,1)S(1)}, bf16[21,32,128]{2,1,0:T(8,128)(2,1)S(1)}, u32[]{:S(2)}, u32[]{:S(2)}) collective-permute-start(bf16[21,32,128]{2,1,0:T(8,128)(2,1)S(1)} %pad_maximum_fusion.9.after_ref), channel_id=1, source_target_pairs={{16,0},{20,4},{24,8},{28,12},{17,1},{21,5},{25,9},{29,13},{18,2},{... | collective-permute-start | bytes 516104 | tf_op jit(solution)/shard_map/ppermute | solution.py:286
  83.9 5.6 %collective-permute-start.13 = (bf16[20,32,128]{2,1,0:T(8,128)(2,1)S(1)}, bf16[20,32,128]{2,1,0:T(8,128)(2,1)S(1)}, u32[]{:S(2)}, u32[]{:S(2)}) collective-permute-start(bf16[20,32,128]{2,1,0:T(8,128)(2,1)S(1)} %select_convert_fusion.1), channel_id=1, source_target_pairs={{0,4},{4,0},{8,12},{12,8},{16,20},{20,16},{24,28},{28,24},{1,5},{5... | collective-permute-start | bytes 491528 | tf_op jit(solution)/shard_map/ppermute | solution.py:281
  84.8 2.9 %copy-start.18 = (f32[4,160,640]{2,1,0:T(8,128)}, f32[4,160,640]{2,1,0:T(8,128)S(1)}, u32[]{:S(2)}) copy-start(f32[4,160,640]{2,1,0:T(8,128)S(1)} %convert_add_fusion.1) | copy-start | bytes 4915204
  84.9 12.5 %collective-permute-start.14 = (bf16[2,160,640]{2,1,0:T(8,128)(2,1)S(1)}, bf16[2,160,640]{2,1,0:T(8,128)(2,1)}, u32[]{:S(2)}, u32[]{:S(2)}) collective-permute-start(bf16[2,160,640]{2,1,0:T(8,128)(2,1)S(1)} %fusion.after_a_ref), channel_id=1, source_target_pairs={{0,8},{4,12},{8,0},{12,4},{16,24},{20,28},{24,16},{28,20},{1,9},{5... | collective-permute-start | bytes 1228808 | tf_op jit(solution)/shard_map/ppermute | solution.py:281
  87.8 10.4 %collective-permute-start.15 = (bf16[2,160,640]{2,1,0:T(8,128)(2,1)S(1)}, bf16[2,160,640]{2,1,0:T(8,128)(2,1)}, u32[]{:S(2)}, u32[]{:S(2)}) collective-permute-start(bf16[2,160,640]{2,1,0:T(8,128)(2,1)S(1)} %fusion.1.after_b_ref), channel_id=1, source_target_pairs={{0,4},{4,0},{8,12},{12,8},{16,20},{20,16},{24,28},{28,24},{1,5},{5... | collective-permute-start | bytes 1228808 | tf_op jit(solution)/shard_map/ppermute | solution.py:281
  95.2 4.5 %copy-start.19 = (f32[4,160,640]{2,1,0:T(8,128)S(1)}, f32[4,160,640]{2,1,0:T(8,128)}, u32[]{:S(2)}) copy-start(f32[4,160,640]{2,1,0:T(8,128)} %copy-done.18) | copy-start | bytes 4915204
  95.2 2.1 %collective-permute-start.16 = (f32[2,20,128]{2,1,0:T(8,128)S(1)}, f32[2,20,128]{2,1,0:T(8,128)S(1)}, u32[]{:S(2)}, u32[]{:S(2)}) collective-permute-start(f32[2,20,128]{2,1,0:T(8,128)S(1)} %get-tuple-element.77), channel_id=1, source_target_pairs={{0,2},{2,0},{1,3},{3,1},{4,6},{6,4},{5,7},{7,5},{8,10},{10,8},{9,1... | collective-permute-start | bytes 61448 | tf_op jit(solution)/shard_map/ppermute | solution.py:281
  95.2 28.5 %collective-permute-start.17 = (f32[512,256]{1,0:T(8,128)S(1)}, f32[512,256]{1,0:T(8,128)}, u32[]{:S(2)}, u32[]{:S(2)}) collective-permute-start(f32[512,256]{1,0:T(8,128)S(1)} %get-tuple-element.78), channel_id=1, source_target_pairs={{0,1},{1,0},{2,3},{3,2},{4,5},{5,4},{6,7},{7,6},{8,9},{9,8},{10,11... | collective-permute-start | bytes 1572872 | tf_op jit(solution)/shard_map/ppermute | solution.py:281
  99.6 19.6 %collective-permute-start.19 = (bf16[160,640]{1,0:T(8,128)(2,1)S(1)}, bf16[160,640]{1,0:T(8,128)(2,1)}, u32[]{:S(2)}, u32[]{:S(2)}) collective-permute-start(bf16[160,640]{1,0:T(8,128)(2,1)S(1)} %fusion.13), channel_id=1, source_target_pairs={{0,16},{4,20},{8,24},{12,28},{16,0},{20,4},{24,8},{28,12},{1,17},{... | collective-permute-start | bytes 614408 | tf_op jit(solution)/shard_map/ppermute | solution.py:281
  101.8 21.0 %copy-start.24 = (f32[2,160,640]{2,1,0:T(8,128)S(1)}, f32[2,160,640]{2,1,0:T(8,128)}, u32[]{:S(2)}) copy-start(f32[2,160,640]{2,1,0:T(8,128)} %copy-done.23) | copy-start | bytes 2457604
  101.8 21.0 %collective-permute-start.18 = (bf16[160,640]{1,0:T(8,128)(2,1)S(1)}, bf16[160,640]{1,0:T(8,128)(2,1)S(1)}, u32[]{:S(2)}, u32[]{:S(2)}) collective-permute-start(bf16[160,640]{1,0:T(8,128)(2,1)S(1)} %fusion.12), channel_id=1, source_target_pairs={{0,16},{4,20},{8,24},{12,28},{16,0},{20,4},{24,8},{28,12},{1,17},{... | collective-permute-start | bytes 614408 | tf_op jit(solution)/shard_map/ppermute | solution.py:281
  105.5 18.2 %all-to-all-start = ((f32[8,2,20,128]{3,1,2,0:T(2,128)}), f32[8,2,20,128]{3,1,2,0:T(2,128)S(1)}, u32[]{:S(2)}, u32[]{:S(2)}) async-start(f32[8,2,20,128]{3,1,2,0:T(2,128)} %broadcast_in_dim.76), calls=%async_computation | async-start | bytes 327680 | tf_op jit(solution)/shard_map/all_to_all | solution.py:593
  (14 other events, 20.6 us)

commit v4 on v3

--- a/solution.py
+++ b/solution.py
@@ -15,7 +15,7 @@
 TN = (((0,), (0,)), ((), ()))
 VMEM_BYTES = 32 * 1024 * 1024
 COST_SCALE = 20
-FIRST_VMEM_BYTES = 32 * 1024 * 1024
+FIRST_VMEM_BYTES = 58 * 1024 * 1024
 
 
 def dot(a, b, dims=NN):
@@ -100,36 +100,66 @@
 ANY = pl.BlockSpec(memory_space=pl.ANY)
 
 
-def decay_kernel(x_ref, b_ref, dt_ref, alog_ref, skip_ref, grown_ref, shrunk_ref, skips_ref, total_ref, gathered_ref):
-    heads, length = dt_ref.shape
-    group = x_ref.shape[0] // HEAD_DIM
-
-    @pl.when(pl.program_id(0) == 0)
-    def _():
-        step_size = softplus(dt_ref[...])
-        cumulative = running_sum(step_size * -jnp.exp(as_column(alog_ref[...])))
-        grown = jnp.exp(cumulative)
-        shrunk = step_size * jnp.exp(-cumulative)
-        skips = jnp.broadcast_to(as_column(skip_ref[...]), (heads, length))
-        for h in range(heads):
-            grown_ref[h] = grown[h : h + 1]
-            shrunk_ref[h] = shrunk[h : h + 1]
-            skips_ref[h] = skips[h : h + 1]
-        total_ref[...] = jnp.broadcast_to(cumulative[:, length - 1 :], total_ref.shape)
-
-    shrunk = shrunk_ref[pl.ds(pl.program_id(0) * group, group)]
-    xs = (per_head(x_ref[...].astype(F32), group) * shrunk).reshape(x_ref.shape)
-    high, low = split(xs)
-    gathered_ref[...] = dot(high, b_ref[...]) + dot(low, b_ref[...])
-
-
-def inner_kernel(x_ref, b_ref, c_ref, shrunk_ref, after_ref, inner_ref, high_ref, low_ref):
+def decay_kernel(upper_ref, x_hbm, b_hbm, dt_hbm, alog_hbm, grown_ref, shrunk_ref, total_ref, gathered_ref,
+                 payload_ref, mine_ref, x_ref, b_ref, dt_ref, alog_ref, rows_dt, sems):
+    heads, length = rows_dt.shape
+    group = 4 if heads % 4 == 0 else 1
+    block = group * HEAD_DIM
+    parts = heads // group
+    pieces = [(dt_hbm, dt_ref), (alog_hbm, alog_ref), (b_hbm, b_ref)]
+    for i in range(parts):
+        here = pl.ds(i * block, block)
+        pieces.append((x_hbm.at[here], x_ref.at[here]))
+    copies = [pltpu.make_async_copy(src, dst, sems.at[i]) for i, (src, dst) in enumerate(pieces)]
+    for copy in copies:
+        copy.start()
+    copies[0].wait()
+    copies[1].wait()
+    for h in range(heads):
+        rows_dt[h : h + 1] = dt_ref[h]
+    step_size = softplus(rows_dt[...])
+    cumulative = running_sum(step_size * -jnp.exp(as_column(alog_ref[...])))
+    grown = jnp.exp(cumulative)
+    shrunk = step_size * jnp.exp(-cumulative)
+    for h in range(heads):
+        grown_ref[h] = grown[h : h + 1]
+        shrunk_ref[h] = shrunk[h : h + 1]
+    total = jnp.broadcast_to(cumulative[:, length - 1 :], total_ref.shape)
+    total_ref[...] = total
+    along = lax.broadcasted_iota(jnp.int32, total.shape, 0)
+    across = lax.broadcasted_iota(jnp.int32, total.shape, 1)
+    row = jnp.sum(jnp.where(along == across, total, 0.0), axis=0, keepdims=True)
+    high, low = split(row)
+    middle, low = split(row - high.astype(F32))
+    rows = lax.broadcasted_iota(jnp.int32, payload_ref.shape[1:], 0)
+    terms = jnp.where(rows == 0, high.astype(F32), jnp.where(rows == 1, middle.astype(F32), low.astype(F32)))
+    payload_ref[heads] = jnp.where(rows < 3, terms, 0.0).astype(BF16)
+    upper = upper_ref[0] == 1
+    copies[2].wait()
+    for i in range(parts):
+        copies[3 + i].wait()
+        x = per_head(x_ref[i * block : (i + 1) * block].astype(F32), group)
+        high, low = split((x * shrunk_ref[i * group : (i + 1) * group]).reshape(block, length))
+        gathered = dot(high, b_ref[...]) + dot(low, b_ref[...])
+        gathered_ref[i * block : (i + 1) * block] = gathered
+        for j in range(group):
+            h = i * group + j
+            local = gathered[j * HEAD_DIM : (j + 1) * HEAD_DIM] * jnp.exp(total[h : h + 1])
+            first, second = local[: HEAD_DIM // 2], local[HEAD_DIM // 2 :]
+            mine_ref[h] = jnp.where(upper, second, first)
+            payload_ref[h] = jnp.where(upper, first, second).astype(BF16)
+
+
+def inner_kernel(x_ref, b_ref, c_ref, shrunk_ref, skip_ref, after_ref, inner_ref, skips_ref, high_ref, low_ref):
     group = x_ref.shape[0] // HEAD_DIM
     half = x_ref.shape[1] // 2
 
     @pl.when(pl.program_id(0) == 0)
     def _():
         high_ref[...], low_ref[...] = split(causal_affinity(b_ref[...], c_ref[...]))
+        skips = jnp.broadcast_to(as_column(skip_ref[...]), (skips_ref.shape[0], skips_ref.shape[2]))
+        for h in range(skips_ref.shape[0]):
+            skips_ref[h] = skips[h : h + 1]
 
     xs = split((per_head(x_ref[...].astype(F32), group) * shrunk_ref[...]).reshape(x_ref.shape))
     affinity = (high_ref, low_ref)
@@ -231,10 +261,10 @@
 def last_kernel(x_ref, cotan_ref, outer_ref, ends_ref, gathered_ref, state_ref, shrunk_ref, skips_ref,
                 b_ref, dt_ref, alog_ref, from_y_ref, grad_b_ref, grad_c_ref, after_a_ref, after_b_ref,
                 grad_inputs_ref, grad_dt_ref, small_ref, both_ref,
-                from_x_s, from_end_s, from_skip_s, rows_x, rows_y, rows_skip, rows_end):
+                from_x_s, from_end_s, from_skip_s, rows_x, rows_y, rows_skip, rows_end, rows_dt):
     step = pl.program_id(0)
     group = x_ref.shape[0] // HEAD_DIM
-    heads, length = dt_ref.shape
+    heads, length = rows_x.shape
     n_state = b_ref.shape[1]
     ends = ends_ref[...]
     outer = per_head(outer_ref[...] + dot(ends, b_ref[...], NT), group)
@@ -264,13 +294,16 @@
             rows_y[h : h + 1] = from_y_ref[h]
             rows_skip[h : h + 1] = from_skip_s[h]
             rows_end[h : h + 1] = from_end_s[h]
+            rows_dt[h : h + 1] = dt_ref[h]
         from_x = rows_x[...]
         from_end = jnp.sum(rows_end[...], axis=1, keepdims=True)
         flow = running_sum(rows_y[...] - from_x, reverse=True) + from_end
-        dt = dt_ref[...]
+        dt = rows_dt[...]
         step_size = softplus(dt)
         rate = -jnp.exp(as_column(alog_ref[...]))
-        grad_dt_ref[...] = (from_x / step_size + flow * rate) / (1.0 + jnp.exp(-dt))
+        grad_dt = (from_x / step_size + flow * rate) / (1.0 + jnp.exp(-dt))
+        for h in range(heads):
+            grad_dt_ref[h] = grad_dt[h : h + 1]
         alog = jnp.sum(flow * step_size * rate, axis=1, keepdims=True)
         skip = jnp.sum(rows_skip[...], axis=1, keepdims=True)
         small_ref[0] = jnp.broadcast_to(alog, small_ref.shape[1:])
@@ -306,24 +339,29 @@
     return jnp.exp(total)[:, None, None]
 
 
-def pair_scan(local, total, n_seq, reverse, beside):
-    works = []
-
-    def traveling(payload, got):
-        if len(works) in beside:
-            work = beside[len(works)](payload)
-            got, work = lax.optimization_barrier((got, work))
-            works.append(work)
-        return got
-
+def halves_of(local, total):
     heads, width, lanes = local.shape
-    place = lax.axis_index("seq")
-    upper = lax.rem(place, 2) == 1
-    late = jnp.logical_not(upper) if reverse else upper
+    upper = lax.rem(lax.axis_index("seq"), 2) == 1
     halves = local.reshape(heads, 2, width // 2, lanes)
     mine = jnp.where(upper, halves[:, 1], halves[:, 0])
     theirs = jnp.where(upper, halves[:, 0], halves[:, 1])
-    payload = pack(theirs, total)
+    return pack(theirs, total), mine
+
+
+def pair_scan(payload, mine, total, n_seq, reverse, beside):
+    heads, half_width, lanes = mine.shape
+    upper = lax.rem(lax.axis_index("seq"), 2) == 1
+    late = jnp.logical_not(upper) if reverse else upper
+    works, taken = [], []
+
+    def traveling(payload, got):
+        if len(taken) in beside:
+            work = beside[len(taken)](payload)
+            got, work = lax.optimization_barrier((got, work))
+            works.append(work)
+        taken.append(payload)
+        return got
+
     other, other_total = unpack(traveling(payload, swap(payload, "seq", n_seq, 1)))
     first = jnp.where(late, other, mine)
     second = jnp.where(late, mine, other)
@@ -352,7 +390,7 @@
     got = swap(give, "seq", n_seq, 1)
     low = jnp.where(upper, got, keep)
     high = jnp.where(upper, keep, got)
-    result = jnp.concatenate([low[:, None], high[:, None]], axis=1).reshape(heads * width, lanes)
+    result = jnp.concatenate([low[:, None], high[:, None]], axis=1).reshape(heads * 2 * half_width, lanes)
     return works, result, give
 
 
@@ -368,7 +406,7 @@
     group = 4 if heads % 4 == 0 else 1
     block = group * HEAD_DIM
     grid = (heads // group,)
-    alog2, skip2 = a_log[None], d_skip[None]
+    alog2, skip2, dt3 = a_log[None], d_skip[None], dt[:, None]
 
     if n_tensor == 2:
         g_first, half_index = g, my_tensor
@@ -378,28 +416,40 @@
         g_first, g_second, half_index = g_all[: features // 2], g_all[features // 2 :], 0
 
     long = jax.ShapeDtypeStruct((heads, 1, length), F32)
-    grown, shrunk, skips, totals, gathered = call(
+    upper = lax.rem(my_seq, 2).astype(jnp.int32).reshape(1)
+    half_state = (HEAD_DIM // 2, n_state)
+    grown, shrunk, totals, gathered, payload, mine = call(
         decay_kernel,
-        grid,
-        [by_row(block, length), whole(length, n_state), whole(heads, length), whole(1, heads), whole(1, heads)],
-        [whole(heads, 1, length)] * 3 + [whole(heads, 128), by_row(block, n_state)],
-        [long] * 3
-        + [jax.ShapeDtypeStruct((heads, 128), F32), jax.ShapeDtypeStruct((channels, n_state), F32)],
+        (1,),
+        [ANY] * 4,
+        [whole(heads, 1, length)] * 2
+        + [whole(heads, 128), whole(channels, n_state), whole(heads + 1, *half_state), whole(heads, *half_state)],
+        [long] * 2
+        + [jax.ShapeDtypeStruct((heads, 128), F32), jax.ShapeDtypeStruct((channels, n_state), F32)]
+        + [jax.ShapeDtypeStruct((heads + 1, *half_state), BF16), jax.ShapeDtypeStruct((heads, *half_state), F32)],
+        [
+            pltpu.VMEM((channels, length), BF16),
+            pltpu.VMEM((length, n_state), BF16),
+            pltpu.VMEM((heads, 1, length), F32),
+            pltpu.VMEM((1, heads), F32),
+            pltpu.VMEM((heads, length), F32),
+            pltpu.SemaphoreType.DMA((3 + heads // group,)),
+        ],
         flops=4 * channels * length * n_state,
         vmem=FIRST_VMEM_BYTES,
-    )(x, b, dt, alog2, skip2)
+        prefetch=1,
+    )(upper, x, b, dt3, alog2)
     total = totals[:, 0]
-    local_state = decay(total) * gathered.reshape(heads, HEAD_DIM, n_state)
 
     inners = lambda after: call(
         inner_kernel,
         grid,
-        [by_row(block, length), whole(length, n_state), whole(length, n_state), by_row(group, 1, length), ANY],
-        by_row(block, length),
-        jax.ShapeDtypeStruct((channels, length), F32),
+        [by_row(block, length), whole(length, n_state), whole(length, n_state), by_row(group, 1, length), whole(1, heads), ANY],
+        [by_row(block, length), whole(heads, 1, length)],
+        [jax.ShapeDtypeStruct((channels, length), F32), long],
         [pltpu.VMEM((length, length), BF16)] * 2,
         flops=5 * channels * length * length,
-    )(x, b, c, shrunk, after)
+    )(x, b, c, shrunk, skip2, after)
 
     w_other = swap(w_out, "dp", 2, 1)
     flag = (my_dp == half_index).astype(jnp.int32).reshape(1)
@@ -434,11 +484,10 @@
         prefetch=1,
     )(flag, w_out, w_other, g_second, first, c, grown, after)
 
-    beside = {0: inners, 1: first}
-    (inner, first_sum), state_in, give = pair_scan(local_state, total, n_seq, False, beside)
-    if n_tensor == 2:
-        g_second, give = lax.optimization_barrier((g_second, give))
-    y_cotan, local_cotan = cotans(g_second, first_sum, give)
+    beside = {1: first}
+    (first_sum,), state_in, give = pair_scan(payload, mine, total, n_seq, False, beside)
+
+    inner, skips = inners(give)
 
     def mix(after):
         return call(
@@ -452,15 +501,6 @@
             flops=2 * channels * length * n_state,
         )(inner, state_in, c, x, grown, skips, after)
 
-    firsts = g_first.reshape(n_seq // 2, n_dp, out_columns, length)
-    seconds = g_second.reshape(n_seq // 2, n_dp, out_columns, length)
-
-    def chosen(place):
-        pick = lambda blocks: lax.dynamic_index_in_dim(blocks, place, 1, keepdims=False)
-        return jnp.concatenate([pick(firsts), pick(seconds)])
-
-    g_mine = chosen(my_dp)
-    g_other = swap(chosen(1 - my_dp), "dp", 2, 1)
     n_bits = n_seq.bit_length() - 1
     half = channels // 2
 
@@ -492,10 +532,20 @@
     orders = [list(range(n_bits)), [1, 0] + list(range(2, n_bits))]
     held = {}
 
-    def traded(after):
-        mixed = mix(after)
-        held["mixed"] = mixed, swap(mixed, "dp", 2, 1)
-        return mixed
+    mixed = mix(give)
+    held["mixed"] = mixed, swap(mixed, "dp", 2, 1)
+    if n_tensor == 2:
+        g_second, _ = lax.optimization_barrier((g_second, mixed))
+    firsts = g_first.reshape(n_seq // 2, n_dp, out_columns, length)
+    seconds = g_second.reshape(n_seq // 2, n_dp, out_columns, length)
+
+    def chosen(place):
+        pick = lambda blocks: lax.dynamic_index_in_dim(blocks, place, 1, keepdims=False)
+        return jnp.concatenate([pick(firsts), pick(seconds)])
+
+    g_mine = chosen(my_dp)
+    g_other = swap(chosen(1 - my_dp), "dp", 2, 1)
+    y_cotan, local_cotan = cotans(g_second, first_sum, mixed)
 
     def sending(after):
         held["sends"] = [
@@ -527,11 +577,10 @@
         flops=10 * channels * length * length,
     )(x, y_cotan, inner, state_in, b, c, grown, shrunk, after)
     works, cotan_end, _ = pair_scan(
-        local_cotan.reshape(heads, HEAD_DIM, n_state), total, n_seq, True,
-        {0: traded, 1: sending, 2: keeping},
+        *halves_of(local_cotan.reshape(heads, HEAD_DIM, n_state), total), total, n_seq, True,
+        {1: sending, 2: keeping},
     )
-    mixed = held["mixed"][0]
-    keeps, (outer, from_y, grad_b, grad_c), gots = works[2]
+    keeps, (outer, from_y, grad_b, grad_c), gots = works[-1]
 
     def halve(sums, left):
         axis = sorted(left, reverse=True).index(left[0])
@@ -549,18 +598,18 @@
         [by_row(block, length)] * 3
         + [by_row(block, n_state)] * 3
         + [by_row(group, 1, length)] * 2
-        + [whole(length, n_state), whole(heads, length), whole(1, heads), whole(heads, 1, length)]
+        + [whole(length, n_state), whole(heads, 1, length), whole(1, heads), whole(heads, 1, length)]
         + [whole(length, n_state)] * 2
         + [ANY] * 2,
         [
             by_row(block, length),
-            whole(heads, length),
+            whole(heads, 1, length),
             whole(2, heads, 128),
             whole(length, 2 * n_state),
         ],
         [
             jax.ShapeDtypeStruct((channels, length), BF16),
-            jax.ShapeDtypeStruct((heads, length), F32),
+            long,
             jax.ShapeDtypeStruct((2, heads, 128), F32),
             jax.ShapeDtypeStruct((length, 2 * n_state), F32),
         ],
@@ -572,11 +621,12 @@
             pltpu.VMEM((heads, length), F32),
             pltpu.VMEM((heads, length), F32),
             pltpu.VMEM((heads, n_state), F32),
+            pltpu.VMEM((heads, length), F32),
         ],
         flops=6 * channels * length * n_state,
     )(
         x, y_cotan, outer, cotan_end, gathered, state_in, shrunk, skips,
-        b, dt, alog2, from_y, grad_b, grad_c, streams[0][1], streams[1][1],
+        b, dt3, alog2, from_y, grad_b, grad_c, streams[0][1], streams[1][1],
     )
     if n_tensor == 2:
         both_other = swap(both, "tensor", 2, 1)
@@ -585,26 +635,23 @@
         gots = [swap(streams[s][1], "seq", n_seq, 1 << orders[s][done]) for s in (0, 1)]
         if done == 1:
             gots, both, small = lax.optimization_barrier((gots, both, small))
+        if done + 1 == n_bits:
+            small = lax.all_to_all(jnp.broadcast_to(small, (n_seq,) + small.shape), "seq", 0, 0)
+            both = (both + both_other if n_tensor == 2 else lax.psum(both, "tensor")).astype(BF16)
+            gots, both = lax.optimization_barrier((gots, both))
         pairs = [streams[s][0] + gots[s].astype(F32) for s in (0, 1)]
         if done + 1 < n_bits:
             streams = [halve(pairs[s], orders[s][done + 1 :]) for s in (0, 1)]
             if done + 2 == n_bits:
                 small, _ = lax.optimization_barrier((small, [stream[1] for stream in streams]))
-    small = lax.all_to_all(jnp.broadcast_to(small, (n_seq,) + small.shape), "seq", 0, 0)
     small = jnp.sum(small[:, :, :, 0], axis=0)
-    if n_tensor == 2:
-        both_other, small = lax.optimization_barrier((both_other, small))
-        both = both + both_other
-    else:
-        both = lax.psum(both, "tensor")
-    both = both.astype(BF16)
     grad_w = jnp.concatenate(pairs, axis=1).T.astype(BF16)
     return (
         mixed[None],
         grad_inputs[None],
         both[None, :, :n_state],
         both[None, :, n_state:],
-        grad_dt[None],
+        grad_dt[:, 0][None],
         small[0],
         small[1],
         grad_w,

time: 127 us -> 126 us (level)
  local copies, waits for them, and re-layouts: 14.1 us -> 5.87 us
  starting transfers between devices: 34.9 us -> 41.1 us
  other arithmetic: 7.95 us -> 5.62 us
  Pallas kernels: 32.5 us -> 34.4 us
  waiting for transfers between devices: 35.5 us -> 36.8 us
    unnamed x52 -> x38, local copies, waits for them, and re-layouts: 11.4 us -> 1.78 us
    ppermute x16, starting transfers between devices: 18.8 us -> 24.7 us  [swap(): return lax.ppermute(value, axis, [(i, i ^ bit) for i in range(size)])]
    ppermute x16, waiting for transfers between devices: 31.7 us -> 33.7 us  [swap(): return lax.ppermute(value, axis, [(i, i ^ bit) for i in range(size)])]
    pallas_call x1, Pallas kernels: 2.27 us -> 4.19 us  [per_device(): call(decay_kernel, (1,), [ANY] * 4, [whole(heads, 1, length)] * 2 + [whol...]
  transfers between devices with their start and end apart: 21 -> 21, of which waited for: 11 -> 10; matrix products, arithmetic and copies ran while one was open for 7% -> 7% of each run, Pallas kernels for 24% -> 28%
where the time goes in v4:
time: 126 us; the launch traced here: 125 us
  starting transfers between devices  41.1 us (33%)
  waiting for transfers between devices  36.8 us (29%)
  Pallas kernels  34.4 us (27%)
  local copies, waits for them, and re-layouts  5.87 us (5%)
  other arithmetic  5.62 us (4%)
  between operations  1.3 us (1%)
    ppermute x16, waiting for transfers between devices, swap(): return lax.ppermute(value, axis, [(i, i ^ bit) for i in range(size)])  33.7 us
    ppermute x16, starting transfers between devices, swap(): return lax.ppermute(value, axis, [(i, i ^ bit) for i in range(size)])  24.7 us
    ppermute x4, starting transfers between devices, shifted(): return lax.ppermute(value, axis, pairs)  11.7 us
    pallas_call x1, Pallas kernels, per_device(): call(back_kernel, grid, [by_row(block, length)] * 3 + [by_row(block, n_st...  6.47 us
    pallas_call x1, Pallas kernels, per_device(): call(last_kernel, grid, [by_row(block, length)] * 3 + [by_row(block, n_st...  5.23 us
    pallas_call x4, Pallas kernels, terms(): call(terms_kernel, (1,), [columns, columns, rows, rows, ANY], whole(n_seq...  4.83 us
    all_to_all x1, starting transfers between devices, per_device(): lax.all_to_all(jnp.broadcast_to(small, (n_seq,) + small.shape), 'seq', 0, 0)  4.63 us
    pallas_call x1, Pallas kernels, per_device(): call(cotan_kernel, wide_grid, [weights(0), weights(1)] + [whole(half_feat...  4.54 us
  transfers between devices with their start and end apart: 21, of which 10 were waited for; matrix products, arithmetic and copies ran while one was open for 7% of the time, Pallas kernels for 28%

profile of v4, /device:TPU:0, one launch (start us, length us, event | category | flops | bytes accessed | tf_op | source)
XLA Modules:
  0.0 125.1 jit_solution(7678226315986235700)
XLA Ops:
  1.2 4.2 %shard_map.143 = (f32[20,1,512]{2,1,0:T(1,128)}, f32[20,1,512]{2,1,0:T(1,128)}, f32[20,128]{1,0:T(8,128)}, f32[1280,128]{1,0:T(8,128)}, bf16[21,32,128]{2,1,0:T(8,128)(2,1)}, /*index=5*/f32[20,32,128]{2,1,0:T(8,128)}) custom-call(s32[1]{0:T(128)} %bitcast.3.upper_ref, bf16[1280,512]{1,0:T(8,128)(2,1)} %bitcast.194, bf16[512,128]{1,0:T(8,128)(2,1)} %bitcast.208, ...), custom_call_target="tpu_custom_call" | custom-call | flops 6710886400 | bytes 80000000 | tf_op jit(solution)/shard_map/pallas_call | solution.py:421
  5.4 2.6 %collective-permute-start = (bf16[21,32,128]{2,1,0:T(8,128)(2,1)}, bf16[21,32,128]{2,1,0:T(8,128)(2,1)S(1)}, u32[]{:S(2)}, u32[]{:S(2)}) collective-permute-start(bf16[21,32,128]{2,1,0:T(8,128)(2,1)} %get-tuple-element.49), channel_id=1, source_target_pairs={{0,4},{4,0},{8,12},{12,8},{16,20},{20,16},{24,28},{28,24},{1,5},{5... | collective-permute-start | bytes 516104 | tf_op jit(solution)/shard_map/ppermute | solution.py:314
  8.0 1.5 %collective-permute-start.5 = (bf16[1280,512]{1,0:T(8,128)(2,1)S(1)}, bf16[1280,512]{1,0:T(8,128)(2,1)S(1)}, u32[]{:S(2)}, u32[]{:S(2)}) collective-permute-start(bf16[1280,512]{1,0:T(8,128)(2,1)S(1)} %bitcast.182), channel_id=1, source_target_pairs={{0,1},{1,0},{2,3},{3,2},{4,5},{5,4},{6,7},{7,6},{8,9},{9,8},{10,11... | collective-permute-start | bytes 3932168 | tf_op jit(solution)/shard_map/ppermute | solution.py:314
  10.4 2.8 %collective-permute-done = bf16[21,32,128]{2,1,0:T(8,128)(2,1)S(1)} collective-permute-done((bf16[21,32,128]{2,1,0:T(8,128)(2,1)}, bf16[21,32,128]{2,1,0:T(8,128)(2,1)S(1)}, u32[]{:S(2)}, u32[]{:S(2)}) %collective-permute-start) | collective-permute-done | bytes 172064 | tf_op jit(solution)/shard_map/ppermute | solution.py:314
  13.4 3.7 %collective-permute-start.1 = (bf16[21,32,128]{2,1,0:T(8,128)(2,1)S(1)}, bf16[21,32,128]{2,1,0:T(8,128)(2,1)S(1)}, u32[]{:S(2)}, u32[]{:S(2)}) collective-permute-start(bf16[21,32,128]{2,1,0:T(8,128)(2,1)S(1)} %pad_maximum_fusion.4.after_ref), channel_id=1, source_target_pairs={{0,8},{4,12},{8,16},{12,20},{16,24},{20,28},{1,9},{5,13},{9,17},{1... | collective-permute-start | bytes 516104 | tf_op jit(solution)/shard_map/ppermute | solution.py:319
  17.2 3.5 %shard_map.144.first_ref = f32[1280,512]{1,0:T(8,128)S(1)} custom-call(s32[1]{0:T(128)} %bitcast.10.flag_ref, bf16[1280,1280]{1,0:T(8,128)(2,1)S(1)} %copy-done.1, bf16[1280,1280]{1,0:T(8,128)(2,1)} %collective-permute-done.2.other_ref, bf16[1280,512]{1,0:T(8,128)(2,1)S(1)} %bitcast.184, bf16[21,32,128]{2,1,0:T(8,128)(2,1)S(1)} %pad_maximum_fusion.4.after_ref), custom_call_target="tpu_custom_call" | custom-call | flops 33554432000 | bytes 80000000 | tf_op jit(solution)/shard_map/pallas_call | solution.py:466
  21.0 5.2 %collective-permute-start.3 = (bf16[21,32,128]{2,1,0:T(8,128)(2,1)S(1)}, bf16[21,32,128]{2,1,0:T(8,128)(2,1)S(1)}, u32[]{:S(2)}, u32[]{:S(2)}) collective-permute-start(bf16[21,32,128]{2,1,0:T(8,128)(2,1)S(1)} %pad_maximum_fusion.5), channel_id=1, source_target_pairs={{0,16},{4,20},{8,24},{12,28},{1,17},{5,21},{9,25},{13,29},{2,18},{... | collective-permute-start | bytes 516104 | tf_op jit(solution)/shard_map/ppermute | solution.py:319
  26.3 2.9 %collective-permute-done.3 = bf16[21,32,128]{2,1,0:T(8,128)(2,1)S(1)} collective-permute-done((bf16[21,32,128]{2,1,0:T(8,128)(2,1)S(1)}, bf16[21,32,128]{2,1,0:T(8,128)(2,1)S(1)}, u32[]{:S(2)}, u32[]{:S(2)}) %collective-permute-start.3) | collective-permute-done | bytes 172064 | tf_op jit(solution)/shard_map/ppermute | solution.py:319
  29.3 1.6 %collective-permute-start.4 = (bf16[20,32,128]{2,1,0:T(8,128)(2,1)S(1)}, bf16[20,32,128]{2,1,0:T(8,128)(2,1)S(1)}, u32[]{:S(2)}, u32[]{:S(2)}) collective-permute-start(bf16[20,32,128]{2,1,0:T(8,128)(2,1)S(1)} %select_convert_fusion.4.after_ref), channel_id=1, source_target_pairs={{0,4},{4,0},{8,12},{12,8},{16,20},{20,16},{24,28},{28,24},{1,5},{5... | collective-permute-start | bytes 491528 | tf_op jit(solution)/shard_map/ppermute | solution.py:314
  30.9 2.8 %shard_map.145 = (f32[1280,512]{1,0:T(8,128)S(1)}, f32[20,1,512]{2,1,0:T(1,128)S(1)}) custom-call(bf16[1280,512]{1,0:T(8,128)(2,1)S(1)} %bitcast.195, bf16[512,128]{1,0:T(8,128)(2,1)S(1)} %bitcast.209, bf16[512,128]{1,0:T(8,128)(2,1)S(1)} %bitcast.204, f32[20,1,512]{2,1,0:T(1,128)S(1)} %copy-done.13, f32[1,20]{1,0:T(1,128)S(1)} %bitcast.214, ...), custom_call_target="tpu_custom_call" | custom-call | flops 33554432000 | bytes 80000000 | tf_op jit(solution)/shard_map/pallas_call | solution.py:444
  35.1 2.8 %shard_map.146.after_ref.m0_ref = bf16[1280,512]{1,0:T(8,128)(2,1)} custom-call(f32[1280,512]{1,0:T(8,128)S(1)} %get-tuple-element.52.inner_ref, bf16[1280,128]{1,0:T(8,128)(2,1)S(1)} %bitcast.190, bf16[512,128]{1,0:T(8,128)(2,1)S(1)} %bitcast.205, bf16[1280,512]{1,0:T(8,128)(2,1)S(1)} %bitcast.196, f32[20,1,512]{2,1,0:T(1,128)S(1)} %copy-done.10, ...), custom_call_target="tpu_custom_call" | custom-call | flops 3355443200 | bytes 80000000 | tf_op jit(solution)/shard_map/pallas_call | solution.py:493
  38.8 1.3 %copy-done.3 = bf16[1280,512]{1,0:T(8,128)(2,1)S(1)} copy-done((bf16[1280,512]{1,0:T(8,128)(2,1)S(1)}, bf16[1280,512]{1,0:T(8,128)(2,1)}, u32[]{:S(2)}) %copy-start.3) | copy-done | bytes 1310744
  40.2 4.5 %shard_map.147 = (bf16[1280,512]{1,0:T(8,128)(2,1)S(1)}, f32[1280,128]{1,0:T(8,128)S(1)}) custom-call(s32[1]{0:T(128)} %bitcast.10.flag_ref, bf16[1280,1280]{1,0:T(8,128)(2,1)S(1)} %copy-done.1, bf16[1280,1280]{1,0:T(8,128)(2,1)} %collective-permute-done.2.other_ref, bf16[1280,512]{1,0:T(8,128)(2,1)S(1)} %collective-permute-done.5.g_ref, ...), custom_call_target="tpu_custom_call" | custom-call | flops 40265318400 | bytes 80000000 | tf_op jit(solution)/shard_map/pallas_call | solution.py:475
  46.1 4.6 %collective-permute-done.6 = bf16[21,32,128]{2,1,0:T(8,128)(2,1)S(1)} collective-permute-done((bf16[21,32,128]{2,1,0:T(8,128)(2,1)S(1)}, bf16[21,32,128]{2,1,0:T(8,128)(2,1)S(1)}, u32[]{:S(2)}, u32[]{:S(2)}) %collective-permute-start.6) | collective-permute-done | bytes 172064 | tf_op jit(solution)/shard_map/ppermute | solution.py:314
  50.9 1.3 %collective-permute-start.7 = (bf16[21,32,128]{2,1,0:T(8,128)(2,1)S(1)}, bf16[21,32,128]{2,1,0:T(8,128)(2,1)S(1)}, u32[]{:S(2)}, u32[]{:S(2)}) collective-permute-start(bf16[21,32,128]{2,1,0:T(8,128)(2,1)S(1)} %pad_maximum_fusion.7.after_ref), channel_id=1, source_target_pairs={{8,0},{12,4},{16,8},{20,12},{24,16},{28,20},{9,1},{13,5},{17,9},{2... | collective-permute-start | bytes 516104 | tf_op jit(solution)/shard_map/ppermute | solution.py:319
  52.2 1.2 shard_map.148
  53.4 1.6 %collective-permute-start.11 = (bf16[4,160,640]{2,1,0:T(8,128)(2,1)S(1)}, bf16[4,160,640]{2,1,0:T(8,128)(2,1)S(1)}, u32[]{:S(2)}, u32[]{:S(2)}) collective-permute-start(bf16[4,160,640]{2,1,0:T(8,128)(2,1)S(1)} %shard_map.148), channel_id=1, source_target_pairs={{0,4},{4,0},{8,12},{12,8},{16,20},{20,16},{24,28},{28,24},{1,5},{5... | collective-permute-start | bytes 2457608 | tf_op jit(solution)/shard_map/ppermute | solution.py:314
  56.2 6.3 %collective-permute-start.12 = (bf16[4,160,640]{2,1,0:T(8,128)(2,1)S(1)}, bf16[4,160,640]{2,1,0:T(8,128)(2,1)S(1)}, u32[]{:S(2)}, u32[]{:S(2)}) collective-permute-start(bf16[4,160,640]{2,1,0:T(8,128)(2,1)S(1)} %shard_map.149), channel_id=1, source_target_pairs={{0,8},{4,12},{8,0},{12,4},{16,24},{20,28},{24,16},{28,20},{1,9},{5... | collective-permute-start | bytes 2457608 | tf_op jit(solution)/shard_map/ppermute | solution.py:314
  62.9 1.5 %collective-permute-start.10 = (bf16[21,32,128]{2,1,0:T(8,128)(2,1)S(1)}, bf16[21,32,128]{2,1,0:T(8,128)(2,1)S(1)}, u32[]{:S(2)}, u32[]{:S(2)}) collective-permute-start(bf16[21,32,128]{2,1,0:T(8,128)(2,1)S(1)} %pad_maximum_fusion.8.after_ref), channel_id=1, source_target_pairs={{16,0},{20,4},{24,8},{28,12},{17,1},{21,5},{25,9},{29,13},{18,2},{... | collective-permute-start | bytes 516104 | tf_op jit(solution)/shard_map/ppermute | solution.py:319
  64.4 6.5 %shard_map.152 = (f32[1280,512]{1,0:T(8,128)S(1)}, f32[20,1,512]{2,1,0:T(1,128)S(1)}, f32[512,128]{1,0:T(8,128)S(1)}, f32[512,128]{1,0:T(8,128)S(1)}) custom-call(bf16[1280,512]{1,0:T(8,128)(2,1)S(1)} %bitcast.197, bf16[1280,512]{1,0:T(8,128)(2,1)S(1)} %get-tuple-element.57.cotan_ref, f32[1280,512]{1,0:T(8,128)S(1)} %get-tuple-element.52.inner_ref, ...), custom_call_target="tpu_custom_call" | custom-call | flops 67108864000 | bytes 80000000 | tf_op jit(solution)/shard_map/pallas_call | solution.py:567
  70.9 1.2 shard_map.150
  72.1 1.2 shard_map.151
  73.3 10.7 %collective-permute-done.12 = bf16[4,160,640]{2,1,0:T(8,128)(2,1)S(1)} collective-permute-done((bf16[4,160,640]{2,1,0:T(8,128)(2,1)S(1)}, bf16[4,160,640]{2,1,0:T(8,128)(2,1)S(1)}, u32[]{:S(2)}, u32[]{:S(2)}) %collective-permute-start.12) | collective-permute-done | bytes 819232 | tf_op jit(solution)/shard_map/ppermute | solution.py:314
  84.3 1.4 %collective-permute-start.13 = (bf16[20,32,128]{2,1,0:T(8,128)(2,1)S(1)}, bf16[20,32,128]{2,1,0:T(8,128)(2,1)S(1)}, u32[]{:S(2)}, u32[]{:S(2)}) collective-permute-start(bf16[20,32,128]{2,1,0:T(8,128)(2,1)S(1)} %select_convert_fusion.1), channel_id=1, source_target_pairs={{0,4},{4,0},{8,12},{12,8},{16,20},{20,16},{24,28},{28,24},{1,5},{5... | collective-permute-start | bytes 491528 | tf_op jit(solution)/shard_map/ppermute | solution.py:314
  86.0 2.8 %collective-permute-start.14 = (bf16[2,160,640]{2,1,0:T(8,128)(2,1)S(1)}, bf16[2,160,640]{2,1,0:T(8,128)(2,1)}, u32[]{:S(2)}, u32[]{:S(2)}) collective-permute-start(bf16[2,160,640]{2,1,0:T(8,128)(2,1)S(1)} %fusion.after_a_ref), channel_id=1, source_target_pairs={{0,8},{4,12},{8,0},{12,4},{16,24},{20,28},{24,16},{28,20},{1,9},{5... | collective-permute-start | bytes 1228808 | tf_op jit(solution)/shard_map/ppermute | solution.py:314
  90.7 5.2 %shard_map.153 = (bf16[1280,512]{1,0:T(8,128)(2,1)}, f32[20,1,512]{2,1,0:T(1,128)}, f32[2,20,128]{2,1,0:T(8,128)S(1)}, f32[512,256]{1,0:T(8,128)S(1)}) custom-call(bf16[1280,512]{1,0:T(8,128)(2,1)S(1)} %bitcast.198, bf16[1280,512]{1,0:T(8,128)(2,1)S(1)} %get-tuple-element.57.cotan_ref, f32[1280,512]{1,0:T(8,128)S(1)} %get-tuple-element.64.outer_ref, ...), custom_call_target="tpu_custom_call" | custom-call | flops 10066329600 | bytes 80000000 | tf_op jit(solution)/shard_map/pallas_call | solution.py:595
  95.9 1.6 %collective-permute-start.19 = (f32[512,256]{1,0:T(8,128)S(1)}, f32[512,256]{1,0:T(8,128)S(1)}, u32[]{:S(2)}, u32[]{:S(2)}) collective-permute-start(f32[512,256]{1,0:T(8,128)S(1)} %get-tuple-element.79), channel_id=1, source_target_pairs={{0,1},{1,0},{2,3},{3,2},{4,5},{5,4},{6,7},{7,6},{8,9},{9,8},{10,11... | collective-permute-start | bytes 1572872 | tf_op jit(solution)/shard_map/ppermute | solution.py:314
  97.6 1.4 %collective-permute-done.15 = bf16[2,160,640]{2,1,0:T(8,128)(2,1)} collective-permute-done((bf16[2,160,640]{2,1,0:T(8,128)(2,1)S(1)}, bf16[2,160,640]{2,1,0:T(8,128)(2,1)}, u32[]{:S(2)}, u32[]{:S(2)}) %collective-permute-start.15) | collective-permute-done | bytes 409632 | tf_op jit(solution)/shard_map/ppermute | solution.py:314
  102.6 2.3 %collective-permute-start.18 = (bf16[160,640]{1,0:T(8,128)(2,1)}, bf16[160,640]{1,0:T(8,128)(2,1)S(1)}, u32[]{:S(2)}, u32[]{:S(2)}) collective-permute-start(bf16[160,640]{1,0:T(8,128)(2,1)} %fusion.13), channel_id=1, source_target_pairs={{0,16},{4,20},{8,24},{12,28},{16,0},{20,4},{24,8},{28,12},{1,17},{... | collective-permute-start | bytes 614408 | tf_op jit(solution)/shard_map/ppermute | solution.py:314
  105.6 4.6 %all-to-all-start = ((f32[8,2,20,128]{3,1,2,0:T(2,128)}), f32[8,2,20,128]{3,1,2,0:T(2,128)S(1)}, u32[]{:S(2)}, u32[]{:S(2)}) async-start(f32[8,2,20,128]{3,1,2,0:T(2,128)} %broadcast_in_dim.73), calls=%async_computation | async-start | bytes 327680 | tf_op jit(solution)/shard_map/all_to_all | solution.py:639
  110.4 8.0 %collective-permute-done.17 = bf16[160,640]{1,0:T(8,128)(2,1)S(1)} collective-permute-done((bf16[160,640]{1,0:T(8,128)(2,1)S(1)}, bf16[160,640]{1,0:T(8,128)(2,1)S(1)}, u32[]{:S(2)}, u32[]{:S(2)}) %collective-permute-start.17) | collective-permute-done | bytes 204832 | tf_op jit(solution)/shard_map/ppermute | solution.py:314
  118.4 4.3 %collective-permute-done.18 = bf16[160,640]{1,0:T(8,128)(2,1)S(1)} collective-permute-done((bf16[160,640]{1,0:T(8,128)(2,1)}, bf16[160,640]{1,0:T(8,128)(2,1)S(1)}, u32[]{:S(2)}, u32[]{:S(2)}) %collective-permute-start.18) | collective-permute-done | bytes 204832 | tf_op jit(solution)/shard_map/ppermute | solution.py:314
  (123 shorter events, 16.5 us)
Async XLA Ops:
  0.6 16.5 %collective-permute-start.2 = (bf16[1280,1280]{1,0:T(8,128)(2,1)}, bf16[1280,1280]{1,0:T(8,128)(2,1)}, u32[]{:S(2)}, u32[]{:S(2)}) collective-permute-start(bf16[1280,1280]{1,0:T(8,128)(2,1)} %mine_ref.3), channel_id=1, source_target_pairs={{0,2},{2,0},{1,3},{3,1},{4,6},{6,4},{5,7},{7,5},{8,10},{10,8},{9,1... | collective-permute-start | bytes 9830408 | tf_op jit(solution)/shard_map/ppermute | solution.py:314
  1.2 6.8 %copy-start = (bf16[1,1280,512]{2,1,0:T(8,128)(2,1)S(1)}, bf16[1,1280,512]{2,1,0:T(8,128)(2,1)}, u32[]{:S(2)}) copy-start(bf16[1,1280,512]{2,1,0:T(8,128)(2,1)} %param.15) | copy-start | bytes 3932164
  5.4 7.9 %copy-start.14 = (f32[20,32,128]{2,1,0:T(8,128)S(1)}, f32[20,32,128]{2,1,0:T(8,128)}, u32[]{:S(2)}) copy-start(f32[20,32,128]{2,1,0:T(8,128)} %get-tuple-element.50) | copy-start | bytes 983044
  5.4 7.8 %collective-permute-start = (bf16[21,32,128]{2,1,0:T(8,128)(2,1)}, bf16[21,32,128]{2,1,0:T(8,128)(2,1)S(1)}, u32[]{:S(2)}, u32[]{:S(2)}) collective-permute-start(bf16[21,32,128]{2,1,0:T(8,128)(2,1)} %get-tuple-element.49), channel_id=1, source_target_pairs={{0,4},{4,0},{8,12},{12,8},{16,20},{20,16},{24,28},{28,24},{1,5},{5... | collective-permute-start | bytes 516104 | tf_op jit(solution)/shard_map/ppermute | solution.py:314
  8.0 30.9 %collective-permute-start.5 = (bf16[1280,512]{1,0:T(8,128)(2,1)S(1)}, bf16[1280,512]{1,0:T(8,128)(2,1)S(1)}, u32[]{:S(2)}, u32[]{:S(2)}) collective-permute-start(bf16[1280,512]{1,0:T(8,128)(2,1)S(1)} %bitcast.182), channel_id=1, source_target_pairs={{0,1},{1,0},{2,3},{3,2},{4,5},{5,4},{6,7},{7,6},{8,9},{9,8},{10,11... | collective-permute-start | bytes 3932168 | tf_op jit(solution)/shard_map/ppermute | solution.py:314
  10.3 6.9 %copy-start.1 = (bf16[1280,1280]{1,0:T(8,128)(2,1)S(1)}, bf16[1280,1280]{1,0:T(8,128)(2,1)}, u32[]{:S(2)}) copy-start(bf16[1280,1280]{1,0:T(8,128)(2,1)} %mine_ref.3) | copy-start | bytes 9830404
  13.4 7.4 %collective-permute-start.1 = (bf16[21,32,128]{2,1,0:T(8,128)(2,1)S(1)}, bf16[21,32,128]{2,1,0:T(8,128)(2,1)S(1)}, u32[]{:S(2)}, u32[]{:S(2)}) collective-permute-start(bf16[21,32,128]{2,1,0:T(8,128)(2,1)S(1)} %pad_maximum_fusion.4.after_ref), channel_id=1, source_target_pairs={{0,8},{4,12},{8,16},{12,20},{16,24},{20,28},{1,9},{5,13},{9,17},{1... | collective-permute-start | bytes 516104 | tf_op jit(solution)/shard_map/ppermute | solution.py:319
  20.7 10.2 %copy-start.2 = (bf16[1,1280,512]{2,1,0:T(8,128)(2,1)S(1)}, bf16[1,1280,512]{2,1,0:T(8,128)(2,1)}, u32[]{:S(2)}) copy-start(bf16[1,1280,512]{2,1,0:T(8,128)(2,1)} %param.8) | copy-start | bytes 3932164
  20.7 10.2 %copy-start.4 = (bf16[1,512,128]{2,1,0:T(8,128)(2,1)S(1)}, bf16[1,512,128]{2,1,0:T(8,128)(2,1)}, u32[]{:S(2)}) copy-start(bf16[1,512,128]{2,1,0:T(8,128)(2,1)} %param.10) | copy-start | bytes 393220
  20.7 10.2 %copy-start.5 = (bf16[1,512,128]{2,1,0:T(8,128)(2,1)S(1)}, bf16[1,512,128]{2,1,0:T(8,128)(2,1)}, u32[]{:S(2)}) copy-start(bf16[1,512,128]{2,1,0:T(8,128)(2,1)} %param.9) | copy-start | bytes 393220
  20.7 10.2 %copy-start.7 = (f32[20]{0:T(128)S(1)}, f32[20]{0:T(128)}, u32[]{:S(2)}) copy-start(f32[20]{0:T(128)} %param.13) | copy-start | bytes 244
  20.8 10.2 %copy-start.13 = (f32[20,1,512]{2,1,0:T(1,128)S(1)}, f32[20,1,512]{2,1,0:T(1,128)}, u32[]{:S(2)}) copy-start(f32[20,1,512]{2,1,0:T(1,128)} %get-tuple-element.47.shrunk_ref) | copy-start | bytes 122884
  21.0 8.1 %collective-permute-start.3 = (bf16[21,32,128]{2,1,0:T(8,128)(2,1)S(1)}, bf16[21,32,128]{2,1,0:T(8,128)(2,1)S(1)}, u32[]{:S(2)}, u32[]{:S(2)}) collective-permute-start(bf16[21,32,128]{2,1,0:T(8,128)(2,1)S(1)} %pad_maximum_fusion.5), channel_id=1, source_target_pairs={{0,16},{4,20},{8,24},{12,28},{1,17},{5,21},{9,25},{13,29},{2,18},{... | collective-permute-start | bytes 516104 | tf_op jit(solution)/shard_map/ppermute | solution.py:319
  29.3 5.4 %collective-permute-start.4 = (bf16[20,32,128]{2,1,0:T(8,128)(2,1)S(1)}, bf16[20,32,128]{2,1,0:T(8,128)(2,1)S(1)}, u32[]{:S(2)}, u32[]{:S(2)}) collective-permute-start(bf16[20,32,128]{2,1,0:T(8,128)(2,1)S(1)} %select_convert_fusion.4.after_ref), channel_id=1, source_target_pairs={{0,4},{4,0},{8,12},{12,8},{16,20},{20,16},{24,28},{28,24},{1,5},{5... | collective-permute-start | bytes 491528 | tf_op jit(solution)/shard_map/ppermute | solution.py:314
  33.7 4.2 %copy-start.11 = (f32[20,1,512]{2,1,0:T(1,128)}, f32[20,1,512]{2,1,0:T(1,128)S(1)}, u32[]{:S(2)}) copy-start(f32[20,1,512]{2,1,0:T(1,128)S(1)} %get-tuple-element.54.skips_ref) | copy-start | bytes 122884
  37.9 14.3 %collective-permute-start.9 = (bf16[1280,512]{1,0:T(8,128)(2,1)}, bf16[1280,512]{1,0:T(8,128)(2,1)S(1)}, u32[]{:S(2)}, u32[]{:S(2)}) collective-permute-start(bf16[1280,512]{1,0:T(8,128)(2,1)} %shard_map.146.after_ref.m0_ref), channel_id=1, source_target_pairs={{0,2},{2,0},{1,3},{3,1},{4,6},{6,4},{5,7},{7,5},{8,10},{10,8},{9,1... | collective-permute-start | bytes 3932168 | tf_op jit(solution)/shard_map/ppermute | solution.py:314
  44.8 5.9 %collective-permute-start.6 = (bf16[21,32,128]{2,1,0:T(8,128)(2,1)S(1)}, bf16[21,32,128]{2,1,0:T(8,128)(2,1)S(1)}, u32[]{:S(2)}, u32[]{:S(2)}) collective-permute-start(bf16[21,32,128]{2,1,0:T(8,128)(2,1)S(1)} %pad_maximum_fusion.6), channel_id=1, source_target_pairs={{0,4},{4,0},{8,12},{12,8},{16,20},{20,16},{24,28},{28,24},{1,5},{5... | collective-permute-start | bytes 516104 | tf_op jit(solution)/shard_map/ppermute | solution.py:314
  45.7 6.6 %collective-permute-start.8 = (bf16[8,160,512]{2,1,0:T(8,128)(2,1)S(1)}, bf16[8,160,512]{2,1,0:T(8,128)(2,1)S(1)}, u32[]{:S(2)}, u32[]{:S(2)}) collective-permute-start(bf16[8,160,512]{2,1,0:T(8,128)(2,1)S(1)} %pad_maximum_fusion.1), channel_id=1, source_target_pairs={{0,2},{2,0},{1,3},{3,1},{4,6},{6,4},{5,7},{7,5},{8,10},{10,8},{9,1... | collective-permute-start | bytes 3932168 | tf_op jit(solution)/shard_map/ppermute | solution.py:314
  50.9 11.8 %collective-permute-start.7 = (bf16[21,32,128]{2,1,0:T(8,128)(2,1)S(1)}, bf16[21,32,128]{2,1,0:T(8,128)(2,1)S(1)}, u32[]{:S(2)}, u32[]{:S(2)}) collective-permute-start(bf16[21,32,128]{2,1,0:T(8,128)(2,1)S(1)} %pad_maximum_fusion.7.after_ref), channel_id=1, source_target_pairs={{8,0},{12,4},{16,8},{20,12},{24,16},{28,20},{9,1},{13,5},{17,9},{2... | collective-permute-start | bytes 516104 | tf_op jit(solution)/shard_map/ppermute | solution.py:319
  53.4 19.9 %collective-permute-start.11 = (bf16[4,160,640]{2,1,0:T(8,128)(2,1)S(1)}, bf16[4,160,640]{2,1,0:T(8,128)(2,1)S(1)}, u32[]{:S(2)}, u32[]{:S(2)}) collective-permute-start(bf16[4,160,640]{2,1,0:T(8,128)(2,1)S(1)} %shard_map.148), channel_id=1, source_target_pairs={{0,4},{4,0},{8,12},{12,8},{16,20},{20,16},{24,28},{28,24},{1,5},{5... | collective-permute-start | bytes 2457608 | tf_op jit(solution)/shard_map/ppermute | solution.py:314
  56.2 27.9 %collective-permute-start.12 = (bf16[4,160,640]{2,1,0:T(8,128)(2,1)S(1)}, bf16[4,160,640]{2,1,0:T(8,128)(2,1)S(1)}, u32[]{:S(2)}, u32[]{:S(2)}) collective-permute-start(bf16[4,160,640]{2,1,0:T(8,128)(2,1)S(1)} %shard_map.149), channel_id=1, source_target_pairs={{0,8},{4,12},{8,0},{12,4},{16,24},{20,28},{24,16},{28,20},{1,9},{5... | collective-permute-start | bytes 2457608 | tf_op jit(solution)/shard_map/ppermute | solution.py:314
  62.9 10.4 %collective-permute-start.10 = (bf16[21,32,128]{2,1,0:T(8,128)(2,1)S(1)}, bf16[21,32,128]{2,1,0:T(8,128)(2,1)S(1)}, u32[]{:S(2)}, u32[]{:S(2)}) collective-permute-start(bf16[21,32,128]{2,1,0:T(8,128)(2,1)S(1)} %pad_maximum_fusion.8.after_ref), channel_id=1, source_target_pairs={{16,0},{20,4},{24,8},{28,12},{17,1},{21,5},{25,9},{29,13},{18,2},{... | collective-permute-start | bytes 516104 | tf_op jit(solution)/shard_map/ppermute | solution.py:319
  84.3 5.7 %collective-permute-start.13 = (bf16[20,32,128]{2,1,0:T(8,128)(2,1)S(1)}, bf16[20,32,128]{2,1,0:T(8,128)(2,1)S(1)}, u32[]{:S(2)}, u32[]{:S(2)}) collective-permute-start(bf16[20,32,128]{2,1,0:T(8,128)(2,1)S(1)} %select_convert_fusion.1), channel_id=1, source_target_pairs={{0,4},{4,0},{8,12},{12,8},{16,20},{20,16},{24,28},{28,24},{1,5},{5... | collective-permute-start | bytes 491528 | tf_op jit(solution)/shard_map/ppermute | solution.py:314
  86.0 11.6 %collective-permute-start.14 = (bf16[2,160,640]{2,1,0:T(8,128)(2,1)S(1)}, bf16[2,160,640]{2,1,0:T(8,128)(2,1)}, u32[]{:S(2)}, u32[]{:S(2)}) collective-permute-start(bf16[2,160,640]{2,1,0:T(8,128)(2,1)S(1)} %fusion.after_a_ref), channel_id=1, source_target_pairs={{0,8},{4,12},{8,0},{12,4},{16,24},{20,28},{24,16},{28,20},{1,9},{5... | collective-permute-start | bytes 1228808 | tf_op jit(solution)/shard_map/ppermute | solution.py:314
  89.1 9.9 %collective-permute-start.15 = (bf16[2,160,640]{2,1,0:T(8,128)(2,1)S(1)}, bf16[2,160,640]{2,1,0:T(8,128)(2,1)}, u32[]{:S(2)}, u32[]{:S(2)}) collective-permute-start(bf16[2,160,640]{2,1,0:T(8,128)(2,1)S(1)} %fusion.1.after_b_ref), channel_id=1, source_target_pairs={{0,4},{4,0},{8,12},{12,8},{16,20},{20,16},{24,28},{28,24},{1,5},{5... | collective-permute-start | bytes 1228808 | tf_op jit(solution)/shard_map/ppermute | solution.py:314
  95.9 1.6 %collective-permute-start.16 = (f32[2,20,128]{2,1,0:T(8,128)S(1)}, f32[2,20,128]{2,1,0:T(8,128)S(1)}, u32[]{:S(2)}, u32[]{:S(2)}) collective-permute-start(f32[2,20,128]{2,1,0:T(8,128)S(1)} %get-tuple-element.76), channel_id=1, source_target_pairs={{0,2},{2,0},{1,3},{3,1},{4,6},{6,4},{5,7},{7,5},{8,10},{10,8},{9,1... | collective-permute-start | bytes 61448 | tf_op jit(solution)/shard_map/ppermute | solution.py:314
  95.9 4.9 %copy-start.16 = (f32[4,160,640]{2,1,0:T(8,128)S(1)}, f32[4,160,640]{2,1,0:T(8,128)}, u32[]{:S(2)}) copy-start(f32[4,160,640]{2,1,0:T(8,128)} %copy-done.15) | copy-start | bytes 4915204
  95.9 14.3 %collective-permute-start.19 = (f32[512,256]{1,0:T(8,128)S(1)}, f32[512,256]{1,0:T(8,128)S(1)}, u32[]{:S(2)}, u32[]{:S(2)}) collective-permute-start(f32[512,256]{1,0:T(8,128)S(1)} %get-tuple-element.79), channel_id=1, source_target_pairs={{0,1},{1,0},{2,3},{3,2},{4,5},{5,4},{6,7},{7,6},{8,9},{9,8},{10,11... | collective-permute-start | bytes 1572872 | tf_op jit(solution)/shard_map/ppermute | solution.py:314
  100.1 18.2 %collective-permute-start.17 = (bf16[160,640]{1,0:T(8,128)(2,1)S(1)}, bf16[160,640]{1,0:T(8,128)(2,1)S(1)}, u32[]{:S(2)}, u32[]{:S(2)}) collective-permute-start(bf16[160,640]{1,0:T(8,128)(2,1)S(1)} %fusion.12), channel_id=1, source_target_pairs={{0,16},{4,20},{8,24},{12,28},{16,0},{20,4},{24,8},{28,12},{1,17},{... | collective-permute-start | bytes 614408 | tf_op jit(solution)/shard_map/ppermute | solution.py:314
  102.6 20.0 %copy-start.18 = (f32[2,160,640]{2,1,0:T(8,128)S(1)}, f32[2,160,640]{2,1,0:T(8,128)}, u32[]{:S(2)}) copy-start(f32[2,160,640]{2,1,0:T(8,128)} %copy-done.17) | copy-start | bytes 2457604
  102.6 20.0 %collective-permute-start.18 = (bf16[160,640]{1,0:T(8,128)(2,1)}, bf16[160,640]{1,0:T(8,128)(2,1)S(1)}, u32[]{:S(2)}, u32[]{:S(2)}) collective-permute-start(bf16[160,640]{1,0:T(8,128)(2,1)} %fusion.13), channel_id=1, source_target_pairs={{0,16},{4,20},{8,24},{12,28},{16,0},{20,4},{24,8},{28,12},{1,17},{... | collective-permute-start | bytes 614408 | tf_op jit(solution)/shard_map/ppermute | solution.py:314
  105.6 18.6 %all-to-all-start = ((f32[8,2,20,128]{3,1,2,0:T(2,128)}), f32[8,2,20,128]{3,1,2,0:T(2,128)S(1)}, u32[]{:S(2)}, u32[]{:S(2)}) async-start(f32[8,2,20,128]{3,1,2,0:T(2,128)} %broadcast_in_dim.73), calls=%async_computation | async-start | bytes 327680 | tf_op jit(solution)/shard_map/all_to_all | solution.py:639
  (8 other events, 11.6 us)

commit v5 on v4

--- a/solution.py
+++ b/solution.py
@@ -502,7 +502,8 @@
         )(inner, state_in, c, x, grown, skips, after)
 
     n_bits = n_seq.bit_length() - 1
-    half = channels // 2
+    unit = channels // 5 if channels % 640 == 0 else channels // 2
+    sizes = (3 * unit, 2 * unit) if channels % 640 == 0 else (unit, unit)
 
     def my_bit(bit):
         value = jnp.bitwise_and(my_seq >> bit, 1)
@@ -511,18 +512,19 @@
     def terms(mixed, mixed_other, stream, bit, value, dtype, after):
         low = 1 << bit
         high = n_seq // (2 * low)
-        rows = pl.BlockSpec((half, length), lambda i, pick: (stream, 0))
+        offset = sizes[0] // unit if stream else 0
+        rows = pl.BlockSpec((unit, length), lambda i, pick: (offset + i, 0))
         columns = pl.BlockSpec(
             (high, 1, low, out_columns, length), lambda i, pick: (0, pick[0], 0, 0, 0)
         )
         split_blocks = lambda blocks: blocks.reshape(high, 2, low, out_columns, length)
         return call(
             terms_kernel,
-            (1,),
+            (sizes[stream] // unit,),
             [columns, columns, rows, rows, ANY],
-            whole(n_seq // 2, out_columns, half),
-            jax.ShapeDtypeStruct((n_seq // 2, out_columns, half), dtype),
-            flops=n_seq * out_columns * half * 2 * length,
+            pl.BlockSpec((n_seq // 2, out_columns, unit), lambda i, pick: (0, 0, i)),
+            jax.ShapeDtypeStruct((n_seq // 2, out_columns, sizes[stream]), dtype),
+            flops=n_seq * out_columns * sizes[stream] * 2 * length,
             prefetch=1,
         )(
             value.astype(jnp.int32).reshape(1),
@@ -547,20 +549,23 @@
     g_other = swap(chosen(1 - my_dp), "dp", 2, 1)
     y_cotan, local_cotan = cotans(g_second, first_sum, mixed)
 
-    def sending(after):
-        held["sends"] = [
-            terms(*held["mixed"], s, orders[s][0], 1 - my_bit(orders[s][0]), BF16, after) for s in (0, 1)
-        ]
-        return held["sends"]
-
-    def keeping(after):
-        sends = held["sends"]
-        held["gots"] = [swap(sends[s], "seq", n_seq, 1 << orders[s][0]) for s in (0, 1)]
-        held["keeps"] = [
-            terms(*held["mixed"], s, orders[s][0], my_bit(orders[s][0]), F32, after) for s in (0, 1)
-        ]
-        held["back"] = back(after)
-        return held["keeps"], held["back"], held["gots"]
+    def keeping(s, after):
+        return terms(*held["mixed"], s, orders[s][0], my_bit(orders[s][0]), F32, after)
+
+    def sending(s, after):
+        send = terms(*held["mixed"], s, orders[s][0], 1 - my_bit(orders[s][0]), BF16, after)
+        held[s] = swap(send, "seq", n_seq, 1 << orders[s][0])
+        return send
+
+    def sending_a(after):
+        held["send"] = sending(0, after)
+        return held["send"], keeping(0, held["send"])
+
+    def sending_b(after):
+        return sending(1, after)
+
+    def behind(after):
+        return [keeping(s, after) for s in (1,)], back(after), (held[0], held[1])
 
     long = jax.ShapeDtypeStruct((heads, 1, length), F32)
     wide = jax.ShapeDtypeStruct((length, n_state), F32)
@@ -578,9 +583,10 @@
     )(x, y_cotan, inner, state_in, b, c, grown, shrunk, after)
     works, cotan_end, _ = pair_scan(
         *halves_of(local_cotan.reshape(heads, HEAD_DIM, n_state), total), total, n_seq, True,
-        {1: sending, 2: keeping},
+        {0: sending_a, 1: sending_b, 2: behind},
     )
-    keeps, (outer, from_y, grad_b, grad_c), gots = works[-1]
+    (_, keep_a), _, ((keep_b,), (outer, from_y, grad_b, grad_c), gots) = works
+    keeps = keep_a, keep_b
 
     def halve(sums, left):
         axis = sorted(left, reverse=True).index(left[0])
@@ -590,7 +596,7 @@
     streams = []
     for s in (0, 1):
         sums = keeps[s] + gots[s].astype(F32)
-        sums = sums.reshape((2,) * (n_bits - 1) + (out_columns, half))
+        sums = sums.reshape((2,) * (n_bits - 1) + (out_columns, sizes[s]))
         streams.append(halve(sums, orders[s][1:]))
     grad_inputs, grad_dt, small, both = call(
         last_kernel,
@@ -638,7 +644,8 @@
         if done + 1 == n_bits:
             small = lax.all_to_all(jnp.broadcast_to(small, (n_seq,) + small.shape), "seq", 0, 0)
             both = (both + both_other if n_tensor == 2 else lax.psum(both, "tensor")).astype(BF16)
-            gots, both = lax.optimization_barrier((gots, both))
+            grad_b, grad_c = both[:, :n_state], both[:, n_state:]
+            gots, grad_b, grad_c = lax.optimization_barrier((gots, grad_b, grad_c))
         pairs = [streams[s][0] + gots[s].astype(F32) for s in (0, 1)]
         if done + 1 < n_bits:
             streams = [halve(pairs[s], orders[s][done + 1 :]) for s in (0, 1)]
@@ -649,8 +656,8 @@
     return (
         mixed[None],
         grad_inputs[None],
-        both[None, :, :n_state],
-        both[None, :, n_state:],
+        grad_b[None],
+        grad_c[None],
         grad_dt[:, 0][None],
         small[0],
         small[1],

time: 126 us -> 123 us (0.976)
  waiting for transfers between devices: 36.8 us -> 30.2 us
  other arithmetic: 5.62 us -> 6.97 us
  Pallas kernels: 34.4 us -> 35.7 us
    ppermute x16, waiting for transfers between devices: 33.7 us -> 23.4 us  [swap(): return lax.ppermute(value, axis, [(i, i ^ bit) for i in range(size)])]
    ppermute x4, waiting for transfers between devices: 3.05 us -> 6.8 us  [shifted(): return lax.ppermute(value, axis, pairs)]
    unnamed x38 -> x40, local copies, waits for them, and re-layouts: 1.78 us -> 3.5 us
    pallas_call x4, Pallas kernels: 4.83 us -> 6.23 us  [terms(): call(terms_kernel, (sizes[stream] // unit,), [columns, columns, rows, row...]
  transfers between devices with their start and end apart: 21 -> 21, of which waited for: 10 -> 10; matrix products, arithmetic and copies ran while one was open for 7% -> 8% of each run, Pallas kernels for 28% -> 29%
where the time goes in v5:
time: 123 us; the launch traced here: 122 us
  starting transfers between devices  40.9 us (33%)
  Pallas kernels  35.7 us (29%)
  waiting for transfers between devices  30.2 us (25%)
  other arithmetic  6.97 us (6%)
  local copies, waits for them, and re-layouts  6.87 us (6%)
  between operations  1.39 us (1%)
    ppermute x16, starting transfers between devices, swap(): return lax.ppermute(value, axis, [(i, i ^ bit) for i in range(size)])  24.3 us
    ppermute x16, waiting for transfers between devices, swap(): return lax.ppermute(value, axis, [(i, i ^ bit) for i in range(size)])  23.4 us
    ppermute x4, starting transfers between devices, shifted(): return lax.ppermute(value, axis, pairs)  11.7 us
    ppermute x4, waiting for transfers between devices, shifted(): return lax.ppermute(value, axis, pairs)  6.8 us
    pallas_call x1, Pallas kernels, per_device(): call(back_kernel, grid, [by_row(block, length)] * 3 + [by_row(block, n_st...  6.4 us
    pallas_call x4, Pallas kernels, terms(): call(terms_kernel, (sizes[stream] // unit,), [columns, columns, rows, row...  6.23 us
    pallas_call x1, Pallas kernels, per_device(): call(last_kernel, grid, [by_row(block, length)] * 3 + [by_row(block, n_st...  5.22 us
    all_to_all x1, starting transfers between devices, per_device(): lax.all_to_all(jnp.broadcast_to(small, (n_seq,) + small.shape), 'seq', 0, 0)  4.85 us
  transfers between devices with their start and end apart: 21, of which 10 were waited for; matrix products, arithmetic and copies ran while one was open for 8% of the time, Pallas kernels for 29%

profile of v5, /device:TPU:0, one launch (start us, length us, event | category | flops | bytes accessed | tf_op | source)
XLA Modules:
  0.0 122.0 jit_solution(11802022346918282440)
XLA Ops:
  1.2 4.2 %shard_map.143 = (f32[20,1,512]{2,1,0:T(1,128)}, f32[20,1,512]{2,1,0:T(1,128)}, f32[20,128]{1,0:T(8,128)}, f32[1280,128]{1,0:T(8,128)}, bf16[21,32,128]{2,1,0:T(8,128)(2,1)}, /*index=5*/f32[20,32,128]{2,1,0:T(8,128)}) custom-call(s32[1]{0:T(128)} %bitcast.3.upper_ref, bf16[1280,512]{1,0:T(8,128)(2,1)} %bitcast.192, bf16[512,128]{1,0:T(8,128)(2,1)} %bitcast.206, ...), custom_call_target="tpu_custom_call" | custom-call | flops 6710886400 | bytes 80000000 | tf_op jit(solution)/shard_map/pallas_call | solution.py:421
  5.4 2.6 %collective-permute-start = (bf16[21,32,128]{2,1,0:T(8,128)(2,1)}, bf16[21,32,128]{2,1,0:T(8,128)(2,1)S(1)}, u32[]{:S(2)}, u32[]{:S(2)}) collective-permute-start(bf16[21,32,128]{2,1,0:T(8,128)(2,1)} %get-tuple-element.51), channel_id=1, source_target_pairs={{0,4},{4,0},{8,12},{12,8},{16,20},{20,16},{24,28},{28,24},{1,5},{5... | collective-permute-start | bytes 516104 | tf_op jit(solution)/shard_map/ppermute | solution.py:314
  7.9 1.5 %collective-permute-start.5 = (bf16[1280,512]{1,0:T(8,128)(2,1)S(1)}, bf16[1280,512]{1,0:T(8,128)(2,1)S(1)}, u32[]{:S(2)}, u32[]{:S(2)}) collective-permute-start(bf16[1280,512]{1,0:T(8,128)(2,1)S(1)} %bitcast.180), channel_id=1, source_target_pairs={{0,1},{1,0},{2,3},{3,2},{4,5},{5,4},{6,7},{7,6},{8,9},{9,8},{10,11... | collective-permute-start | bytes 3932168 | tf_op jit(solution)/shard_map/ppermute | solution.py:314
  10.4 2.7 %collective-permute-done = bf16[21,32,128]{2,1,0:T(8,128)(2,1)S(1)} collective-permute-done((bf16[21,32,128]{2,1,0:T(8,128)(2,1)}, bf16[21,32,128]{2,1,0:T(8,128)(2,1)S(1)}, u32[]{:S(2)}, u32[]{:S(2)}) %collective-permute-start) | collective-permute-done | bytes 172064 | tf_op jit(solution)/shard_map/ppermute | solution.py:314
  13.4 3.7 %collective-permute-start.1 = (bf16[21,32,128]{2,1,0:T(8,128)(2,1)S(1)}, bf16[21,32,128]{2,1,0:T(8,128)(2,1)S(1)}, u32[]{:S(2)}, u32[]{:S(2)}) collective-permute-start(bf16[21,32,128]{2,1,0:T(8,128)(2,1)S(1)} %pad_maximum_fusion.4.after_ref), channel_id=1, source_target_pairs={{0,8},{4,12},{8,16},{12,20},{16,24},{20,28},{1,9},{5,13},{9,17},{1... | collective-permute-start | bytes 516104 | tf_op jit(solution)/shard_map/ppermute | solution.py:319
  17.2 3.5 %shard_map.144.first_ref = f32[1280,512]{1,0:T(8,128)S(1)} custom-call(s32[1]{0:T(128)} %bitcast.10.flag_ref, bf16[1280,1280]{1,0:T(8,128)(2,1)S(1)} %copy-done.1, bf16[1280,1280]{1,0:T(8,128)(2,1)} %collective-permute-done.2.other_ref, bf16[1280,512]{1,0:T(8,128)(2,1)S(1)} %bitcast.182, bf16[21,32,128]{2,1,0:T(8,128)(2,1)S(1)} %pad_maximum_fusion.4.after_ref), custom_call_target="tpu_custom_call" | custom-call | flops 33554432000 | bytes 80000000 | tf_op jit(solution)/shard_map/pallas_call | solution.py:466
  21.0 5.2 %collective-permute-start.3 = (bf16[21,32,128]{2,1,0:T(8,128)(2,1)S(1)}, bf16[21,32,128]{2,1,0:T(8,128)(2,1)S(1)}, u32[]{:S(2)}, u32[]{:S(2)}) collective-permute-start(bf16[21,32,128]{2,1,0:T(8,128)(2,1)S(1)} %pad_maximum_fusion.5), channel_id=1, source_target_pairs={{0,16},{4,20},{8,24},{12,28},{1,17},{5,21},{9,25},{13,29},{2,18},{... | collective-permute-start | bytes 516104 | tf_op jit(solution)/shard_map/ppermute | solution.py:319
  26.3 2.9 %collective-permute-done.3 = bf16[21,32,128]{2,1,0:T(8,128)(2,1)S(1)} collective-permute-done((bf16[21,32,128]{2,1,0:T(8,128)(2,1)S(1)}, bf16[21,32,128]{2,1,0:T(8,128)(2,1)S(1)}, u32[]{:S(2)}, u32[]{:S(2)}) %collective-permute-start.3) | collective-permute-done | bytes 172064 | tf_op jit(solution)/shard_map/ppermute | solution.py:319
  29.3 1.6 %collective-permute-start.4 = (bf16[20,32,128]{2,1,0:T(8,128)(2,1)S(1)}, bf16[20,32,128]{2,1,0:T(8,128)(2,1)S(1)}, u32[]{:S(2)}, u32[]{:S(2)}) collective-permute-start(bf16[20,32,128]{2,1,0:T(8,128)(2,1)S(1)} %select_convert_fusion.4.after_ref), channel_id=1, source_target_pairs={{0,4},{4,0},{8,12},{12,8},{16,20},{20,16},{24,28},{28,24},{1,5},{5... | collective-permute-start | bytes 491528 | tf_op jit(solution)/shard_map/ppermute | solution.py:314
  30.9 2.8 %shard_map.145 = (f32[1280,512]{1,0:T(8,128)S(1)}, f32[20,1,512]{2,1,0:T(1,128)S(1)}) custom-call(bf16[1280,512]{1,0:T(8,128)(2,1)S(1)} %bitcast.193, bf16[512,128]{1,0:T(8,128)(2,1)S(1)} %bitcast.207, bf16[512,128]{1,0:T(8,128)(2,1)S(1)} %bitcast.202, f32[20,1,512]{2,1,0:T(1,128)S(1)} %copy-done.11, f32[1,20]{1,0:T(1,128)S(1)} %bitcast.212, ...), custom_call_target="tpu_custom_call" | custom-call | flops 33554432000 | bytes 80000000 | tf_op jit(solution)/shard_map/pallas_call | solution.py:444
  35.1 2.8 %shard_map.146.after_ref.m0_ref = bf16[1280,512]{1,0:T(8,128)(2,1)} custom-call(f32[1280,512]{1,0:T(8,128)S(1)} %get-tuple-element.54.inner_ref, bf16[1280,128]{1,0:T(8,128)(2,1)S(1)} %bitcast.188, bf16[512,128]{1,0:T(8,128)(2,1)S(1)} %bitcast.203, bf16[1280,512]{1,0:T(8,128)(2,1)S(1)} %bitcast.194, f32[20,1,512]{2,1,0:T(1,128)S(1)} %copy-done.10, ...), custom_call_target="tpu_custom_call" | custom-call | flops 3355443200 | bytes 80000000 | tf_op jit(solution)/shard_map/pallas_call | solution.py:493
  40.2 4.5 %shard_map.147 = (bf16[1280,512]{1,0:T(8,128)(2,1)S(1)}, f32[1280,128]{1,0:T(8,128)S(1)}) custom-call(s32[1]{0:T(128)} %bitcast.10.flag_ref, bf16[1280,1280]{1,0:T(8,128)(2,1)S(1)} %copy-done.1, bf16[1280,1280]{1,0:T(8,128)(2,1)} %collective-permute-done.2.other_ref, bf16[1280,512]{1,0:T(8,128)(2,1)S(1)} %collective-permute-done.5.g_ref, ...), custom_call_target="tpu_custom_call" | custom-call | flops 40265318400 | bytes 80000000 | tf_op jit(solution)/shard_map/pallas_call | solution.py:475
  45.6 1.8 %shard_map.148.after_ref = bf16[4,160,768]{2,1,0:T(8,128)(2,1)S(1)} custom-call(s32[1]{0:T(128)} %bitcast.22.pick_ref, bf16[4,2,1,160,512]{4,3,2,1,0:T(8,128)(2,1)S(1)} %bitcast.184, bf16[4,2,1,160,512]{4,3,2,1,0:T(8,128)(2,1)S(1)} %bitcast.198, bf16[1280,512]{1,0:T(8,128)(2,1)S(1)} %copy-done.3, bf16[1280,512]{1,0:T(8,128)(2,1)S(1)} %collective-permute-done.8.m1_ref, ...), custom_call_target="tpu_custom_call" | custom-call | flops 20132659200 | bytes 80000000 | tf_op jit(solution)/shard_map/pallas_call | solution.py:521
  47.4 1.5 %collective-permute-start.11 = (bf16[4,160,768]{2,1,0:T(8,128)(2,1)S(1)}, bf16[4,160,768]{2,1,0:T(8,128)(2,1)S(1)}, u32[]{:S(2)}, u32[]{:S(2)}) collective-permute-start(bf16[4,160,768]{2,1,0:T(8,128)(2,1)S(1)} %shard_map.148.after_ref), channel_id=1, source_target_pairs={{0,4},{4,0},{8,12},{12,8},{16,20},{20,16},{24,28},{28,24},{1,5},{5... | collective-permute-start | bytes 2949128 | tf_op jit(solution)/shard_map/ppermute | solution.py:314
  49.0 1.8 %shard_map.149 = f32[4,160,768]{2,1,0:T(8,128)S(1)} custom-call(s32[1]{0:T(128)} %bitcast.31.pick_ref, bf16[4,2,1,160,512]{4,3,2,1,0:T(8,128)(2,1)S(1)} %bitcast.185, bf16[4,2,1,160,512]{4,3,2,1,0:T(8,128)(2,1)S(1)} %bitcast.199, bf16[1280,512]{1,0:T(8,128)(2,1)S(1)} %copy-done.3, bf16[1280,512]{1,0:T(8,128)(2,1)S(1)} %collective-permute-done.8.m1_ref, ...), custom_call_target="tpu_custom_call" | custom-call | flops 20132659200 | bytes 80000000 | tf_op jit(solution)/shard_map/pallas_call | solution.py:521
  51.4 1.3 %collective-permute-start.9 = (bf16[21,32,128]{2,1,0:T(8,128)(2,1)S(1)}, bf16[21,32,128]{2,1,0:T(8,128)(2,1)S(1)}, u32[]{:S(2)}, u32[]{:S(2)}) collective-permute-start(bf16[21,32,128]{2,1,0:T(8,128)(2,1)S(1)} %pad_maximum_fusion.7.after_ref), channel_id=1, source_target_pairs={{8,0},{12,4},{16,8},{20,12},{24,16},{28,20},{9,1},{13,5},{17,9},{2... | collective-permute-start | bytes 516104 | tf_op jit(solution)/shard_map/ppermute | solution.py:319
  52.7 1.3 %shard_map.150 = bf16[4,160,512]{2,1,0:T(8,128)(2,1)S(1)} custom-call(s32[1]{0:T(128)} %bitcast.36.pick_ref, bf16[2,2,2,160,512]{4,3,2,1,0:T(8,128)(2,1)S(1)} %bitcast.186, bf16[2,2,2,160,512]{4,3,2,1,0:T(8,128)(2,1)S(1)} %bitcast.200, bf16[1280,512]{1,0:T(8,128)(2,1)S(1)} %copy-done.3, bf16[1280,512]{1,0:T(8,128)(2,1)S(1)} %collective-permute-done.8.m1_ref, ...), custom_call_target="tpu_custom_call" | custom-call | flops 13421772800 | bytes 80000000 | tf_op jit(solution)/shard_map/pallas_call | solution.py:521
  53.9 6.3 %collective-permute-start.12 = (bf16[4,160,512]{2,1,0:T(8,128)(2,1)S(1)}, bf16[4,160,512]{2,1,0:T(8,128)(2,1)S(1)}, u32[]{:S(2)}, u32[]{:S(2)}) collective-permute-start(bf16[4,160,512]{2,1,0:T(8,128)(2,1)S(1)} %shard_map.150), channel_id=1, source_target_pairs={{0,8},{4,12},{8,0},{12,4},{16,24},{20,28},{24,16},{28,20},{1,9},{5... | collective-permute-start | bytes 1966088 | tf_op jit(solution)/shard_map/ppermute | solution.py:314
  60.3 3.9 %collective-permute-done.9 = bf16[21,32,128]{2,1,0:T(8,128)(2,1)S(1)} collective-permute-done((bf16[21,32,128]{2,1,0:T(8,128)(2,1)S(1)}, bf16[21,32,128]{2,1,0:T(8,128)(2,1)S(1)}, u32[]{:S(2)}, u32[]{:S(2)}) %collective-permute-start.9) | collective-permute-done | bytes 172064 | tf_op jit(solution)/shard_map/ppermute | solution.py:319
  64.4 1.5 %collective-permute-start.10 = (bf16[21,32,128]{2,1,0:T(8,128)(2,1)S(1)}, bf16[21,32,128]{2,1,0:T(8,128)(2,1)S(1)}, u32[]{:S(2)}, u32[]{:S(2)}) collective-permute-start(bf16[21,32,128]{2,1,0:T(8,128)(2,1)S(1)} %pad_maximum_fusion.8.after_ref), channel_id=1, source_target_pairs={{16,0},{20,4},{24,8},{28,12},{17,1},{21,5},{25,9},{29,13},{18,2},{... | collective-permute-start | bytes 516104 | tf_op jit(solution)/shard_map/ppermute | solution.py:319
  65.9 6.4 %shard_map.152 = (f32[1280,512]{1,0:T(8,128)S(1)}, f32[20,1,512]{2,1,0:T(1,128)S(1)}, f32[512,128]{1,0:T(8,128)S(1)}, f32[512,128]{1,0:T(8,128)S(1)}) custom-call(bf16[1280,512]{1,0:T(8,128)(2,1)S(1)} %bitcast.195, bf16[1280,512]{1,0:T(8,128)(2,1)S(1)} %get-tuple-element.59.cotan_ref, f32[1280,512]{1,0:T(8,128)S(1)} %get-tuple-element.54.inner_ref, ...), custom_call_target="tpu_custom_call" | custom-call | flops 67108864000 | bytes 80000000 | tf_op jit(solution)/shard_map/pallas_call | solution.py:572
  72.3 1.3 %shard_map.151 = f32[4,160,512]{2,1,0:T(8,128)S(1)} custom-call(s32[1]{0:T(128)} %bitcast.41.pick_ref, bf16[2,2,2,160,512]{4,3,2,1,0:T(8,128)(2,1)S(1)} %bitcast.187, bf16[2,2,2,160,512]{4,3,2,1,0:T(8,128)(2,1)S(1)} %bitcast.201, bf16[1280,512]{1,0:T(8,128)(2,1)S(1)} %copy-done.3, bf16[1280,512]{1,0:T(8,128)(2,1)S(1)} %collective-permute-done.8.m1_ref, ...), custom_call_target="tpu_custom_call" | custom-call | flops 13421772800 | bytes 80000000 | tf_op jit(solution)/shard_map/pallas_call | solution.py:521
  73.6 6.9 %collective-permute-done.12 = bf16[4,160,512]{2,1,0:T(8,128)(2,1)S(1)} collective-permute-done((bf16[4,160,512]{2,1,0:T(8,128)(2,1)S(1)}, bf16[4,160,512]{2,1,0:T(8,128)(2,1)S(1)}, u32[]{:S(2)}, u32[]{:S(2)}) %collective-permute-start.12) | collective-permute-done | bytes 655392 | tf_op jit(solution)/shard_map/ppermute | solution.py:314
  80.7 1.6 %collective-permute-start.13 = (bf16[20,32,128]{2,1,0:T(8,128)(2,1)S(1)}, bf16[20,32,128]{2,1,0:T(8,128)(2,1)S(1)}, u32[]{:S(2)}, u32[]{:S(2)}) collective-permute-start(bf16[20,32,128]{2,1,0:T(8,128)(2,1)S(1)} %select_convert_fusion.1), channel_id=1, source_target_pairs={{0,4},{4,0},{8,12},{12,8},{16,20},{20,16},{24,28},{28,24},{1,5},{5... | collective-permute-start | bytes 491528 | tf_op jit(solution)/shard_map/ppermute | solution.py:314
  82.5 2.8 %collective-permute-start.14 = (bf16[2,160,768]{2,1,0:T(8,128)(2,1)S(1)}, bf16[2,160,768]{2,1,0:T(8,128)(2,1)}, u32[]{:S(2)}, u32[]{:S(2)}) collective-permute-start(bf16[2,160,768]{2,1,0:T(8,128)(2,1)S(1)} %fusion.after_a_ref), channel_id=1, source_target_pairs={{0,8},{4,12},{8,0},{12,4},{16,24},{20,28},{24,16},{28,20},{1,9},{5... | collective-permute-start | bytes 1474568 | tf_op jit(solution)/shard_map/ppermute | solution.py:314
  87.2 5.2 %shard_map.153 = (bf16[1280,512]{1,0:T(8,128)(2,1)}, f32[20,1,512]{2,1,0:T(1,128)}, f32[2,20,128]{2,1,0:T(8,128)S(1)}, f32[512,256]{1,0:T(8,128)S(1)}) custom-call(bf16[1280,512]{1,0:T(8,128)(2,1)S(1)} %bitcast.196, bf16[1280,512]{1,0:T(8,128)(2,1)S(1)} %get-tuple-element.59.cotan_ref, f32[1280,512]{1,0:T(8,128)S(1)} %get-tuple-element.67.outer_ref, ...), custom_call_target="tpu_custom_call" | custom-call | flops 10066329600 | bytes 80000000 | tf_op jit(solution)/shard_map/pallas_call | solution.py:601
  92.5 1.6 %collective-permute-start.19 = (f32[512,256]{1,0:T(8,128)S(1)}, f32[512,256]{1,0:T(8,128)}, u32[]{:S(2)}, u32[]{:S(2)}) collective-permute-start(f32[512,256]{1,0:T(8,128)S(1)} %get-tuple-element.82), channel_id=1, source_target_pairs={{0,1},{1,0},{2,3},{3,2},{4,5},{5,4},{6,7},{7,6},{8,9},{9,8},{10,11... | collective-permute-start | bytes 1572872 | tf_op jit(solution)/shard_map/ppermute | solution.py:314
  95.3 1.3 %bitcast_add_fusion.1 = f32[2,160,512]{2,1,0:T(8,128)S(1)} fusion(bf16[2,160,512]{2,1,0:T(8,128)(2,1)} %collective-permute-done.15, f32[2,2,160,512]{3,2,1,0:T(8,128)} %bitcast.218, s32[]{:T(128)S(6)} %select_n.225), kind=kLoop, calls=%fused_computation.7 | loop fusion | flops 327680 | bytes 1638404 | tf_op jit(solution)/shard_map/add | solution.py:649
  99.5 3.0 %collective-permute-start.17 = (bf16[160,768]{1,0:T(8,128)(2,1)S(1)}, bf16[160,768]{1,0:T(8,128)(2,1)S(1)}, u32[]{:S(2)}, u32[]{:S(2)}) collective-permute-start(bf16[160,768]{1,0:T(8,128)(2,1)S(1)} %fusion.12), channel_id=1, source_target_pairs={{0,16},{4,20},{8,24},{12,28},{16,0},{20,4},{24,8},{28,12},{1,17},{... | collective-permute-start | bytes 737288 | tf_op jit(solution)/shard_map/ppermute | solution.py:314
  103.3 4.9 %all-to-all-start = ((f32[8,2,20,128]{3,1,2,0:T(2,128)}), f32[8,2,20,128]{3,1,2,0:T(2,128)S(1)}, u32[]{:S(2)}, u32[]{:S(2)}) async-start(f32[8,2,20,128]{3,1,2,0:T(2,128)} %broadcast_in_dim.73), calls=%async_computation | async-start | bytes 327680 | tf_op jit(solution)/shard_map/all_to_all | solution.py:645
  110.0 5.7 %collective-permute-done.18 = bf16[160,512]{1,0:T(8,128)(2,1)S(1)} collective-permute-done((bf16[160,512]{1,0:T(8,128)(2,1)S(1)}, bf16[160,512]{1,0:T(8,128)(2,1)S(1)}, u32[]{:S(2)}, u32[]{:S(2)}) %collective-permute-start.18) | collective-permute-done | bytes 163872 | tf_op jit(solution)/shard_map/ppermute | solution.py:314
  115.7 4.6 %collective-permute-done.17 = bf16[160,768]{1,0:T(8,128)(2,1)S(1)} collective-permute-done((bf16[160,768]{1,0:T(8,128)(2,1)S(1)}, bf16[160,768]{1,0:T(8,128)(2,1)S(1)}, u32[]{:S(2)}, u32[]{:S(2)}) %collective-permute-start.17) | collective-permute-done | bytes 245792 | tf_op jit(solution)/shard_map/ppermute | solution.py:314
  (126 shorter events, 17.9 us)
Async XLA Ops:
  0.6 16.5 %collective-permute-start.2 = (bf16[1280,1280]{1,0:T(8,128)(2,1)}, bf16[1280,1280]{1,0:T(8,128)(2,1)}, u32[]{:S(2)}, u32[]{:S(2)}) collective-permute-start(bf16[1280,1280]{1,0:T(8,128)(2,1)} %mine_ref.3), channel_id=1, source_target_pairs={{0,2},{2,0},{1,3},{3,1},{4,6},{6,4},{5,7},{7,5},{8,10},{10,8},{9,1... | collective-permute-start | bytes 9830408 | tf_op jit(solution)/shard_map/ppermute | solution.py:314
  1.2 6.8 %copy-start = (bf16[1,1280,512]{2,1,0:T(8,128)(2,1)S(1)}, bf16[1,1280,512]{2,1,0:T(8,128)(2,1)}, u32[]{:S(2)}) copy-start(bf16[1,1280,512]{2,1,0:T(8,128)(2,1)} %param.15) | copy-start | bytes 3932164
  5.4 7.8 %collective-permute-start = (bf16[21,32,128]{2,1,0:T(8,128)(2,1)}, bf16[21,32,128]{2,1,0:T(8,128)(2,1)S(1)}, u32[]{:S(2)}, u32[]{:S(2)}) collective-permute-start(bf16[21,32,128]{2,1,0:T(8,128)(2,1)} %get-tuple-element.51), channel_id=1, source_target_pairs={{0,4},{4,0},{8,12},{12,8},{16,20},{20,16},{24,28},{28,24},{1,5},{5... | collective-permute-start | bytes 516104 | tf_op jit(solution)/shard_map/ppermute | solution.py:314
  7.9 30.9 %collective-permute-start.5 = (bf16[1280,512]{1,0:T(8,128)(2,1)S(1)}, bf16[1280,512]{1,0:T(8,128)(2,1)S(1)}, u32[]{:S(2)}, u32[]{:S(2)}) collective-permute-start(bf16[1280,512]{1,0:T(8,128)(2,1)S(1)} %bitcast.180), channel_id=1, source_target_pairs={{0,1},{1,0},{2,3},{3,2},{4,5},{5,4},{6,7},{7,6},{8,9},{9,8},{10,11... | collective-permute-start | bytes 3932168 | tf_op jit(solution)/shard_map/ppermute | solution.py:314
  10.3 3.0 %copy-start.12 = (f32[20,32,128]{2,1,0:T(8,128)S(1)}, f32[20,32,128]{2,1,0:T(8,128)}, u32[]{:S(2)}) copy-start(f32[20,32,128]{2,1,0:T(8,128)} %get-tuple-element.52) | copy-start | bytes 983044
  10.3 6.9 %copy-start.1 = (bf16[1280,1280]{1,0:T(8,128)(2,1)S(1)}, bf16[1280,1280]{1,0:T(8,128)(2,1)}, u32[]{:S(2)}) copy-start(bf16[1280,1280]{1,0:T(8,128)(2,1)} %mine_ref.3) | copy-start | bytes 9830404
  13.4 7.4 %collective-permute-start.1 = (bf16[21,32,128]{2,1,0:T(8,128)(2,1)S(1)}, bf16[21,32,128]{2,1,0:T(8,128)(2,1)S(1)}, u32[]{:S(2)}, u32[]{:S(2)}) collective-permute-start(bf16[21,32,128]{2,1,0:T(8,128)(2,1)S(1)} %pad_maximum_fusion.4.after_ref), channel_id=1, source_target_pairs={{0,8},{4,12},{8,16},{12,20},{16,24},{20,28},{1,9},{5,13},{9,17},{1... | collective-permute-start | bytes 516104 | tf_op jit(solution)/shard_map/ppermute | solution.py:319
  20.7 10.2 %copy-start.2 = (bf16[1,1280,512]{2,1,0:T(8,128)(2,1)S(1)}, bf16[1,1280,512]{2,1,0:T(8,128)(2,1)}, u32[]{:S(2)}) copy-start(bf16[1,1280,512]{2,1,0:T(8,128)(2,1)} %param.8) | copy-start | bytes 3932164
  20.7 10.2 %copy-start.4 = (bf16[1,512,128]{2,1,0:T(8,128)(2,1)S(1)}, bf16[1,512,128]{2,1,0:T(8,128)(2,1)}, u32[]{:S(2)}) copy-start(bf16[1,512,128]{2,1,0:T(8,128)(2,1)} %param.10) | copy-start | bytes 393220
  20.7 10.2 %copy-start.5 = (bf16[1,512,128]{2,1,0:T(8,128)(2,1)S(1)}, bf16[1,512,128]{2,1,0:T(8,128)(2,1)}, u32[]{:S(2)}) copy-start(bf16[1,512,128]{2,1,0:T(8,128)(2,1)} %param.9) | copy-start | bytes 393220
  20.7 10.2 %copy-start.7 = (f32[20]{0:T(128)S(1)}, f32[20]{0:T(128)}, u32[]{:S(2)}) copy-start(f32[20]{0:T(128)} %param.13) | copy-start | bytes 244
  20.8 10.2 %copy-start.11 = (f32[20,1,512]{2,1,0:T(1,128)S(1)}, f32[20,1,512]{2,1,0:T(1,128)}, u32[]{:S(2)}) copy-start(f32[20,1,512]{2,1,0:T(1,128)} %get-tuple-element.49.shrunk_ref) | copy-start | bytes 122884
  21.0 8.1 %collective-permute-start.3 = (bf16[21,32,128]{2,1,0:T(8,128)(2,1)S(1)}, bf16[21,32,128]{2,1,0:T(8,128)(2,1)S(1)}, u32[]{:S(2)}, u32[]{:S(2)}) collective-permute-start(bf16[21,32,128]{2,1,0:T(8,128)(2,1)S(1)} %pad_maximum_fusion.5), channel_id=1, source_target_pairs={{0,16},{4,20},{8,24},{12,28},{1,17},{5,21},{9,25},{13,29},{2,18},{... | collective-permute-start | bytes 516104 | tf_op jit(solution)/shard_map/ppermute | solution.py:319
  29.3 5.4 %collective-permute-start.4 = (bf16[20,32,128]{2,1,0:T(8,128)(2,1)S(1)}, bf16[20,32,128]{2,1,0:T(8,128)(2,1)S(1)}, u32[]{:S(2)}, u32[]{:S(2)}) collective-permute-start(bf16[20,32,128]{2,1,0:T(8,128)(2,1)S(1)} %select_convert_fusion.4.after_ref), channel_id=1, source_target_pairs={{0,4},{4,0},{8,12},{12,8},{16,20},{20,16},{24,28},{28,24},{1,5},{5... | collective-permute-start | bytes 491528 | tf_op jit(solution)/shard_map/ppermute | solution.py:314
  37.9 7.7 %collective-permute-start.8 = (bf16[1280,512]{1,0:T(8,128)(2,1)}, bf16[1280,512]{1,0:T(8,128)(2,1)S(1)}, u32[]{:S(2)}, u32[]{:S(2)}) collective-permute-start(bf16[1280,512]{1,0:T(8,128)(2,1)} %shard_map.146.after_ref.m0_ref), channel_id=1, source_target_pairs={{0,2},{2,0},{1,3},{3,1},{4,6},{6,4},{5,7},{7,5},{8,10},{10,8},{9,1... | collective-permute-start | bytes 3932168 | tf_op jit(solution)/shard_map/ppermute | solution.py:314
  39.1 6.5 %collective-permute-start.7 = (bf16[8,160,512]{2,1,0:T(8,128)(2,1)S(1)}, bf16[8,160,512]{2,1,0:T(8,128)(2,1)S(1)}, u32[]{:S(2)}, u32[]{:S(2)}) collective-permute-start(bf16[8,160,512]{2,1,0:T(8,128)(2,1)S(1)} %pad_maximum_fusion.1), channel_id=1, source_target_pairs={{0,2},{2,0},{1,3},{3,1},{4,6},{6,4},{5,7},{7,5},{8,10},{10,8},{9,1... | collective-permute-start | bytes 3932168 | tf_op jit(solution)/shard_map/ppermute | solution.py:314
  44.9 6.3 %collective-permute-start.6 = (bf16[21,32,128]{2,1,0:T(8,128)(2,1)S(1)}, bf16[21,32,128]{2,1,0:T(8,128)(2,1)S(1)}, u32[]{:S(2)}, u32[]{:S(2)}) collective-permute-start(bf16[21,32,128]{2,1,0:T(8,128)(2,1)S(1)} %pad_maximum_fusion.6.after_ref), channel_id=1, source_target_pairs={{0,4},{4,0},{8,12},{12,8},{16,20},{20,16},{24,28},{28,24},{1,5},{5... | collective-permute-start | bytes 516104 | tf_op jit(solution)/shard_map/ppermute | solution.py:314
  47.4 33.1 %collective-permute-start.11 = (bf16[4,160,768]{2,1,0:T(8,128)(2,1)S(1)}, bf16[4,160,768]{2,1,0:T(8,128)(2,1)S(1)}, u32[]{:S(2)}, u32[]{:S(2)}) collective-permute-start(bf16[4,160,768]{2,1,0:T(8,128)(2,1)S(1)} %shard_map.148.after_ref), channel_id=1, source_target_pairs={{0,4},{4,0},{8,12},{12,8},{16,20},{20,16},{24,28},{28,24},{1,5},{5... | collective-permute-start | bytes 2949128 | tf_op jit(solution)/shard_map/ppermute | solution.py:314
  51.4 12.8 %collective-permute-start.9 = (bf16[21,32,128]{2,1,0:T(8,128)(2,1)S(1)}, bf16[21,32,128]{2,1,0:T(8,128)(2,1)S(1)}, u32[]{:S(2)}, u32[]{:S(2)}) collective-permute-start(bf16[21,32,128]{2,1,0:T(8,128)(2,1)S(1)} %pad_maximum_fusion.7.after_ref), channel_id=1, source_target_pairs={{8,0},{12,4},{16,8},{20,12},{24,16},{28,20},{9,1},{13,5},{17,9},{2... | collective-permute-start | bytes 516104 | tf_op jit(solution)/shard_map/ppermute | solution.py:319
  53.9 26.6 %collective-permute-start.12 = (bf16[4,160,512]{2,1,0:T(8,128)(2,1)S(1)}, bf16[4,160,512]{2,1,0:T(8,128)(2,1)S(1)}, u32[]{:S(2)}, u32[]{:S(2)}) collective-permute-start(bf16[4,160,512]{2,1,0:T(8,128)(2,1)S(1)} %shard_map.150), channel_id=1, source_target_pairs={{0,8},{4,12},{8,0},{12,4},{16,24},{20,28},{24,16},{28,20},{1,9},{5... | collective-permute-start | bytes 1966088 | tf_op jit(solution)/shard_map/ppermute | solution.py:314
  64.4 9.2 %collective-permute-start.10 = (bf16[21,32,128]{2,1,0:T(8,128)(2,1)S(1)}, bf16[21,32,128]{2,1,0:T(8,128)(2,1)S(1)}, u32[]{:S(2)}, u32[]{:S(2)}) collective-permute-start(bf16[21,32,128]{2,1,0:T(8,128)(2,1)S(1)} %pad_maximum_fusion.8.after_ref), channel_id=1, source_target_pairs={{16,0},{20,4},{24,8},{28,12},{17,1},{21,5},{25,9},{29,13},{18,2},{... | collective-permute-start | bytes 516104 | tf_op jit(solution)/shard_map/ppermute | solution.py:319
  80.7 5.6 %collective-permute-start.13 = (bf16[20,32,128]{2,1,0:T(8,128)(2,1)S(1)}, bf16[20,32,128]{2,1,0:T(8,128)(2,1)S(1)}, u32[]{:S(2)}, u32[]{:S(2)}) collective-permute-start(bf16[20,32,128]{2,1,0:T(8,128)(2,1)S(1)} %select_convert_fusion.1), channel_id=1, source_target_pairs={{0,4},{4,0},{8,12},{12,8},{16,20},{20,16},{24,28},{28,24},{1,5},{5... | collective-permute-start | bytes 491528 | tf_op jit(solution)/shard_map/ppermute | solution.py:314
  82.5 12.7 %collective-permute-start.14 = (bf16[2,160,768]{2,1,0:T(8,128)(2,1)S(1)}, bf16[2,160,768]{2,1,0:T(8,128)(2,1)}, u32[]{:S(2)}, u32[]{:S(2)}) collective-permute-start(bf16[2,160,768]{2,1,0:T(8,128)(2,1)S(1)} %fusion.after_a_ref), channel_id=1, source_target_pairs={{0,8},{4,12},{8,0},{12,4},{16,24},{20,28},{24,16},{28,20},{1,9},{5... | collective-permute-start | bytes 1474568 | tf_op jit(solution)/shard_map/ppermute | solution.py:314
  85.6 6.8 %copy-start.13 = (f32[4,160,512]{2,1,0:T(8,128)}, f32[4,160,512]{2,1,0:T(8,128)S(1)}, u32[]{:S(2)}) copy-start(f32[4,160,512]{2,1,0:T(8,128)S(1)} %convert_add_fusion.1) | copy-start | bytes 3932164
  85.7 8.3 %collective-permute-start.15 = (bf16[2,160,512]{2,1,0:T(8,128)(2,1)S(1)}, bf16[2,160,512]{2,1,0:T(8,128)(2,1)}, u32[]{:S(2)}, u32[]{:S(2)}) collective-permute-start(bf16[2,160,512]{2,1,0:T(8,128)(2,1)S(1)} %fusion.9.after_b_ref), channel_id=1, source_target_pairs={{0,4},{4,0},{8,12},{12,8},{16,20},{20,16},{24,28},{28,24},{1,5},{5... | collective-permute-start | bytes 983048 | tf_op jit(solution)/shard_map/ppermute | solution.py:314
  92.4 1.6 %collective-permute-start.16 = (f32[2,20,128]{2,1,0:T(8,128)S(1)}, f32[2,20,128]{2,1,0:T(8,128)S(1)}, u32[]{:S(2)}, u32[]{:S(2)}) collective-permute-start(f32[2,20,128]{2,1,0:T(8,128)S(1)} %get-tuple-element.79), channel_id=1, source_target_pairs={{0,2},{2,0},{1,3},{3,1},{4,6},{6,4},{5,7},{7,5},{8,10},{10,8},{9,1... | collective-permute-start | bytes 61448 | tf_op jit(solution)/shard_map/ppermute | solution.py:314
  92.5 15.7 %collective-permute-start.19 = (f32[512,256]{1,0:T(8,128)S(1)}, f32[512,256]{1,0:T(8,128)}, u32[]{:S(2)}, u32[]{:S(2)}) collective-permute-start(f32[512,256]{1,0:T(8,128)S(1)} %get-tuple-element.82), channel_id=1, source_target_pairs={{0,1},{1,0},{2,3},{3,2},{4,5},{5,4},{6,7},{7,6},{8,9},{9,8},{10,11... | collective-permute-start | bytes 1572872 | tf_op jit(solution)/shard_map/ppermute | solution.py:314
  97.4 18.3 %collective-permute-start.18 = (bf16[160,512]{1,0:T(8,128)(2,1)S(1)}, bf16[160,512]{1,0:T(8,128)(2,1)S(1)}, u32[]{:S(2)}, u32[]{:S(2)}) collective-permute-start(bf16[160,512]{1,0:T(8,128)(2,1)S(1)} %fusion.14), channel_id=1, source_target_pairs={{0,16},{4,20},{8,24},{12,28},{16,0},{20,4},{24,8},{28,12},{1,17},{... | collective-permute-start | bytes 491528 | tf_op jit(solution)/shard_map/ppermute | solution.py:314
  99.5 20.8 %copy-start.15 = (f32[2,160,768]{2,1,0:T(8,128)S(1)}, f32[2,160,768]{2,1,0:T(8,128)}, u32[]{:S(2)}) copy-start(f32[2,160,768]{2,1,0:T(8,128)} %copy-done.14) | copy-start | bytes 2949124
  99.5 20.8 %collective-permute-start.17 = (bf16[160,768]{1,0:T(8,128)(2,1)S(1)}, bf16[160,768]{1,0:T(8,128)(2,1)S(1)}, u32[]{:S(2)}, u32[]{:S(2)}) collective-permute-start(bf16[160,768]{1,0:T(8,128)(2,1)S(1)} %fusion.12), channel_id=1, source_target_pairs={{0,16},{4,20},{8,24},{12,28},{16,0},{20,4},{24,8},{28,12},{1,17},{... | collective-permute-start | bytes 737288 | tf_op jit(solution)/shard_map/ppermute | solution.py:314
  103.3 17.9 %all-to-all-start = ((f32[8,2,20,128]{3,1,2,0:T(2,128)}), f32[8,2,20,128]{3,1,2,0:T(2,128)S(1)}, u32[]{:S(2)}, u32[]{:S(2)}) async-start(f32[8,2,20,128]{3,1,2,0:T(2,128)} %broadcast_in_dim.73), calls=%async_computation | async-start | bytes 327680 | tf_op jit(solution)/shard_map/all_to_all | solution.py:645
  108.1 12.2 %copy-start.17 = (f32[2,160,512]{2,1,0:T(8,128)S(1)}, f32[2,160,512]{2,1,0:T(8,128)}, u32[]{:S(2)}) copy-start(f32[2,160,512]{2,1,0:T(8,128)} %copy-done.16) | copy-start | bytes 1966084
  (9 other events, 13.1 us)

commit v6 on v5

--- a/solution.py
+++ b/solution.py
@@ -13,7 +13,7 @@
 NN = (((1,), (0,)), ((), ()))
 NT = (((1,), (1,)), ((), ()))
 TN = (((0,), (0,)), ((), ()))
-VMEM_BYTES = 32 * 1024 * 1024
+VMEM_BYTES = 16 * 1024 * 1024
 COST_SCALE = 20
 FIRST_VMEM_BYTES = 58 * 1024 * 1024
 
@@ -178,25 +178,20 @@
     mixed_ref[...] = mixed.reshape(x_ref.shape).astype(BF16)
 
 
-def cotan_first_kernel(flag_ref, mine_ref, other_ref, g_ref, after_ref, out_ref):
+def cotan_first_kernel(flag_ref, mine_ref, other_ref, g_ref, after_ref, out_ref, later_ref):
     @pl.when(flag_ref[0] == 1)
     def _():
         out_ref[...] = dot(mine_ref[...], g_ref[...])
+        later_ref[...] = other_ref[...]
 
     @pl.when(flag_ref[0] == 0)
     def _():
         out_ref[...] = dot(other_ref[...], g_ref[...])
-
-
-def cotan_kernel(flag_ref, mine_ref, other_ref, g_ref, first_ref, c_ref, grown_ref, after_ref, cotan_ref, local_ref, sum_ref):
-    @pl.when(flag_ref[0] == 0)
-    def _():
-        sum_ref[...] = first_ref[...] + dot(mine_ref[...], g_ref[...])
-
-    @pl.when(flag_ref[0] == 1)
-    def _():
-        sum_ref[...] = first_ref[...] + dot(other_ref[...], g_ref[...])
-
+        later_ref[...] = mine_ref[...]
+
+
+def cotan_kernel(weights_ref, g_ref, first_ref, c_ref, grown_ref, after_ref, cotan_ref, local_ref, sum_ref):
+    sum_ref[...] = first_ref[...] + dot(weights_ref[...], g_ref[...])
     cotan = sum_ref[...].astype(BF16)
     cotan_ref[...] = cotan
     group = cotan.shape[0] // HEAD_DIM
@@ -458,34 +453,28 @@
     wide_block = wide_group * HEAD_DIM
     wide_grid = (heads // wide_group,)
 
-    def weights(wanted):
-        return pl.BlockSpec(
-            (wide_block, half_features), lambda i, flag: (jnp.where(flag[0] == wanted, i, 0), 0)
-        )
-
     first = lambda after: call(
         cotan_first_kernel,
         wide_grid,
-        [weights(1), weights(0), whole(half_features, length), ANY],
-        by_row(wide_block, length),
-        jax.ShapeDtypeStruct((channels, length), F32),
+        [by_row(wide_block, half_features)] * 2 + [whole(half_features, length), ANY],
+        [by_row(wide_block, length), by_row(wide_block, half_features)],
+        [jax.ShapeDtypeStruct((channels, length), F32), jax.ShapeDtypeStruct((channels, half_features), BF16)],
         flops=2 * channels * half_features * length,
         prefetch=1,
     )(flag, w_out, w_other, g_first, after)
-    cotans = lambda g_second, first, after: call(
+    cotans = lambda g_second, first, later, after: call(
         cotan_kernel,
         wide_grid,
-        [weights(0), weights(1)]
+        [by_row(wide_block, half_features)]
         + [whole(half_features, length), by_row(wide_block, length), whole(length, n_state), by_row(wide_group, 1, length), ANY],
         [by_row(wide_block, length), by_row(wide_block, n_state)],
         [jax.ShapeDtypeStruct((channels, length), BF16), jax.ShapeDtypeStruct((channels, n_state), F32)],
         [pltpu.VMEM((wide_block, length), F32)],
         flops=2 * channels * length * (half_features + 2 * n_state),
-        prefetch=1,
-    )(flag, w_out, w_other, g_second, first, c, grown, after)
+    )(later, g_second, first, c, grown, after)
 
     beside = {1: first}
-    (first_sum,), state_in, give = pair_scan(payload, mine, total, n_seq, False, beside)
+    ((first_sum, later),), state_in, give = pair_scan(payload, mine, total, n_seq, False, beside)
 
     inner, skips = inners(give)
 
@@ -547,7 +536,7 @@
 
     g_mine = chosen(my_dp)
     g_other = swap(chosen(1 - my_dp), "dp", 2, 1)
-    y_cotan, local_cotan = cotans(g_second, first_sum, mixed)
+    y_cotan, local_cotan = cotans(g_second, first_sum, later, mixed)
 
     def keeping(s, after):
         return terms(*held["mixed"], s, orders[s][0], my_bit(orders[s][0]), F32, after)

time: 123 us -> 122 us (level)
    unnamed x40 -> x44, local copies, waits for them, and re-layouts: 3.5 us -> 3.52 us
where the time goes in v6:
time: 122 us; the launch traced here: 121 us
  starting transfers between devices  40.7 us (33%)
  Pallas kernels  35 us (29%)
  waiting for transfers between devices  30.2 us (25%)
  other arithmetic  7.01 us (6%)
  local copies, waits for them, and re-layouts  6.97 us (6%)
  between operations  1.41 us (1%)
    ppermute x16, starting transfers between devices, swap(): return lax.ppermute(value, axis, [(i, i ^ bit) for i in range(size)])  24.3 us
    ppermute x16, waiting for transfers between devices, swap(): return lax.ppermute(value, axis, [(i, i ^ bit) for i in range(size)])  23.4 us
    ppermute x4, starting transfers between devices, shifted(): return lax.ppermute(value, axis, pairs)  11.6 us
    ppermute x4, waiting for transfers between devices, shifted(): return lax.ppermute(value, axis, pairs)  6.79 us
    pallas_call x1, Pallas kernels, per_device(): call(back_kernel, grid, [by_row(block, length)] * 3 + [by_row(block, n_st...  6.42 us
    pallas_call x4, Pallas kernels, terms(): call(terms_kernel, (sizes[stream] // unit,), [columns, columns, rows, row...  6.26 us
    pallas_call x1, Pallas kernels, per_device(): call(last_kernel, grid, [by_row(block, length)] * 3 + [by_row(block, n_st...  5.24 us
    all_to_all x1, starting transfers between devices, per_device(): lax.all_to_all(jnp.broadcast_to(small, (n_seq,) + small.shape), 'seq', 0, 0)  4.79 us
  transfers between devices with their start and end apart: 21, of which 10 were waited for; matrix products, arithmetic and copies ran while one was open for 8% of the time, Pallas kernels for 29%

profile of v6, /device:TPU:0, one launch (start us, length us, event | category | flops | bytes accessed | tf_op | source)
XLA Modules:
  0.0 121.3 jit_solution(10809417499972642884)
XLA Ops:
  1.2 4.2 %shard_map.143 = (f32[20,1,512]{2,1,0:T(1,128)}, f32[20,1,512]{2,1,0:T(1,128)}, f32[20,128]{1,0:T(8,128)}, f32[1280,128]{1,0:T(8,128)}, bf16[21,32,128]{2,1,0:T(8,128)(2,1)}, /*index=5*/f32[20,32,128]{2,1,0:T(8,128)}) custom-call(s32[1]{0:T(128)} %bitcast.3.upper_ref, bf16[1280,512]{1,0:T(8,128)(2,1)} %bitcast.192, bf16[512,128]{1,0:T(8,128)(2,1)} %bitcast.206, ...), custom_call_target="tpu_custom_call" | custom-call | flops 6710886400 | bytes 80000000 | tf_op jit(solution)/shard_map/pallas_call | solution.py:416
  5.4 2.6 %collective-permute-start = (bf16[21,32,128]{2,1,0:T(8,128)(2,1)}, bf16[21,32,128]{2,1,0:T(8,128)(2,1)S(1)}, u32[]{:S(2)}, u32[]{:S(2)}) collective-permute-start(bf16[21,32,128]{2,1,0:T(8,128)(2,1)} %get-tuple-element.54), channel_id=1, source_target_pairs={{0,4},{4,0},{8,12},{12,8},{16,20},{20,16},{24,28},{28,24},{1,5},{5... | collective-permute-start | bytes 516104 | tf_op jit(solution)/shard_map/ppermute | solution.py:309
  7.9 1.5 %collective-permute-start.5 = (bf16[1280,512]{1,0:T(8,128)(2,1)S(1)}, bf16[1280,512]{1,0:T(8,128)(2,1)S(1)}, u32[]{:S(2)}, u32[]{:S(2)}) collective-permute-start(bf16[1280,512]{1,0:T(8,128)(2,1)S(1)} %bitcast.180), channel_id=1, source_target_pairs={{0,1},{1,0},{2,3},{3,2},{4,5},{5,4},{6,7},{7,6},{8,9},{9,8},{10,11... | collective-permute-start | bytes 3932168 | tf_op jit(solution)/shard_map/ppermute | solution.py:309
  10.5 2.7 %collective-permute-done = bf16[21,32,128]{2,1,0:T(8,128)(2,1)S(1)} collective-permute-done((bf16[21,32,128]{2,1,0:T(8,128)(2,1)}, bf16[21,32,128]{2,1,0:T(8,128)(2,1)S(1)}, u32[]{:S(2)}, u32[]{:S(2)}) %collective-permute-start) | collective-permute-done | bytes 172064 | tf_op jit(solution)/shard_map/ppermute | solution.py:309
  13.4 3.7 %collective-permute-start.1 = (bf16[21,32,128]{2,1,0:T(8,128)(2,1)S(1)}, bf16[21,32,128]{2,1,0:T(8,128)(2,1)S(1)}, u32[]{:S(2)}, u32[]{:S(2)}) collective-permute-start(bf16[21,32,128]{2,1,0:T(8,128)(2,1)S(1)} %pad_maximum_fusion.4.after_ref), channel_id=1, source_target_pairs={{0,8},{4,12},{8,16},{12,20},{16,24},{20,28},{1,9},{5,13},{9,17},{1... | collective-permute-start | bytes 516104 | tf_op jit(solution)/shard_map/ppermute | solution.py:314
  17.2 3.6 %shard_map.144 = (f32[1280,512]{1,0:T(8,128)S(1)}, bf16[1280,1280]{1,0:T(8,128)(2,1)S(1)}) custom-call(s32[1]{0:T(128)} %bitcast.10.flag_ref, bf16[1280,1280]{1,0:T(8,128)(2,1)S(1)} %copy-done.1, bf16[1280,1280]{1,0:T(8,128)(2,1)} %collective-permute-done.2.other_ref, bf16[1280,512]{1,0:T(8,128)(2,1)S(1)} %bitcast.182, ...), custom_call_target="tpu_custom_call" | custom-call | flops 33554432000 | bytes 80000000 | tf_op jit(solution)/shard_map/pallas_call | solution.py:456
  21.1 5.1 %collective-permute-start.3 = (bf16[21,32,128]{2,1,0:T(8,128)(2,1)S(1)}, bf16[21,32,128]{2,1,0:T(8,128)(2,1)S(1)}, u32[]{:S(2)}, u32[]{:S(2)}) collective-permute-start(bf16[21,32,128]{2,1,0:T(8,128)(2,1)S(1)} %pad_maximum_fusion.5), channel_id=1, source_target_pairs={{0,16},{4,20},{8,24},{12,28},{1,17},{5,21},{9,25},{13,29},{2,18},{... | collective-permute-start | bytes 516104 | tf_op jit(solution)/shard_map/ppermute | solution.py:314
  26.3 2.9 %collective-permute-done.3 = bf16[21,32,128]{2,1,0:T(8,128)(2,1)S(1)} collective-permute-done((bf16[21,32,128]{2,1,0:T(8,128)(2,1)S(1)}, bf16[21,32,128]{2,1,0:T(8,128)(2,1)S(1)}, u32[]{:S(2)}, u32[]{:S(2)}) %collective-permute-start.3) | collective-permute-done | bytes 172064 | tf_op jit(solution)/shard_map/ppermute | solution.py:314
  29.3 1.6 %collective-permute-start.4 = (bf16[20,32,128]{2,1,0:T(8,128)(2,1)S(1)}, bf16[20,32,128]{2,1,0:T(8,128)(2,1)S(1)}, u32[]{:S(2)}, u32[]{:S(2)}) collective-permute-start(bf16[20,32,128]{2,1,0:T(8,128)(2,1)S(1)} %select_convert_fusion.4.after_ref), channel_id=1, source_target_pairs={{0,4},{4,0},{8,12},{12,8},{16,20},{20,16},{24,28},{28,24},{1,5},{5... | collective-permute-start | bytes 491528 | tf_op jit(solution)/shard_map/ppermute | solution.py:309
  30.9 2.8 %shard_map.145 = (f32[1280,512]{1,0:T(8,128)S(1)}, f32[20,1,512]{2,1,0:T(1,128)S(1)}) custom-call(bf16[1280,512]{1,0:T(8,128)(2,1)S(1)} %bitcast.193, bf16[512,128]{1,0:T(8,128)(2,1)S(1)} %bitcast.207, bf16[512,128]{1,0:T(8,128)(2,1)S(1)} %bitcast.202, f32[20,1,512]{2,1,0:T(1,128)S(1)} %copy-done.13, f32[1,20]{1,0:T(1,128)S(1)} %bitcast.212, ...), custom_call_target="tpu_custom_call" | custom-call | flops 33554432000 | bytes 80000000 | tf_op jit(solution)/shard_map/pallas_call | solution.py:439
  35.1 2.8 %shard_map.146.after_ref.m0_ref = bf16[1280,512]{1,0:T(8,128)(2,1)} custom-call(f32[1280,512]{1,0:T(8,128)S(1)} %get-tuple-element.59.inner_ref, bf16[1280,128]{1,0:T(8,128)(2,1)S(1)} %bitcast.188, bf16[512,128]{1,0:T(8,128)(2,1)S(1)} %bitcast.203, bf16[1280,512]{1,0:T(8,128)(2,1)S(1)} %bitcast.194, f32[20,1,512]{2,1,0:T(1,128)S(1)} %copy-done.10, ...), custom_call_target="tpu_custom_call" | custom-call | flops 3355443200 | bytes 80000000 | tf_op jit(solution)/shard_map/pallas_call | solution.py:482
  40.3 3.7 %shard_map.147 = (bf16[1280,512]{1,0:T(8,128)(2,1)S(1)}, f32[1280,128]{1,0:T(8,128)S(1)}) custom-call(bf16[1280,1280]{1,0:T(8,128)(2,1)S(1)} %get-tuple-element.62.weights_ref, bf16[1280,512]{1,0:T(8,128)(2,1)S(1)} %collective-permute-done.5.g_ref, f32[1280,512]{1,0:T(8,128)S(1)} %get-tuple-element.64.first_ref, bf16[512,128]{1,0:T(8,128)(2,1)S(1)} %bitcast.204, ...), custom_call_target="tpu_custom_call" | custom-call | flops 40265318400 | bytes 80000000 | tf_op jit(solution)/shard_map/pallas_call | solution.py:465
  44.8 1.8 %shard_map.148.after_ref = bf16[4,160,768]{2,1,0:T(8,128)(2,1)S(1)} custom-call(s32[1]{0:T(128)} %bitcast.22.pick_ref, bf16[4,2,1,160,512]{4,3,2,1,0:T(8,128)(2,1)S(1)} %bitcast.184, bf16[4,2,1,160,512]{4,3,2,1,0:T(8,128)(2,1)S(1)} %bitcast.198, bf16[1280,512]{1,0:T(8,128)(2,1)S(1)} %copy-done.3, bf16[1280,512]{1,0:T(8,128)(2,1)S(1)} %collective-permute-done.8.m1_ref, ...), custom_call_target="tpu_custom_call" | custom-call | flops 20132659200 | bytes 80000000 | tf_op jit(solution)/shard_map/pallas_call | solution.py:510
  46.6 1.5 %collective-permute-start.11 = (bf16[4,160,768]{2,1,0:T(8,128)(2,1)S(1)}, bf16[4,160,768]{2,1,0:T(8,128)(2,1)S(1)}, u32[]{:S(2)}, u32[]{:S(2)}) collective-permute-start(bf16[4,160,768]{2,1,0:T(8,128)(2,1)S(1)} %shard_map.148.after_ref), channel_id=1, source_target_pairs={{0,4},{4,0},{8,12},{12,8},{16,20},{20,16},{24,28},{28,24},{1,5},{5... | collective-permute-start | bytes 2949128 | tf_op jit(solution)/shard_map/ppermute | solution.py:309
  48.2 1.8 %shard_map.149 = f32[4,160,768]{2,1,0:T(8,128)S(1)} custom-call(s32[1]{0:T(128)} %bitcast.31.pick_ref, bf16[4,2,1,160,512]{4,3,2,1,0:T(8,128)(2,1)S(1)} %bitcast.185, bf16[4,2,1,160,512]{4,3,2,1,0:T(8,128)(2,1)S(1)} %bitcast.199, bf16[1280,512]{1,0:T(8,128)(2,1)S(1)} %copy-done.3, bf16[1280,512]{1,0:T(8,128)(2,1)S(1)} %collective-permute-done.8.m1_ref, ...), custom_call_target="tpu_custom_call" | custom-call | flops 20132659200 | bytes 80000000 | tf_op jit(solution)/shard_map/pallas_call | solution.py:510
  50.5 1.3 %collective-permute-start.9 = (bf16[21,32,128]{2,1,0:T(8,128)(2,1)S(1)}, bf16[21,32,128]{2,1,0:T(8,128)(2,1)S(1)}, u32[]{:S(2)}, u32[]{:S(2)}) collective-permute-start(bf16[21,32,128]{2,1,0:T(8,128)(2,1)S(1)} %pad_maximum_fusion.7.after_ref), channel_id=1, source_target_pairs={{8,0},{12,4},{16,8},{20,12},{24,16},{28,20},{9,1},{13,5},{17,9},{2... | collective-permute-start | bytes 516104 | tf_op jit(solution)/shard_map/ppermute | solution.py:314
  51.8 1.3 %shard_map.150 = bf16[4,160,512]{2,1,0:T(8,128)(2,1)S(1)} custom-call(s32[1]{0:T(128)} %bitcast.36.pick_ref, bf16[2,2,2,160,512]{4,3,2,1,0:T(8,128)(2,1)S(1)} %bitcast.186, bf16[2,2,2,160,512]{4,3,2,1,0:T(8,128)(2,1)S(1)} %bitcast.200, bf16[1280,512]{1,0:T(8,128)(2,1)S(1)} %copy-done.3, bf16[1280,512]{1,0:T(8,128)(2,1)S(1)} %collective-permute-done.8.m1_ref, ...), custom_call_target="tpu_custom_call" | custom-call | flops 13421772800 | bytes 80000000 | tf_op jit(solution)/shard_map/pallas_call | solution.py:510
  53.1 6.3 %collective-permute-start.12 = (bf16[4,160,512]{2,1,0:T(8,128)(2,1)S(1)}, bf16[4,160,512]{2,1,0:T(8,128)(2,1)S(1)}, u32[]{:S(2)}, u32[]{:S(2)}) collective-permute-start(bf16[4,160,512]{2,1,0:T(8,128)(2,1)S(1)} %shard_map.150), channel_id=1, source_target_pairs={{0,8},{4,12},{8,0},{12,4},{16,24},{20,28},{24,16},{28,20},{1,9},{5... | collective-permute-start | bytes 1966088 | tf_op jit(solution)/shard_map/ppermute | solution.py:309
  59.5 3.9 %collective-permute-done.9 = bf16[21,32,128]{2,1,0:T(8,128)(2,1)S(1)} collective-permute-done((bf16[21,32,128]{2,1,0:T(8,128)(2,1)S(1)}, bf16[21,32,128]{2,1,0:T(8,128)(2,1)S(1)}, u32[]{:S(2)}, u32[]{:S(2)}) %collective-permute-start.9) | collective-permute-done | bytes 172064 | tf_op jit(solution)/shard_map/ppermute | solution.py:314
  63.6 1.5 %collective-permute-start.10 = (bf16[21,32,128]{2,1,0:T(8,128)(2,1)S(1)}, bf16[21,32,128]{2,1,0:T(8,128)(2,1)S(1)}, u32[]{:S(2)}, u32[]{:S(2)}) collective-permute-start(bf16[21,32,128]{2,1,0:T(8,128)(2,1)S(1)} %pad_maximum_fusion.8.after_ref), channel_id=1, source_target_pairs={{16,0},{20,4},{24,8},{28,12},{17,1},{21,5},{25,9},{29,13},{18,2},{... | collective-permute-start | bytes 516104 | tf_op jit(solution)/shard_map/ppermute | solution.py:314
  65.1 6.4 %shard_map.152 = (f32[1280,512]{1,0:T(8,128)S(1)}, f32[20,1,512]{2,1,0:T(1,128)S(1)}, f32[512,128]{1,0:T(8,128)S(1)}, f32[512,128]{1,0:T(8,128)S(1)}) custom-call(bf16[1280,512]{1,0:T(8,128)(2,1)S(1)} %bitcast.195, bf16[1280,512]{1,0:T(8,128)(2,1)S(1)} %get-tuple-element.65.cotan_ref, f32[1280,512]{1,0:T(8,128)S(1)} %get-tuple-element.59.inner_ref, ...), custom_call_target="tpu_custom_call" | custom-call | flops 67108864000 | bytes 80000000 | tf_op jit(solution)/shard_map/pallas_call | solution.py:561
  71.5 1.3 %shard_map.151 = f32[4,160,512]{2,1,0:T(8,128)S(1)} custom-call(s32[1]{0:T(128)} %bitcast.41.pick_ref, bf16[2,2,2,160,512]{4,3,2,1,0:T(8,128)(2,1)S(1)} %bitcast.187, bf16[2,2,2,160,512]{4,3,2,1,0:T(8,128)(2,1)S(1)} %bitcast.201, bf16[1280,512]{1,0:T(8,128)(2,1)S(1)} %copy-done.3, bf16[1280,512]{1,0:T(8,128)(2,1)S(1)} %collective-permute-done.8.m1_ref, ...), custom_call_target="tpu_custom_call" | custom-call | flops 13421772800 | bytes 80000000 | tf_op jit(solution)/shard_map/pallas_call | solution.py:510
  72.8 6.9 %collective-permute-done.12 = bf16[4,160,512]{2,1,0:T(8,128)(2,1)S(1)} collective-permute-done((bf16[4,160,512]{2,1,0:T(8,128)(2,1)S(1)}, bf16[4,160,512]{2,1,0:T(8,128)(2,1)S(1)}, u32[]{:S(2)}, u32[]{:S(2)}) %collective-permute-start.12) | collective-permute-done | bytes 655392 | tf_op jit(solution)/shard_map/ppermute | solution.py:309
  79.9 1.6 %collective-permute-start.13 = (bf16[20,32,128]{2,1,0:T(8,128)(2,1)S(1)}, bf16[20,32,128]{2,1,0:T(8,128)(2,1)S(1)}, u32[]{:S(2)}, u32[]{:S(2)}) collective-permute-start(bf16[20,32,128]{2,1,0:T(8,128)(2,1)S(1)} %select_convert_fusion.1), channel_id=1, source_target_pairs={{0,4},{4,0},{8,12},{12,8},{16,20},{20,16},{24,28},{28,24},{1,5},{5... | collective-permute-start | bytes 491528 | tf_op jit(solution)/shard_map/ppermute | solution.py:309
  81.8 2.8 %collective-permute-start.14 = (bf16[2,160,768]{2,1,0:T(8,128)(2,1)S(1)}, bf16[2,160,768]{2,1,0:T(8,128)(2,1)}, u32[]{:S(2)}, u32[]{:S(2)}) collective-permute-start(bf16[2,160,768]{2,1,0:T(8,128)(2,1)S(1)} %fusion.after_a_ref), channel_id=1, source_target_pairs={{0,8},{4,12},{8,0},{12,4},{16,24},{20,28},{24,16},{28,20},{1,9},{5... | collective-permute-start | bytes 1474568 | tf_op jit(solution)/shard_map/ppermute | solution.py:309
  86.5 5.2 %shard_map.153 = (bf16[1280,512]{1,0:T(8,128)(2,1)}, f32[20,1,512]{2,1,0:T(1,128)}, f32[2,20,128]{2,1,0:T(8,128)S(1)}, f32[512,256]{1,0:T(8,128)S(1)}) custom-call(bf16[1280,512]{1,0:T(8,128)(2,1)S(1)} %bitcast.196, bf16[1280,512]{1,0:T(8,128)(2,1)S(1)} %get-tuple-element.65.cotan_ref, f32[1280,512]{1,0:T(8,128)S(1)} %get-tuple-element.73.outer_ref, ...), custom_call_target="tpu_custom_call" | custom-call | flops 10066329600 | bytes 80000000 | tf_op jit(solution)/shard_map/pallas_call | solution.py:590
  91.7 1.6 %collective-permute-start.19 = (f32[512,256]{1,0:T(8,128)S(1)}, f32[512,256]{1,0:T(8,128)}, u32[]{:S(2)}, u32[]{:S(2)}) collective-permute-start(f32[512,256]{1,0:T(8,128)S(1)} %get-tuple-element.88), channel_id=1, source_target_pairs={{0,1},{1,0},{2,3},{3,2},{4,5},{5,4},{6,7},{7,6},{8,9},{9,8},{10,11... | collective-permute-start | bytes 1572872 | tf_op jit(solution)/shard_map/ppermute | solution.py:309
  94.6 1.3 %bitcast_add_fusion.1 = f32[2,160,512]{2,1,0:T(8,128)S(1)} fusion(bf16[2,160,512]{2,1,0:T(8,128)(2,1)} %collective-permute-done.15, f32[2,2,160,512]{3,2,1,0:T(8,128)} %bitcast.218, s32[]{:T(128)S(6)} %select_n.225), kind=kLoop, calls=%fused_computation.7 | loop fusion | flops 327680 | bytes 1638404 | tf_op jit(solution)/shard_map/add | solution.py:638
  98.8 3.0 %collective-permute-start.17 = (bf16[160,768]{1,0:T(8,128)(2,1)S(1)}, bf16[160,768]{1,0:T(8,128)(2,1)S(1)}, u32[]{:S(2)}, u32[]{:S(2)}) collective-permute-start(bf16[160,768]{1,0:T(8,128)(2,1)S(1)} %fusion.12), channel_id=1, source_target_pairs={{0,16},{4,20},{8,24},{12,28},{16,0},{20,4},{24,8},{28,12},{1,17},{... | collective-permute-start | bytes 737288 | tf_op jit(solution)/shard_map/ppermute | solution.py:309
  102.6 4.8 %all-to-all-start = ((f32[8,2,20,128]{3,1,2,0:T(2,128)}), f32[8,2,20,128]{3,1,2,0:T(2,128)S(1)}, u32[]{:S(2)}, u32[]{:S(2)}) async-start(f32[8,2,20,128]{3,1,2,0:T(2,128)} %broadcast_in_dim.73), calls=%async_computation | async-start | bytes 327680 | tf_op jit(solution)/shard_map/all_to_all | solution.py:634
  109.2 5.8 %collective-permute-done.18 = bf16[160,512]{1,0:T(8,128)(2,1)S(1)} collective-permute-done((bf16[160,512]{1,0:T(8,128)(2,1)S(1)}, bf16[160,512]{1,0:T(8,128)(2,1)S(1)}, u32[]{:S(2)}, u32[]{:S(2)}) %collective-permute-start.18) | collective-permute-done | bytes 163872 | tf_op jit(solution)/shard_map/ppermute | solution.py:309
  115.1 4.5 %collective-permute-done.17 = bf16[160,768]{1,0:T(8,128)(2,1)S(1)} collective-permute-done((bf16[160,768]{1,0:T(8,128)(2,1)S(1)}, bf16[160,768]{1,0:T(8,128)(2,1)S(1)}, u32[]{:S(2)}, u32[]{:S(2)}) %collective-permute-start.17) | collective-permute-done | bytes 245792 | tf_op jit(solution)/shard_map/ppermute | solution.py:309
  (130 shorter events, 18.1 us)
Async XLA Ops:
  0.6 16.5 %collective-permute-start.2 = (bf16[1280,1280]{1,0:T(8,128)(2,1)}, bf16[1280,1280]{1,0:T(8,128)(2,1)}, u32[]{:S(2)}, u32[]{:S(2)}) collective-permute-start(bf16[1280,1280]{1,0:T(8,128)(2,1)} %mine_ref.1), channel_id=1, source_target_pairs={{0,2},{2,0},{1,3},{3,1},{4,6},{6,4},{5,7},{7,5},{8,10},{10,8},{9,1... | collective-permute-start | bytes 9830408 | tf_op jit(solution)/shard_map/ppermute | solution.py:309
  1.2 6.8 %copy-start = (bf16[1,1280,512]{2,1,0:T(8,128)(2,1)S(1)}, bf16[1,1280,512]{2,1,0:T(8,128)(2,1)}, u32[]{:S(2)}) copy-start(bf16[1,1280,512]{2,1,0:T(8,128)(2,1)} %param.15) | copy-start | bytes 3932164
  5.4 7.8 %collective-permute-start = (bf16[21,32,128]{2,1,0:T(8,128)(2,1)}, bf16[21,32,128]{2,1,0:T(8,128)(2,1)S(1)}, u32[]{:S(2)}, u32[]{:S(2)}) collective-permute-start(bf16[21,32,128]{2,1,0:T(8,128)(2,1)} %get-tuple-element.54), channel_id=1, source_target_pairs={{0,4},{4,0},{8,12},{12,8},{16,20},{20,16},{24,28},{28,24},{1,5},{5... | collective-permute-start | bytes 516104 | tf_op jit(solution)/shard_map/ppermute | solution.py:309
  7.9 30.9 %collective-permute-start.5 = (bf16[1280,512]{1,0:T(8,128)(2,1)S(1)}, bf16[1280,512]{1,0:T(8,128)(2,1)S(1)}, u32[]{:S(2)}, u32[]{:S(2)}) collective-permute-start(bf16[1280,512]{1,0:T(8,128)(2,1)S(1)} %bitcast.180), channel_id=1, source_target_pairs={{0,1},{1,0},{2,3},{3,2},{4,5},{5,4},{6,7},{7,6},{8,9},{9,8},{10,11... | collective-permute-start | bytes 3932168 | tf_op jit(solution)/shard_map/ppermute | solution.py:309
  10.3 3.0 %copy-start.14 = (f32[20,32,128]{2,1,0:T(8,128)S(1)}, f32[20,32,128]{2,1,0:T(8,128)}, u32[]{:S(2)}) copy-start(f32[20,32,128]{2,1,0:T(8,128)} %get-tuple-element.55) | copy-start | bytes 983044
  10.3 6.9 %copy-start.1 = (bf16[1280,1280]{1,0:T(8,128)(2,1)S(1)}, bf16[1280,1280]{1,0:T(8,128)(2,1)}, u32[]{:S(2)}) copy-start(bf16[1280,1280]{1,0:T(8,128)(2,1)} %mine_ref.1) | copy-start | bytes 9830404
  13.4 7.5 %collective-permute-start.1 = (bf16[21,32,128]{2,1,0:T(8,128)(2,1)S(1)}, bf16[21,32,128]{2,1,0:T(8,128)(2,1)S(1)}, u32[]{:S(2)}, u32[]{:S(2)}) collective-permute-start(bf16[21,32,128]{2,1,0:T(8,128)(2,1)S(1)} %pad_maximum_fusion.4.after_ref), channel_id=1, source_target_pairs={{0,8},{4,12},{8,16},{12,20},{16,24},{20,28},{1,9},{5,13},{9,17},{1... | collective-permute-start | bytes 516104 | tf_op jit(solution)/shard_map/ppermute | solution.py:314
  20.8 10.1 %copy-start.2 = (bf16[1,1280,512]{2,1,0:T(8,128)(2,1)S(1)}, bf16[1,1280,512]{2,1,0:T(8,128)(2,1)}, u32[]{:S(2)}) copy-start(bf16[1,1280,512]{2,1,0:T(8,128)(2,1)} %param.8) | copy-start | bytes 3932164
  20.8 10.1 %copy-start.4 = (bf16[1,512,128]{2,1,0:T(8,128)(2,1)S(1)}, bf16[1,512,128]{2,1,0:T(8,128)(2,1)}, u32[]{:S(2)}) copy-start(bf16[1,512,128]{2,1,0:T(8,128)(2,1)} %param.10) | copy-start | bytes 393220
  20.8 10.0 %copy-start.5 = (bf16[1,512,128]{2,1,0:T(8,128)(2,1)S(1)}, bf16[1,512,128]{2,1,0:T(8,128)(2,1)}, u32[]{:S(2)}) copy-start(bf16[1,512,128]{2,1,0:T(8,128)(2,1)} %param.9) | copy-start | bytes 393220
  20.9 10.0 %copy-start.7 = (f32[20]{0:T(128)S(1)}, f32[20]{0:T(128)}, u32[]{:S(2)}) copy-start(f32[20]{0:T(128)} %param.13) | copy-start | bytes 244
  20.9 10.0 %copy-start.13 = (f32[20,1,512]{2,1,0:T(1,128)S(1)}, f32[20,1,512]{2,1,0:T(1,128)}, u32[]{:S(2)}) copy-start(f32[20,1,512]{2,1,0:T(1,128)} %get-tuple-element.52.shrunk_ref) | copy-start | bytes 122884
  21.1 8.0 %collective-permute-start.3 = (bf16[21,32,128]{2,1,0:T(8,128)(2,1)S(1)}, bf16[21,32,128]{2,1,0:T(8,128)(2,1)S(1)}, u32[]{:S(2)}, u32[]{:S(2)}) collective-permute-start(bf16[21,32,128]{2,1,0:T(8,128)(2,1)S(1)} %pad_maximum_fusion.5), channel_id=1, source_target_pairs={{0,16},{4,20},{8,24},{12,28},{1,17},{5,21},{9,25},{13,29},{2,18},{... | collective-permute-start | bytes 516104 | tf_op jit(solution)/shard_map/ppermute | solution.py:314
  29.3 5.4 %collective-permute-start.4 = (bf16[20,32,128]{2,1,0:T(8,128)(2,1)S(1)}, bf16[20,32,128]{2,1,0:T(8,128)(2,1)S(1)}, u32[]{:S(2)}, u32[]{:S(2)}) collective-permute-start(bf16[20,32,128]{2,1,0:T(8,128)(2,1)S(1)} %select_convert_fusion.4.after_ref), channel_id=1, source_target_pairs={{0,4},{4,0},{8,12},{12,8},{16,20},{20,16},{24,28},{28,24},{1,5},{5... | collective-permute-start | bytes 491528 | tf_op jit(solution)/shard_map/ppermute | solution.py:309
  37.9 6.9 %collective-permute-start.8 = (bf16[1280,512]{1,0:T(8,128)(2,1)}, bf16[1280,512]{1,0:T(8,128)(2,1)S(1)}, u32[]{:S(2)}, u32[]{:S(2)}) collective-permute-start(bf16[1280,512]{1,0:T(8,128)(2,1)} %shard_map.146.after_ref.m0_ref), channel_id=1, source_target_pairs={{0,2},{2,0},{1,3},{3,1},{4,6},{6,4},{5,7},{7,5},{8,10},{10,8},{9,1... | collective-permute-start | bytes 3932168 | tf_op jit(solution)/shard_map/ppermute | solution.py:309
  39.1 5.7 %collective-permute-start.7 = (bf16[8,160,512]{2,1,0:T(8,128)(2,1)S(1)}, bf16[8,160,512]{2,1,0:T(8,128)(2,1)S(1)}, u32[]{:S(2)}, u32[]{:S(2)}) collective-permute-start(bf16[8,160,512]{2,1,0:T(8,128)(2,1)S(1)} %pad_maximum_fusion.1), channel_id=1, source_target_pairs={{0,2},{2,0},{1,3},{3,1},{4,6},{6,4},{5,7},{7,5},{8,10},{10,8},{9,1... | collective-permute-start | bytes 3932168 | tf_op jit(solution)/shard_map/ppermute | solution.py:309
  44.0 6.3 %collective-permute-start.6 = (bf16[21,32,128]{2,1,0:T(8,128)(2,1)S(1)}, bf16[21,32,128]{2,1,0:T(8,128)(2,1)S(1)}, u32[]{:S(2)}, u32[]{:S(2)}) collective-permute-start(bf16[21,32,128]{2,1,0:T(8,128)(2,1)S(1)} %pad_maximum_fusion.6.after_ref), channel_id=1, source_target_pairs={{0,4},{4,0},{8,12},{12,8},{16,20},{20,16},{24,28},{28,24},{1,5},{5... | collective-permute-start | bytes 516104 | tf_op jit(solution)/shard_map/ppermute | solution.py:309
  46.6 33.1 %collective-permute-start.11 = (bf16[4,160,768]{2,1,0:T(8,128)(2,1)S(1)}, bf16[4,160,768]{2,1,0:T(8,128)(2,1)S(1)}, u32[]{:S(2)}, u32[]{:S(2)}) collective-permute-start(bf16[4,160,768]{2,1,0:T(8,128)(2,1)S(1)} %shard_map.148.after_ref), channel_id=1, source_target_pairs={{0,4},{4,0},{8,12},{12,8},{16,20},{20,16},{24,28},{28,24},{1,5},{5... | collective-permute-start | bytes 2949128 | tf_op jit(solution)/shard_map/ppermute | solution.py:309
  50.5 12.8 %collective-permute-start.9 = (bf16[21,32,128]{2,1,0:T(8,128)(2,1)S(1)}, bf16[21,32,128]{2,1,0:T(8,128)(2,1)S(1)}, u32[]{:S(2)}, u32[]{:S(2)}) collective-permute-start(bf16[21,32,128]{2,1,0:T(8,128)(2,1)S(1)} %pad_maximum_fusion.7.after_ref), channel_id=1, source_target_pairs={{8,0},{12,4},{16,8},{20,12},{24,16},{28,20},{9,1},{13,5},{17,9},{2... | collective-permute-start | bytes 516104 | tf_op jit(solution)/shard_map/ppermute | solution.py:314
  53.1 26.6 %collective-permute-start.12 = (bf16[4,160,512]{2,1,0:T(8,128)(2,1)S(1)}, bf16[4,160,512]{2,1,0:T(8,128)(2,1)S(1)}, u32[]{:S(2)}, u32[]{:S(2)}) collective-permute-start(bf16[4,160,512]{2,1,0:T(8,128)(2,1)S(1)} %shard_map.150), channel_id=1, source_target_pairs={{0,8},{4,12},{8,0},{12,4},{16,24},{20,28},{24,16},{28,20},{1,9},{5... | collective-permute-start | bytes 1966088 | tf_op jit(solution)/shard_map/ppermute | solution.py:309
  63.6 9.2 %collective-permute-start.10 = (bf16[21,32,128]{2,1,0:T(8,128)(2,1)S(1)}, bf16[21,32,128]{2,1,0:T(8,128)(2,1)S(1)}, u32[]{:S(2)}, u32[]{:S(2)}) collective-permute-start(bf16[21,32,128]{2,1,0:T(8,128)(2,1)S(1)} %pad_maximum_fusion.8.after_ref), channel_id=1, source_target_pairs={{16,0},{20,4},{24,8},{28,12},{17,1},{21,5},{25,9},{29,13},{18,2},{... | collective-permute-start | bytes 516104 | tf_op jit(solution)/shard_map/ppermute | solution.py:314
  79.9 5.6 %collective-permute-start.13 = (bf16[20,32,128]{2,1,0:T(8,128)(2,1)S(1)}, bf16[20,32,128]{2,1,0:T(8,128)(2,1)S(1)}, u32[]{:S(2)}, u32[]{:S(2)}) collective-permute-start(bf16[20,32,128]{2,1,0:T(8,128)(2,1)S(1)} %select_convert_fusion.1), channel_id=1, source_target_pairs={{0,4},{4,0},{8,12},{12,8},{16,20},{20,16},{24,28},{28,24},{1,5},{5... | collective-permute-start | bytes 491528 | tf_op jit(solution)/shard_map/ppermute | solution.py:309
  81.8 12.8 %collective-permute-start.14 = (bf16[2,160,768]{2,1,0:T(8,128)(2,1)S(1)}, bf16[2,160,768]{2,1,0:T(8,128)(2,1)}, u32[]{:S(2)}, u32[]{:S(2)}) collective-permute-start(bf16[2,160,768]{2,1,0:T(8,128)(2,1)S(1)} %fusion.after_a_ref), channel_id=1, source_target_pairs={{0,8},{4,12},{8,0},{12,4},{16,24},{20,28},{24,16},{28,20},{1,9},{5... | collective-permute-start | bytes 1474568 | tf_op jit(solution)/shard_map/ppermute | solution.py:309
  84.9 6.9 %copy-start.15 = (f32[4,160,512]{2,1,0:T(8,128)}, f32[4,160,512]{2,1,0:T(8,128)S(1)}, u32[]{:S(2)}) copy-start(f32[4,160,512]{2,1,0:T(8,128)S(1)} %convert_add_fusion.1) | copy-start | bytes 3932164
  85.0 8.3 %collective-permute-start.15 = (bf16[2,160,512]{2,1,0:T(8,128)(2,1)S(1)}, bf16[2,160,512]{2,1,0:T(8,128)(2,1)}, u32[]{:S(2)}, u32[]{:S(2)}) collective-permute-start(bf16[2,160,512]{2,1,0:T(8,128)(2,1)S(1)} %fusion.9.after_b_ref), channel_id=1, source_target_pairs={{0,4},{4,0},{8,12},{12,8},{16,20},{20,16},{24,28},{28,24},{1,5},{5... | collective-permute-start | bytes 983048 | tf_op jit(solution)/shard_map/ppermute | solution.py:309
  91.7 1.6 %collective-permute-start.16 = (f32[2,20,128]{2,1,0:T(8,128)S(1)}, f32[2,20,128]{2,1,0:T(8,128)S(1)}, u32[]{:S(2)}, u32[]{:S(2)}) collective-permute-start(f32[2,20,128]{2,1,0:T(8,128)S(1)} %get-tuple-element.85), channel_id=1, source_target_pairs={{0,2},{2,0},{1,3},{3,1},{4,6},{6,4},{5,7},{7,5},{8,10},{10,8},{9,1... | collective-permute-start | bytes 61448 | tf_op jit(solution)/shard_map/ppermute | solution.py:309
  91.7 15.6 %collective-permute-start.19 = (f32[512,256]{1,0:T(8,128)S(1)}, f32[512,256]{1,0:T(8,128)}, u32[]{:S(2)}, u32[]{:S(2)}) collective-permute-start(f32[512,256]{1,0:T(8,128)S(1)} %get-tuple-element.88), channel_id=1, source_target_pairs={{0,1},{1,0},{2,3},{3,2},{4,5},{5,4},{6,7},{7,6},{8,9},{9,8},{10,11... | collective-permute-start | bytes 1572872 | tf_op jit(solution)/shard_map/ppermute | solution.py:309
  96.7 18.4 %collective-permute-start.18 = (bf16[160,512]{1,0:T(8,128)(2,1)S(1)}, bf16[160,512]{1,0:T(8,128)(2,1)S(1)}, u32[]{:S(2)}, u32[]{:S(2)}) collective-permute-start(bf16[160,512]{1,0:T(8,128)(2,1)S(1)} %fusion.14), channel_id=1, source_target_pairs={{0,16},{4,20},{8,24},{12,28},{16,0},{20,4},{24,8},{28,12},{1,17},{... | collective-permute-start | bytes 491528 | tf_op jit(solution)/shard_map/ppermute | solution.py:309
  98.8 20.8 %copy-start.17 = (f32[2,160,768]{2,1,0:T(8,128)S(1)}, f32[2,160,768]{2,1,0:T(8,128)}, u32[]{:S(2)}) copy-start(f32[2,160,768]{2,1,0:T(8,128)} %copy-done.16) | copy-start | bytes 2949124
  98.8 20.8 %collective-permute-start.17 = (bf16[160,768]{1,0:T(8,128)(2,1)S(1)}, bf16[160,768]{1,0:T(8,128)(2,1)S(1)}, u32[]{:S(2)}, u32[]{:S(2)}) collective-permute-start(bf16[160,768]{1,0:T(8,128)(2,1)S(1)} %fusion.12), channel_id=1, source_target_pairs={{0,16},{4,20},{8,24},{12,28},{16,0},{20,4},{24,8},{28,12},{1,17},{... | collective-permute-start | bytes 737288 | tf_op jit(solution)/shard_map/ppermute | solution.py:309
  102.6 17.9 %all-to-all-start = ((f32[8,2,20,128]{3,1,2,0:T(2,128)}), f32[8,2,20,128]{3,1,2,0:T(2,128)S(1)}, u32[]{:S(2)}, u32[]{:S(2)}) async-start(f32[8,2,20,128]{3,1,2,0:T(2,128)} %broadcast_in_dim.73), calls=%async_computation | async-start | bytes 327680 | tf_op jit(solution)/shard_map/all_to_all | solution.py:634
  107.3 12.3 %copy-start.19 = (f32[2,160,512]{2,1,0:T(8,128)S(1)}, f32[2,160,512]{2,1,0:T(8,128)}, u32[]{:S(2)}) copy-start(f32[2,160,512]{2,1,0:T(8,128)} %copy-done.18) | copy-start | bytes 1966084
  (11 other events, 16.0 us)

commit v7 on v6

--- a/solution.py
+++ b/solution.py
@@ -211,6 +211,12 @@
             for j in range(low):
                 product = dot(g0_ref[i, 0, j], m0_ref[...], NT) + dot(g1_ref[i, 0, j], m1_ref[...], NT)
                 out_ref[i * low + j] = product.astype(out_ref.dtype)
+
+
+def halve_kernel(pick_ref, sums_ref, kept_ref, sent_ref):
+    mine = pick_ref[0]
+    sent_ref[...] = sums_ref[1 - mine].astype(BF16)
+    kept_ref[...] = sums_ref[mine]
 
 
 def back_kernel(x_ref, cotan_ref, inner_ref, state_ref, b_ref, c_ref, grown_ref, shrunk_ref, after_ref,
@@ -639,6 +645,19 @@
         if done + 1 < n_bits:
             streams = [halve(pairs[s], orders[s][done + 1 :]) for s in (0, 1)]
             if done + 2 == n_bits:
+                value = my_bit(n_bits - 1).astype(jnp.int32).reshape(1)
+                streams = [
+                    call(
+                        halve_kernel,
+                        (1,),
+                        [whole(2, out_columns, sizes[s])],
+                        [whole(out_columns, sizes[s])] * 2,
+                        [jax.ShapeDtypeStruct((out_columns, sizes[s]), kind) for kind in (F32, BF16)],
+                        prefetch=1,
+                    )(value, pairs[s].reshape(2, out_columns, sizes[s]))
+                    for s in (0, 1)
+                ]
+            if done + 2 == n_bits:
                 small, _ = lax.optimization_barrier((small, [stream[1] for stream in streams]))
     small = jnp.sum(small[:, :, :, 0], axis=0)
     grad_w = jnp.concatenate(pairs, axis=1).T.astype(BF16)

time: 122 us -> 121 us (level)
  waiting for transfers between devices: 30.2 us -> 33.8 us
  local copies, waits for them, and re-layouts: 6.97 us -> 4.61 us
  other arithmetic: 7.01 us -> 5.05 us
    ppermute x16, waiting for transfers between devices: 23.4 us -> 26.5 us  [swap(): return lax.ppermute(value, axis, [(i, i ^ bit) for i in range(size)])]
    unnamed x44 -> x36, local copies, waits for them, and re-layouts: 3.52 us -> 1.31 us
  transfers between devices with their start and end apart: 21 -> 21, of which waited for: 10 -> 12; matrix products, arithmetic and copies ran while one was open for 8% -> 6% of each run, Pallas kernels for 29% -> 29%
where the time goes in v7:
time: 121 us
  starting transfers between devices  40.7 us (34%)
  Pallas kernels  35.2 us (29%)
  waiting for transfers between devices  33.8 us (28%)
  other arithmetic  5.05 us (4%)
  local copies, waits for them, and re-layouts  4.61 us (4%)
  between operations  1.36 us (1%)
    ppermute x16, waiting for transfers between devices, swap(): return lax.ppermute(value, axis, [(i, i ^ bit) for i in range(size)])  26.5 us
    ppermute x16, starting transfers between devices, swap(): return lax.ppermute(value, axis, [(i, i ^ bit) for i in range(size)])  24.2 us
    ppermute x4, starting transfers between devices, shifted(): return lax.ppermute(value, axis, pairs)  11.6 us
    ppermute x4, waiting for transfers between devices, shifted(): return lax.ppermute(value, axis, pairs)  6.79 us
    pallas_call x1, Pallas kernels, per_device(): call(back_kernel, grid, [by_row(block, length)] * 3 + [by_row(block, n_st...  6.41 us
    pallas_call x4, Pallas kernels, terms(): call(terms_kernel, (sizes[stream] // unit,), [columns, columns, rows, row...  6.23 us
    pallas_call x1, Pallas kernels, per_device(): call(last_kernel, grid, [by_row(block, length)] * 3 + [by_row(block, n_st...  5.28 us
    all_to_all x1, starting transfers between devices, per_device(): lax.all_to_all(jnp.broadcast_to(small, (n_seq,) + small.shape), 'seq', 0, 0)  4.84 us
  transfers between devices with their start and end apart: 21, of which 12 were waited for; matrix products, arithmetic and copies ran while one was open for 6% of the time, Pallas kernels for 29%

profile of v7, /device:TPU:0, one launch (start us, length us, event | category | flops | bytes accessed | tf_op | source)
XLA Modules:
  0.0 120.6 jit_solution(12762656320566824958)
XLA Ops:
  1.2 4.2 %shard_map.143 = (f32[20,1,512]{2,1,0:T(1,128)}, f32[20,1,512]{2,1,0:T(1,128)}, f32[20,128]{1,0:T(8,128)}, f32[1280,128]{1,0:T(8,128)}, bf16[21,32,128]{2,1,0:T(8,128)(2,1)}, /*index=5*/f32[20,32,128]{2,1,0:T(8,128)}) custom-call(s32[1]{0:T(128)} %bitcast.3.upper_ref, bf16[1280,512]{1,0:T(8,128)(2,1)} %bitcast.181, bf16[512,128]{1,0:T(8,128)(2,1)} %bitcast.195, ...), custom_call_target="tpu_custom_call" | custom-call | flops 6710886400 | bytes 80000000 | tf_op jit(solution)/shard_map/pallas_call | solution.py:422
  5.4 2.6 %collective-permute-start = (bf16[21,32,128]{2,1,0:T(8,128)(2,1)}, bf16[21,32,128]{2,1,0:T(8,128)(2,1)S(1)}, u32[]{:S(2)}, u32[]{:S(2)}) collective-permute-start(bf16[21,32,128]{2,1,0:T(8,128)(2,1)} %get-tuple-element.58), channel_id=1, source_target_pairs={{0,4},{4,0},{8,12},{12,8},{16,20},{20,16},{24,28},{28,24},{1,5},{5... | collective-permute-start | bytes 516104 | tf_op jit(solution)/shard_map/ppermute | solution.py:315
  7.9 1.5 %collective-permute-start.5 = (bf16[1280,512]{1,0:T(8,128)(2,1)S(1)}, bf16[1280,512]{1,0:T(8,128)(2,1)S(1)}, u32[]{:S(2)}, u32[]{:S(2)}) collective-permute-start(bf16[1280,512]{1,0:T(8,128)(2,1)S(1)} %bitcast.169), channel_id=1, source_target_pairs={{0,1},{1,0},{2,3},{3,2},{4,5},{5,4},{6,7},{7,6},{8,9},{9,8},{10,11... | collective-permute-start | bytes 3932168 | tf_op jit(solution)/shard_map/ppermute | solution.py:315
  10.4 2.7 %collective-permute-done = bf16[21,32,128]{2,1,0:T(8,128)(2,1)S(1)} collective-permute-done((bf16[21,32,128]{2,1,0:T(8,128)(2,1)}, bf16[21,32,128]{2,1,0:T(8,128)(2,1)S(1)}, u32[]{:S(2)}, u32[]{:S(2)}) %collective-permute-start) | collective-permute-done | bytes 172064 | tf_op jit(solution)/shard_map/ppermute | solution.py:315
  13.4 3.7 %collective-permute-start.1 = (bf16[21,32,128]{2,1,0:T(8,128)(2,1)S(1)}, bf16[21,32,128]{2,1,0:T(8,128)(2,1)S(1)}, u32[]{:S(2)}, u32[]{:S(2)}) collective-permute-start(bf16[21,32,128]{2,1,0:T(8,128)(2,1)S(1)} %pad_maximum_fusion.4.after_ref), channel_id=1, source_target_pairs={{0,8},{4,12},{8,16},{12,20},{16,24},{20,28},{1,9},{5,13},{9,17},{1... | collective-permute-start | bytes 516104 | tf_op jit(solution)/shard_map/ppermute | solution.py:320
  17.2 3.6 %shard_map.144 = (f32[1280,512]{1,0:T(8,128)S(1)}, bf16[1280,1280]{1,0:T(8,128)(2,1)S(1)}) custom-call(s32[1]{0:T(128)} %bitcast.10.flag_ref, bf16[1280,1280]{1,0:T(8,128)(2,1)S(1)} %copy-done.1, bf16[1280,1280]{1,0:T(8,128)(2,1)} %collective-permute-done.2.other_ref, bf16[1280,512]{1,0:T(8,128)(2,1)S(1)} %bitcast.171, ...), custom_call_target="tpu_custom_call" | custom-call | flops 33554432000 | bytes 80000000 | tf_op jit(solution)/shard_map/pallas_call | solution.py:462
  21.1 5.1 %collective-permute-start.3 = (bf16[21,32,128]{2,1,0:T(8,128)(2,1)S(1)}, bf16[21,32,128]{2,1,0:T(8,128)(2,1)S(1)}, u32[]{:S(2)}, u32[]{:S(2)}) collective-permute-start(bf16[21,32,128]{2,1,0:T(8,128)(2,1)S(1)} %pad_maximum_fusion.5), channel_id=1, source_target_pairs={{0,16},{4,20},{8,24},{12,28},{1,17},{5,21},{9,25},{13,29},{2,18},{... | collective-permute-start | bytes 516104 | tf_op jit(solution)/shard_map/ppermute | solution.py:320
  26.3 2.9 %collective-permute-done.3 = bf16[21,32,128]{2,1,0:T(8,128)(2,1)S(1)} collective-permute-done((bf16[21,32,128]{2,1,0:T(8,128)(2,1)S(1)}, bf16[21,32,128]{2,1,0:T(8,128)(2,1)S(1)}, u32[]{:S(2)}, u32[]{:S(2)}) %collective-permute-start.3) | collective-permute-done | bytes 172064 | tf_op jit(solution)/shard_map/ppermute | solution.py:320
  29.3 1.6 %collective-permute-start.4 = (bf16[20,32,128]{2,1,0:T(8,128)(2,1)S(1)}, bf16[20,32,128]{2,1,0:T(8,128)(2,1)S(1)}, u32[]{:S(2)}, u32[]{:S(2)}) collective-permute-start(bf16[20,32,128]{2,1,0:T(8,128)(2,1)S(1)} %select_convert_fusion.4.after_ref), channel_id=1, source_target_pairs={{0,4},{4,0},{8,12},{12,8},{16,20},{20,16},{24,28},{28,24},{1,5},{5... | collective-permute-start | bytes 491528 | tf_op jit(solution)/shard_map/ppermute | solution.py:315
  30.9 2.8 %shard_map.145 = (f32[1280,512]{1,0:T(8,128)S(1)}, f32[20,1,512]{2,1,0:T(1,128)S(1)}) custom-call(bf16[1280,512]{1,0:T(8,128)(2,1)S(1)} %bitcast.182, bf16[512,128]{1,0:T(8,128)(2,1)S(1)} %bitcast.196, bf16[512,128]{1,0:T(8,128)(2,1)S(1)} %bitcast.191, f32[20,1,512]{2,1,0:T(1,128)S(1)} %copy-done.13, f32[1,20]{1,0:T(1,128)S(1)} %bitcast.201, ...), custom_call_target="tpu_custom_call" | custom-call | flops 33554432000 | bytes 80000000 | tf_op jit(solution)/shard_map/pallas_call | solution.py:445
  35.1 2.8 %shard_map.146.after_ref.m0_ref = bf16[1280,512]{1,0:T(8,128)(2,1)} custom-call(f32[1280,512]{1,0:T(8,128)S(1)} %get-tuple-element.63.inner_ref, bf16[1280,128]{1,0:T(8,128)(2,1)S(1)} %bitcast.177, bf16[512,128]{1,0:T(8,128)(2,1)S(1)} %bitcast.192, bf16[1280,512]{1,0:T(8,128)(2,1)S(1)} %bitcast.183, f32[20,1,512]{2,1,0:T(1,128)S(1)} %copy-done.10, ...), custom_call_target="tpu_custom_call" | custom-call | flops 3355443200 | bytes 80000000 | tf_op jit(solution)/shard_map/pallas_call | solution.py:488
  40.2 3.7 %shard_map.147 = (bf16[1280,512]{1,0:T(8,128)(2,1)S(1)}, f32[1280,128]{1,0:T(8,128)S(1)}) custom-call(bf16[1280,1280]{1,0:T(8,128)(2,1)S(1)} %get-tuple-element.66.weights_ref, bf16[1280,512]{1,0:T(8,128)(2,1)S(1)} %collective-permute-done.5.g_ref, f32[1280,512]{1,0:T(8,128)S(1)} %get-tuple-element.68.first_ref, bf16[512,128]{1,0:T(8,128)(2,1)S(1)} %bitcast.193, ...), custom_call_target="tpu_custom_call" | custom-call | flops 40265318400 | bytes 80000000 | tf_op jit(solution)/shard_map/pallas_call | solution.py:471
  44.8 1.8 %shard_map.148.after_ref = bf16[4,160,768]{2,1,0:T(8,128)(2,1)S(1)} custom-call(s32[1]{0:T(128)} %bitcast.22.pick_ref, bf16[4,2,1,160,512]{4,3,2,1,0:T(8,128)(2,1)S(1)} %bitcast.173, bf16[4,2,1,160,512]{4,3,2,1,0:T(8,128)(2,1)S(1)} %bitcast.187, bf16[1280,512]{1,0:T(8,128)(2,1)S(1)} %copy-done.3, bf16[1280,512]{1,0:T(8,128)(2,1)S(1)} %collective-permute-done.8.m1_ref, ...), custom_call_target="tpu_custom_call" | custom-call | flops 20132659200 | bytes 80000000 | tf_op jit(solution)/shard_map/pallas_call | solution.py:516
  46.6 1.5 %collective-permute-start.11 = (bf16[4,160,768]{2,1,0:T(8,128)(2,1)S(1)}, bf16[4,160,768]{2,1,0:T(8,128)(2,1)S(1)}, u32[]{:S(2)}, u32[]{:S(2)}) collective-permute-start(bf16[4,160,768]{2,1,0:T(8,128)(2,1)S(1)} %shard_map.148.after_ref), channel_id=1, source_target_pairs={{0,4},{4,0},{8,12},{12,8},{16,20},{20,16},{24,28},{28,24},{1,5},{5... | collective-permute-start | bytes 2949128 | tf_op jit(solution)/shard_map/ppermute | solution.py:315
  48.1 1.8 %shard_map.149 = f32[4,160,768]{2,1,0:T(8,128)S(1)} custom-call(s32[1]{0:T(128)} %bitcast.31.pick_ref, bf16[4,2,1,160,512]{4,3,2,1,0:T(8,128)(2,1)S(1)} %bitcast.174, bf16[4,2,1,160,512]{4,3,2,1,0:T(8,128)(2,1)S(1)} %bitcast.188, bf16[1280,512]{1,0:T(8,128)(2,1)S(1)} %copy-done.3, bf16[1280,512]{1,0:T(8,128)(2,1)S(1)} %collective-permute-done.8.m1_ref, ...), custom_call_target="tpu_custom_call" | custom-call | flops 20132659200 | bytes 80000000 | tf_op jit(solution)/shard_map/pallas_call | solution.py:516
  50.5 1.3 %collective-permute-start.9 = (bf16[21,32,128]{2,1,0:T(8,128)(2,1)S(1)}, bf16[21,32,128]{2,1,0:T(8,128)(2,1)S(1)}, u32[]{:S(2)}, u32[]{:S(2)}) collective-permute-start(bf16[21,32,128]{2,1,0:T(8,128)(2,1)S(1)} %pad_maximum_fusion.7.after_ref), channel_id=1, source_target_pairs={{8,0},{12,4},{16,8},{20,12},{24,16},{28,20},{9,1},{13,5},{17,9},{2... | collective-permute-start | bytes 516104 | tf_op jit(solution)/shard_map/ppermute | solution.py:320
  53.1 6.3 %collective-permute-start.12 = (bf16[4,160,512]{2,1,0:T(8,128)(2,1)S(1)}, bf16[4,160,512]{2,1,0:T(8,128)(2,1)S(1)}, u32[]{:S(2)}, u32[]{:S(2)}) collective-permute-start(bf16[4,160,512]{2,1,0:T(8,128)(2,1)S(1)} %shard_map.150), channel_id=1, source_target_pairs={{0,8},{4,12},{8,0},{12,4},{16,24},{20,28},{24,16},{28,20},{1,9},{5... | collective-permute-start | bytes 1966088 | tf_op jit(solution)/shard_map/ppermute | solution.py:315
  59.4 3.9 %collective-permute-done.9 = bf16[21,32,128]{2,1,0:T(8,128)(2,1)S(1)} collective-permute-done((bf16[21,32,128]{2,1,0:T(8,128)(2,1)S(1)}, bf16[21,32,128]{2,1,0:T(8,128)(2,1)S(1)}, u32[]{:S(2)}, u32[]{:S(2)}) %collective-permute-start.9) | collective-permute-done | bytes 172064 | tf_op jit(solution)/shard_map/ppermute | solution.py:320
  63.6 1.5 %collective-permute-start.10 = (bf16[21,32,128]{2,1,0:T(8,128)(2,1)S(1)}, bf16[21,32,128]{2,1,0:T(8,128)(2,1)S(1)}, u32[]{:S(2)}, u32[]{:S(2)}) collective-permute-start(bf16[21,32,128]{2,1,0:T(8,128)(2,1)S(1)} %pad_maximum_fusion.8.after_ref), channel_id=1, source_target_pairs={{16,0},{20,4},{24,8},{28,12},{17,1},{21,5},{25,9},{29,13},{18,2},{... | collective-permute-start | bytes 516104 | tf_op jit(solution)/shard_map/ppermute | solution.py:320
  65.0 6.4 %shard_map.152 = (f32[1280,512]{1,0:T(8,128)S(1)}, f32[20,1,512]{2,1,0:T(1,128)S(1)}, f32[512,128]{1,0:T(8,128)S(1)}, f32[512,128]{1,0:T(8,128)S(1)}) custom-call(bf16[1280,512]{1,0:T(8,128)(2,1)S(1)} %bitcast.184, bf16[1280,512]{1,0:T(8,128)(2,1)S(1)} %get-tuple-element.69.cotan_ref, f32[1280,512]{1,0:T(8,128)S(1)} %get-tuple-element.63.inner_ref, ...), custom_call_target="tpu_custom_call" | custom-call | flops 67108864000 | bytes 80000000 | tf_op jit(solution)/shard_map/pallas_call | solution.py:567
  71.5 1.3 %shard_map.151 = f32[4,160,512]{2,1,0:T(8,128)S(1)} custom-call(s32[1]{0:T(128)} %bitcast.41.pick_ref, bf16[2,2,2,160,512]{4,3,2,1,0:T(8,128)(2,1)S(1)} %bitcast.176, bf16[2,2,2,160,512]{4,3,2,1,0:T(8,128)(2,1)S(1)} %bitcast.190, bf16[1280,512]{1,0:T(8,128)(2,1)S(1)} %copy-done.3, bf16[1280,512]{1,0:T(8,128)(2,1)S(1)} %collective-permute-done.8.m1_ref, ...), custom_call_target="tpu_custom_call" | custom-call | flops 13421772800 | bytes 80000000 | tf_op jit(solution)/shard_map/pallas_call | solution.py:516
  72.8 6.9 %collective-permute-done.12 = bf16[4,160,512]{2,1,0:T(8,128)(2,1)S(1)} collective-permute-done((bf16[4,160,512]{2,1,0:T(8,128)(2,1)S(1)}, bf16[4,160,512]{2,1,0:T(8,128)(2,1)S(1)}, u32[]{:S(2)}, u32[]{:S(2)}) %collective-permute-start.12) | collective-permute-done | bytes 655392 | tf_op jit(solution)/shard_map/ppermute | solution.py:315
  79.9 1.6 %collective-permute-start.13 = (bf16[20,32,128]{2,1,0:T(8,128)(2,1)S(1)}, bf16[20,32,128]{2,1,0:T(8,128)(2,1)S(1)}, u32[]{:S(2)}, u32[]{:S(2)}) collective-permute-start(bf16[20,32,128]{2,1,0:T(8,128)(2,1)S(1)} %select_convert_fusion.1), channel_id=1, source_target_pairs={{0,4},{4,0},{8,12},{12,8},{16,20},{20,16},{24,28},{28,24},{1,5},{5... | collective-permute-start | bytes 491528 | tf_op jit(solution)/shard_map/ppermute | solution.py:315
  81.7 2.8 %collective-permute-start.14 = (bf16[2,160,768]{2,1,0:T(8,128)(2,1)S(1)}, bf16[2,160,768]{2,1,0:T(8,128)(2,1)}, u32[]{:S(2)}, u32[]{:S(2)}) collective-permute-start(bf16[2,160,768]{2,1,0:T(8,128)(2,1)S(1)} %fusion.after_a_ref), channel_id=1, source_target_pairs={{0,8},{4,12},{8,0},{12,4},{16,24},{20,28},{24,16},{28,20},{1,9},{5... | collective-permute-start | bytes 1474568 | tf_op jit(solution)/shard_map/ppermute | solution.py:315
  85.9 5.3 %shard_map.153 = (bf16[1280,512]{1,0:T(8,128)(2,1)}, f32[20,1,512]{2,1,0:T(1,128)}, f32[2,20,128]{2,1,0:T(8,128)S(1)}, f32[512,256]{1,0:T(8,128)S(1)}) custom-call(bf16[1280,512]{1,0:T(8,128)(2,1)S(1)} %bitcast.185, bf16[1280,512]{1,0:T(8,128)(2,1)S(1)} %get-tuple-element.69.cotan_ref, f32[1280,512]{1,0:T(8,128)S(1)} %get-tuple-element.77.outer_ref, ...), custom_call_target="tpu_custom_call" | custom-call | flops 10066329600 | bytes 80000000 | tf_op jit(solution)/shard_map/pallas_call | solution.py:596
  91.2 1.5 %collective-permute-start.19 = (f32[512,256]{1,0:T(8,128)S(1)}, f32[512,256]{1,0:T(8,128)S(1)}, u32[]{:S(2)}, u32[]{:S(2)}) collective-permute-start(f32[512,256]{1,0:T(8,128)S(1)} %get-tuple-element.94), channel_id=1, source_target_pairs={{0,1},{1,0},{2,3},{3,2},{4,5},{5,4},{6,7},{7,6},{8,9},{9,8},{10,11... | collective-permute-start | bytes 1572872 | tf_op jit(solution)/shard_map/ppermute | solution.py:315
  92.8 1.7 %collective-permute-done.14 = bf16[2,160,768]{2,1,0:T(8,128)(2,1)} collective-permute-done((bf16[2,160,768]{2,1,0:T(8,128)(2,1)S(1)}, bf16[2,160,768]{2,1,0:T(8,128)(2,1)}, u32[]{:S(2)}, u32[]{:S(2)}) %collective-permute-start.14) | collective-permute-done | bytes 491552 | tf_op jit(solution)/shard_map/ppermute | solution.py:315
  94.6 1.4 %bitcast_add_fusion.sums_ref = f32[2,160,768]{2,1,0:T(8,128)S(1)} fusion(bf16[2,160,768]{2,1,0:T(8,128)(2,1)} %collective-permute-done.14, f32[2,2,160,768]{3,2,1,0:T(8,128)} %bitcast.205, s32[]{:T(128)S(6)} %select_n.213), kind=kLoop, calls=%fused_computation.5 | loop fusion | flops 491520 | bytes 2457604 | tf_op jit(solution)/shard_map/add | solution.py:644
  96.2 2.9 %collective-permute-start.17 = (bf16[160,768]{1,0:T(8,128)(2,1)S(1)}, bf16[160,768]{1,0:T(8,128)(2,1)S(1)}, u32[]{:S(2)}, u32[]{:S(2)}) collective-permute-start(bf16[160,768]{1,0:T(8,128)(2,1)S(1)} %get-tuple-element.91), channel_id=1, source_target_pairs={{0,16},{4,20},{8,24},{12,28},{16,0},{20,4},{24,8},{28,12},{1,17},{... | collective-permute-start | bytes 737288 | tf_op jit(solution)/shard_map/ppermute | solution.py:315
  99.8 4.8 %all-to-all-start = ((f32[8,2,20,128]{3,1,2,0:T(2,128)}), f32[8,2,20,128]{3,1,2,0:T(2,128)S(1)}, u32[]{:S(2)}, u32[]{:S(2)}) async-start(f32[8,2,20,128]{3,1,2,0:T(2,128)} %broadcast_in_dim.73), calls=%async_computation | async-start | bytes 327680 | tf_op jit(solution)/shard_map/all_to_all | solution.py:640
  106.4 8.4 %collective-permute-done.18 = bf16[160,512]{1,0:T(8,128)(2,1)S(1)} collective-permute-done((bf16[160,512]{1,0:T(8,128)(2,1)S(1)}, bf16[160,512]{1,0:T(8,128)(2,1)S(1)}, u32[]{:S(2)}, u32[]{:S(2)}) %collective-permute-start.18) | collective-permute-done | bytes 163872 | tf_op jit(solution)/shard_map/ppermute | solution.py:315
  114.8 3.6 %collective-permute-done.17 = bf16[160,768]{1,0:T(8,128)(2,1)S(1)} collective-permute-done((bf16[160,768]{1,0:T(8,128)(2,1)S(1)}, bf16[160,768]{1,0:T(8,128)(2,1)S(1)}, u32[]{:S(2)}, u32[]{:S(2)}) %collective-permute-start.17) | collective-permute-done | bytes 245792 | tf_op jit(solution)/shard_map/ppermute | solution.py:315
  (122 shorter events, 15.1 us)
Async XLA Ops:
  0.6 16.5 %collective-permute-start.2 = (bf16[1280,1280]{1,0:T(8,128)(2,1)}, bf16[1280,1280]{1,0:T(8,128)(2,1)}, u32[]{:S(2)}, u32[]{:S(2)}) collective-permute-start(bf16[1280,1280]{1,0:T(8,128)(2,1)} %mine_ref.1), channel_id=1, source_target_pairs={{0,2},{2,0},{1,3},{3,1},{4,6},{6,4},{5,7},{7,5},{8,10},{10,8},{9,1... | collective-permute-start | bytes 9830408 | tf_op jit(solution)/shard_map/ppermute | solution.py:315
  1.2 6.8 %copy-start = (bf16[1,1280,512]{2,1,0:T(8,128)(2,1)S(1)}, bf16[1,1280,512]{2,1,0:T(8,128)(2,1)}, u32[]{:S(2)}) copy-start(bf16[1,1280,512]{2,1,0:T(8,128)(2,1)} %param.15) | copy-start | bytes 3932164
  5.4 7.8 %collective-permute-start = (bf16[21,32,128]{2,1,0:T(8,128)(2,1)}, bf16[21,32,128]{2,1,0:T(8,128)(2,1)S(1)}, u32[]{:S(2)}, u32[]{:S(2)}) collective-permute-start(bf16[21,32,128]{2,1,0:T(8,128)(2,1)} %get-tuple-element.58), channel_id=1, source_target_pairs={{0,4},{4,0},{8,12},{12,8},{16,20},{20,16},{24,28},{28,24},{1,5},{5... | collective-permute-start | bytes 516104 | tf_op jit(solution)/shard_map/ppermute | solution.py:315
  7.9 30.9 %collective-permute-start.5 = (bf16[1280,512]{1,0:T(8,128)(2,1)S(1)}, bf16[1280,512]{1,0:T(8,128)(2,1)S(1)}, u32[]{:S(2)}, u32[]{:S(2)}) collective-permute-start(bf16[1280,512]{1,0:T(8,128)(2,1)S(1)} %bitcast.169), channel_id=1, source_target_pairs={{0,1},{1,0},{2,3},{3,2},{4,5},{5,4},{6,7},{7,6},{8,9},{9,8},{10,11... | collective-permute-start | bytes 3932168 | tf_op jit(solution)/shard_map/ppermute | solution.py:315
  10.3 2.9 %copy-start.16 = (f32[20]{0:T(128)}, f32[20]{0:T(128)S(1)}, u32[]{:S(2)}) copy-start(f32[20]{0:T(128)S(1)} %slice_reduce_fusion.3) | copy-start | bytes 244
  10.3 3.0 %copy-start.15 = (f32[20,32,128]{2,1,0:T(8,128)S(1)}, f32[20,32,128]{2,1,0:T(8,128)}, u32[]{:S(2)}) copy-start(f32[20,32,128]{2,1,0:T(8,128)} %get-tuple-element.59) | copy-start | bytes 983044
  10.3 6.9 %copy-start.1 = (bf16[1280,1280]{1,0:T(8,128)(2,1)S(1)}, bf16[1280,1280]{1,0:T(8,128)(2,1)}, u32[]{:S(2)}) copy-start(bf16[1280,1280]{1,0:T(8,128)(2,1)} %mine_ref.1) | copy-start | bytes 9830404
  13.4 7.5 %collective-permute-start.1 = (bf16[21,32,128]{2,1,0:T(8,128)(2,1)S(1)}, bf16[21,32,128]{2,1,0:T(8,128)(2,1)S(1)}, u32[]{:S(2)}, u32[]{:S(2)}) collective-permute-start(bf16[21,32,128]{2,1,0:T(8,128)(2,1)S(1)} %pad_maximum_fusion.4.after_ref), channel_id=1, source_target_pairs={{0,8},{4,12},{8,16},{12,20},{16,24},{20,28},{1,9},{5,13},{9,17},{1... | collective-permute-start | bytes 516104 | tf_op jit(solution)/shard_map/ppermute | solution.py:320
  20.8 10.1 %copy-start.2 = (bf16[1,1280,512]{2,1,0:T(8,128)(2,1)S(1)}, bf16[1,1280,512]{2,1,0:T(8,128)(2,1)}, u32[]{:S(2)}) copy-start(bf16[1,1280,512]{2,1,0:T(8,128)(2,1)} %param.8) | copy-start | bytes 3932164
  20.8 10.1 %copy-start.4 = (bf16[1,512,128]{2,1,0:T(8,128)(2,1)S(1)}, bf16[1,512,128]{2,1,0:T(8,128)(2,1)}, u32[]{:S(2)}) copy-start(bf16[1,512,128]{2,1,0:T(8,128)(2,1)} %param.10) | copy-start | bytes 393220
  20.8 10.0 %copy-start.5 = (bf16[1,512,128]{2,1,0:T(8,128)(2,1)S(1)}, bf16[1,512,128]{2,1,0:T(8,128)(2,1)}, u32[]{:S(2)}) copy-start(bf16[1,512,128]{2,1,0:T(8,128)(2,1)} %param.9) | copy-start | bytes 393220
  20.9 10.0 %copy-start.7 = (f32[20]{0:T(128)S(1)}, f32[20]{0:T(128)}, u32[]{:S(2)}) copy-start(f32[20]{0:T(128)} %param.13) | copy-start | bytes 244
  20.9 10.0 %copy-start.13 = (f32[20,1,512]{2,1,0:T(1,128)S(1)}, f32[20,1,512]{2,1,0:T(1,128)}, u32[]{:S(2)}) copy-start(f32[20,1,512]{2,1,0:T(1,128)} %get-tuple-element.56.shrunk_ref) | copy-start | bytes 122884
  21.1 8.0 %collective-permute-start.3 = (bf16[21,32,128]{2,1,0:T(8,128)(2,1)S(1)}, bf16[21,32,128]{2,1,0:T(8,128)(2,1)S(1)}, u32[]{:S(2)}, u32[]{:S(2)}) collective-permute-start(bf16[21,32,128]{2,1,0:T(8,128)(2,1)S(1)} %pad_maximum_fusion.5), channel_id=1, source_target_pairs={{0,16},{4,20},{8,24},{12,28},{1,17},{5,21},{9,25},{13,29},{2,18},{... | collective-permute-start | bytes 516104 | tf_op jit(solution)/shard_map/ppermute | solution.py:320
  29.3 5.4 %collective-permute-start.4 = (bf16[20,32,128]{2,1,0:T(8,128)(2,1)S(1)}, bf16[20,32,128]{2,1,0:T(8,128)(2,1)S(1)}, u32[]{:S(2)}, u32[]{:S(2)}) collective-permute-start(bf16[20,32,128]{2,1,0:T(8,128)(2,1)S(1)} %select_convert_fusion.4.after_ref), channel_id=1, source_target_pairs={{0,4},{4,0},{8,12},{12,8},{16,20},{20,16},{24,28},{28,24},{1,5},{5... | collective-permute-start | bytes 491528 | tf_op jit(solution)/shard_map/ppermute | solution.py:315
  37.9 6.9 %collective-permute-start.8 = (bf16[1280,512]{1,0:T(8,128)(2,1)}, bf16[1280,512]{1,0:T(8,128)(2,1)S(1)}, u32[]{:S(2)}, u32[]{:S(2)}) collective-permute-start(bf16[1280,512]{1,0:T(8,128)(2,1)} %shard_map.146.after_ref.m0_ref), channel_id=1, source_target_pairs={{0,2},{2,0},{1,3},{3,1},{4,6},{6,4},{5,7},{7,5},{8,10},{10,8},{9,1... | collective-permute-start | bytes 3932168 | tf_op jit(solution)/shard_map/ppermute | solution.py:315
  39.1 5.7 %collective-permute-start.7 = (bf16[8,160,512]{2,1,0:T(8,128)(2,1)S(1)}, bf16[8,160,512]{2,1,0:T(8,128)(2,1)S(1)}, u32[]{:S(2)}, u32[]{:S(2)}) collective-permute-start(bf16[8,160,512]{2,1,0:T(8,128)(2,1)S(1)} %pad_maximum_fusion.1), channel_id=1, source_target_pairs={{0,2},{2,0},{1,3},{3,1},{4,6},{6,4},{5,7},{7,5},{8,10},{10,8},{9,1... | collective-permute-start | bytes 3932168 | tf_op jit(solution)/shard_map/ppermute | solution.py:315
  44.0 6.3 %collective-permute-start.6 = (bf16[21,32,128]{2,1,0:T(8,128)(2,1)S(1)}, bf16[21,32,128]{2,1,0:T(8,128)(2,1)S(1)}, u32[]{:S(2)}, u32[]{:S(2)}) collective-permute-start(bf16[21,32,128]{2,1,0:T(8,128)(2,1)S(1)} %pad_maximum_fusion.6.after_ref), channel_id=1, source_target_pairs={{0,4},{4,0},{8,12},{12,8},{16,20},{20,16},{24,28},{28,24},{1,5},{5... | collective-permute-start | bytes 516104 | tf_op jit(solution)/shard_map/ppermute | solution.py:315
  46.6 33.1 %collective-permute-start.11 = (bf16[4,160,768]{2,1,0:T(8,128)(2,1)S(1)}, bf16[4,160,768]{2,1,0:T(8,128)(2,1)S(1)}, u32[]{:S(2)}, u32[]{:S(2)}) collective-permute-start(bf16[4,160,768]{2,1,0:T(8,128)(2,1)S(1)} %shard_map.148.after_ref), channel_id=1, source_target_pairs={{0,4},{4,0},{8,12},{12,8},{16,20},{20,16},{24,28},{28,24},{1,5},{5... | collective-permute-start | bytes 2949128 | tf_op jit(solution)/shard_map/ppermute | solution.py:315
  48.1 2.2 %copy-start.17 = (f32[20]{0:T(128)S(1)}, f32[20]{0:T(128)}, u32[]{:S(2)}) copy-start(f32[20]{0:T(128)} %copy-done.16) | copy-start | bytes 244
  50.5 12.8 %collective-permute-start.9 = (bf16[21,32,128]{2,1,0:T(8,128)(2,1)S(1)}, bf16[21,32,128]{2,1,0:T(8,128)(2,1)S(1)}, u32[]{:S(2)}, u32[]{:S(2)}) collective-permute-start(bf16[21,32,128]{2,1,0:T(8,128)(2,1)S(1)} %pad_maximum_fusion.7.after_ref), channel_id=1, source_target_pairs={{8,0},{12,4},{16,8},{20,12},{24,16},{28,20},{9,1},{13,5},{17,9},{2... | collective-permute-start | bytes 516104 | tf_op jit(solution)/shard_map/ppermute | solution.py:320
  53.1 26.6 %collective-permute-start.12 = (bf16[4,160,512]{2,1,0:T(8,128)(2,1)S(1)}, bf16[4,160,512]{2,1,0:T(8,128)(2,1)S(1)}, u32[]{:S(2)}, u32[]{:S(2)}) collective-permute-start(bf16[4,160,512]{2,1,0:T(8,128)(2,1)S(1)} %shard_map.150), channel_id=1, source_target_pairs={{0,8},{4,12},{8,0},{12,4},{16,24},{20,28},{24,16},{28,20},{1,9},{5... | collective-permute-start | bytes 1966088 | tf_op jit(solution)/shard_map/ppermute | solution.py:315
  63.6 9.2 %collective-permute-start.10 = (bf16[21,32,128]{2,1,0:T(8,128)(2,1)S(1)}, bf16[21,32,128]{2,1,0:T(8,128)(2,1)S(1)}, u32[]{:S(2)}, u32[]{:S(2)}) collective-permute-start(bf16[21,32,128]{2,1,0:T(8,128)(2,1)S(1)} %pad_maximum_fusion.8.after_ref), channel_id=1, source_target_pairs={{16,0},{20,4},{24,8},{28,12},{17,1},{21,5},{25,9},{29,13},{18,2},{... | collective-permute-start | bytes 516104 | tf_op jit(solution)/shard_map/ppermute | solution.py:320
  79.9 5.6 %collective-permute-start.13 = (bf16[20,32,128]{2,1,0:T(8,128)(2,1)S(1)}, bf16[20,32,128]{2,1,0:T(8,128)(2,1)S(1)}, u32[]{:S(2)}, u32[]{:S(2)}) collective-permute-start(bf16[20,32,128]{2,1,0:T(8,128)(2,1)S(1)} %select_convert_fusion.1), channel_id=1, source_target_pairs={{0,4},{4,0},{8,12},{12,8},{16,20},{20,16},{24,28},{28,24},{1,5},{5... | collective-permute-start | bytes 491528 | tf_op jit(solution)/shard_map/ppermute | solution.py:315
  81.6 4.2 %copy-start.14 = (f32[4,160,768]{2,1,0:T(8,128)}, f32[4,160,768]{2,1,0:T(8,128)S(1)}, u32[]{:S(2)}) copy-start(f32[4,160,768]{2,1,0:T(8,128)S(1)} %convert_add_fusion) | copy-start | bytes 5898244
  81.7 12.8 %collective-permute-start.14 = (bf16[2,160,768]{2,1,0:T(8,128)(2,1)S(1)}, bf16[2,160,768]{2,1,0:T(8,128)(2,1)}, u32[]{:S(2)}, u32[]{:S(2)}) collective-permute-start(bf16[2,160,768]{2,1,0:T(8,128)(2,1)S(1)} %fusion.after_a_ref), channel_id=1, source_target_pairs={{0,8},{4,12},{8,0},{12,4},{16,24},{20,28},{24,16},{28,20},{1,9},{5... | collective-permute-start | bytes 1474568 | tf_op jit(solution)/shard_map/ppermute | solution.py:315
  84.9 7.9 %collective-permute-start.15 = (bf16[2,160,512]{2,1,0:T(8,128)(2,1)S(1)}, bf16[2,160,512]{2,1,0:T(8,128)(2,1)S(1)}, u32[]{:S(2)}, u32[]{:S(2)}) collective-permute-start(bf16[2,160,512]{2,1,0:T(8,128)(2,1)S(1)} %fusion.8.after_b_ref), channel_id=1, source_target_pairs={{0,4},{4,0},{8,12},{12,8},{16,20},{20,16},{24,28},{28,24},{1,5},{5... | collective-permute-start | bytes 983048 | tf_op jit(solution)/shard_map/ppermute | solution.py:315
  91.2 1.5 %collective-permute-start.16 = (f32[2,20,128]{2,1,0:T(8,128)S(1)}, f32[2,20,128]{2,1,0:T(8,128)S(1)}, u32[]{:S(2)}, u32[]{:S(2)}) collective-permute-start(f32[2,20,128]{2,1,0:T(8,128)S(1)} %get-tuple-element.89), channel_id=1, source_target_pairs={{0,2},{2,0},{1,3},{3,1},{4,6},{6,4},{5,7},{7,5},{8,10},{10,8},{9,1... | collective-permute-start | bytes 61448 | tf_op jit(solution)/shard_map/ppermute | solution.py:315
  91.2 14.3 %collective-permute-start.19 = (f32[512,256]{1,0:T(8,128)S(1)}, f32[512,256]{1,0:T(8,128)S(1)}, u32[]{:S(2)}, u32[]{:S(2)}) collective-permute-start(f32[512,256]{1,0:T(8,128)S(1)} %get-tuple-element.94), channel_id=1, source_target_pairs={{0,1},{1,0},{2,3},{3,2},{4,5},{5,4},{6,7},{7,6},{8,9},{9,8},{10,11... | collective-permute-start | bytes 1572872 | tf_op jit(solution)/shard_map/ppermute | solution.py:315
  96.1 18.6 %collective-permute-start.18 = (bf16[160,512]{1,0:T(8,128)(2,1)S(1)}, bf16[160,512]{1,0:T(8,128)(2,1)S(1)}, u32[]{:S(2)}, u32[]{:S(2)}) collective-permute-start(bf16[160,512]{1,0:T(8,128)(2,1)S(1)} %get-tuple-element.93), channel_id=1, source_target_pairs={{0,16},{4,20},{8,24},{12,28},{16,0},{20,4},{24,8},{28,12},{1,17},{... | collective-permute-start | bytes 491528 | tf_op jit(solution)/shard_map/ppermute | solution.py:315
  96.2 22.2 %collective-permute-start.17 = (bf16[160,768]{1,0:T(8,128)(2,1)S(1)}, bf16[160,768]{1,0:T(8,128)(2,1)S(1)}, u32[]{:S(2)}, u32[]{:S(2)}) collective-permute-start(bf16[160,768]{1,0:T(8,128)(2,1)S(1)} %get-tuple-element.91), channel_id=1, source_target_pairs={{0,16},{4,20},{8,24},{12,28},{16,0},{20,4},{24,8},{28,12},{1,17},{... | collective-permute-start | bytes 737288 | tf_op jit(solution)/shard_map/ppermute | solution.py:315
  99.8 20.0 %all-to-all-start = ((f32[8,2,20,128]{3,1,2,0:T(2,128)}), f32[8,2,20,128]{3,1,2,0:T(2,128)S(1)}, u32[]{:S(2)}, u32[]{:S(2)}) async-start(f32[8,2,20,128]{3,1,2,0:T(2,128)} %broadcast_in_dim.73), calls=%async_computation | async-start | bytes 327680 | tf_op jit(solution)/shard_map/all_to_all | solution.py:640
  (7 other events, 8.1 us)
